TPU v7x, 32 devices: a whole 2x2x4 slice. The times are simulated.
32 devices in a mesh: groups: 1, expert: 16 (over z, y, core), dp: 2 (over x).
Axes of the slice: x: 2, y: 2, z: 4, core: 2. Of those that a mesh axis runs over, the one named last changes fastest.
Arguments:
- tokens: bfloat16 [128, 2048], P(('groups', 'expert', 'dp')), may hold values from -6 to 6
- route_ids: int32 [128, 8], P(('groups', 'expert', 'dp')), may hold values from 0 to 15, all different within a row; in each aligned block of 4 rows (0 to 3, 4 to 7, ...) at most 4 rows name the same one
- route_weights: int32 [128, 8], P(('groups', 'expert', 'dp')), may hold values from 8192 to 65535
- w_gate: bfloat16 [16, 2048, 1024], P('expert', None, 'dp'), may hold values from -0.125 to 0.125
- w_up: bfloat16 [16, 2048, 1024], P('expert', None, 'dp'), may hold values from -0.125 to 0.125
- w_down: bfloat16 [16, 1024, 2048], P('expert', 'dp'), may hold values from -0.1875 to 0.1875
- grad_out: bfloat16 [128, 2048], P(('groups', 'expert', 'dp')), may hold values from -6 to 6
Outputs:
- layer_out: bfloat16 [128, 2048], P(('groups', 'expert', 'dp'))
- input_grad: bfloat16 [128, 2048], P(('groups', 'expert', 'dp'))
- gate_grad: bfloat16 [16, 2048, 1024], P(('groups', 'expert'), None, 'dp')
- up_grad: bfloat16 [16, 2048, 1024], P(('groups', 'expert'), None, 'dp')
- down_grad: bfloat16 [16, 1024, 2048], P(('groups', 'expert'), 'dp')
Inputs may be any that keep to these rules, and one draw needn't show every extreme that they name: `route_ids`: each token names 8 different experts; the 4 tokens of one device name one expert at most 4 times, and some device's tokens reach 4.
All inputs are finite; a program needn't handle non-finite values.
Results may differ from a plain program's by a relative error of at most 0.0065.
Values may be sent and summed in bfloat16 or wider, within the bound.
No kernel may reach another device: no remote copies, remote signals or barrier semaphores. Data moves between devices by JAX's collectives and lax.ppermute only.
A program may use at most 128 MiB of HBM per device.

v0:
```python
import jax
import jax.numpy as jnp
from jax import lax
from jax.sharding import PartitionSpec as P


def positions(id_rows, groups, expert_total, capacity, slot_width):
    flat = id_rows.reshape(groups, -1)
    hits = (flat[:, :, None] == jnp.arange(expert_total, dtype=jnp.int32)[None, None, :]).astype(
        jnp.int32
    )
    before = jnp.cumsum(hits, axis=1) - hits
    within = jnp.sum(before * hits, axis=2)
    offset = jnp.arange(groups, dtype=jnp.int32)[:, None] * capacity
    return (flat * slot_width + offset + within).reshape(-1)


def route_rows(tokens, grad_out, route_weights, top_count):
    scale = (route_weights.astype(jnp.float32) / 65536.0).reshape(-1, 1)
    token_rows = jnp.repeat(tokens, top_count, axis=0)
    grad_rows = (scale * jnp.repeat(grad_out, top_count, axis=0).astype(jnp.float32)).astype(
        jnp.bfloat16
    )
    return (token_rows, grad_rows, scale)


def place_rows(rows, target, total_rows):
    return jnp.zeros((total_rows, rows.shape[1]), rows.dtype).at[target].set(rows)


def expert_math(token_rows, grad_rows, w_gate, w_up, w_down):
    gate = jnp.einsum("emd,edf->emf", token_rows, w_gate, preferred_element_type=jnp.float32)
    upper = jnp.einsum("emd,edf->emf", token_rows, w_up, preferred_element_type=jnp.float32)
    sig = jax.nn.sigmoid(gate)
    hidden = (gate * sig * upper).astype(jnp.bfloat16)
    dact = jnp.einsum("emd,efd->emf", grad_rows, w_down, preferred_element_type=jnp.float32)
    dgate = (dact * upper * sig * (1.0 + gate * (1.0 - sig))).astype(jnp.bfloat16)
    dupper = (dact * gate * sig).astype(jnp.bfloat16)
    part_out = jnp.einsum(
        "emf,efd->emd", hidden, w_down, preferred_element_type=jnp.float32
    ).astype(jnp.bfloat16)
    part_back = (
        jnp.einsum("emf,edf->emd", dgate, w_gate, preferred_element_type=jnp.float32)
        + jnp.einsum("emf,edf->emd", dupper, w_up, preferred_element_type=jnp.float32)
    ).astype(jnp.bfloat16)
    gate_term = jnp.einsum("emd,emf->edf", token_rows, dgate, preferred_element_type=jnp.float32)
    up_term = jnp.einsum("emd,emf->edf", token_rows, dupper, preferred_element_type=jnp.float32)
    down_term = jnp.einsum("emf,emd->efd", hidden, grad_rows, preferred_element_type=jnp.float32)
    return (part_out, part_back, gate_term, up_term, down_term)


def combine_rows(returned_out, returned_back, target, scale, token_count, top_count):
    width = returned_out.shape[-1]
    out_rows = (
        returned_out.reshape(-1, width)[target]
        .astype(jnp.float32)
        .reshape(token_count, top_count, width)
    )
    back_rows = (
        returned_back.reshape(-1, width)[target]
        .astype(jnp.float32)
        .reshape(token_count, top_count, width)
    )
    mixed = jnp.sum(scale.reshape(token_count, top_count, 1) * out_rows, axis=1)
    back = jnp.sum(back_rows, axis=1)
    return (mixed, back)


def on_device(tokens, route_ids, route_weights, w_gate, w_up, w_down, grad_out):
    token_count, width = tokens.shape
    top_count = route_ids.shape[1]
    local_experts = w_gate.shape[0]
    expert_count = lax.axis_size("expert")
    data_count = lax.axis_size("dp")
    expert_total = local_experts * expert_count
    capacity = min(token_count, 3 * token_count * top_count // expert_total)
    all_tokens, all_grads = (
        lax.all_gather(tokens, "dp", axis=0, tiled=True),
        lax.all_gather(grad_out, "dp", axis=0, tiled=True),
    )
    all_ids, all_weights = (
        lax.all_gather(route_ids, "dp", axis=0, tiled=True),
        lax.all_gather(route_weights, "dp", axis=0, tiled=True),
    )
    slot_width = data_count * capacity
    target = positions(all_ids, data_count, expert_total, capacity, slot_width)
    token_rows, grad_rows, scale = route_rows(all_tokens, all_grads, all_weights, top_count)
    send_tokens = place_rows(token_rows, target, expert_total * slot_width).reshape(
        expert_total, slot_width, width
    )
    send_grads = place_rows(grad_rows, target, expert_total * slot_width).reshape(
        expert_total, slot_width, width
    )
    recv_tokens, recv_grads = (
        lax.all_to_all(send_tokens, "expert", split_axis=0, concat_axis=1, tiled=True),
        lax.all_to_all(send_grads, "expert", split_axis=0, concat_axis=1, tiled=True),
    )
    part_out, part_back, gate_sum, up_sum, down_sum = expert_math(
        recv_tokens, recv_grads, w_gate, w_up, w_down
    )
    returned_out, returned_back = (
        lax.all_to_all(part_out, "expert", split_axis=1, concat_axis=0, tiled=True),
        lax.all_to_all(part_back, "expert", split_axis=1, concat_axis=0, tiled=True),
    )
    mixed_all, back_all = combine_rows(
        returned_out, returned_back, target, scale, data_count * token_count, top_count
    )
    mixed, back = (
        lax.psum_scatter(mixed_all, "dp", scatter_dimension=0, tiled=True),
        lax.psum_scatter(back_all, "dp", scatter_dimension=0, tiled=True),
    )
    return (
        mixed.astype(jnp.bfloat16),
        back.astype(jnp.bfloat16),
        gate_sum.astype(jnp.bfloat16),
        up_sum.astype(jnp.bfloat16),
        down_sum.astype(jnp.bfloat16),
    )


def solution(mesh):
    in_specs = (
        P(("groups", "expert", "dp"), None),
        P(("groups", "expert", "dp"), None),
        P(("groups", "expert", "dp"), None),
        P("expert", None, "dp"),
        P("expert", None, "dp"),
        P("expert", "dp", None),
        P(("groups", "expert", "dp"), None),
    )
    out_specs = (
        P(("groups", "expert", "dp"), None),
        P(("groups", "expert", "dp"), None),
        P(("groups", "expert"), None, "dp"),
        P(("groups", "expert"), None, "dp"),
        P(("groups", "expert"), "dp", None),
    )
    return jax.shard_map(
        on_device, mesh=mesh, in_specs=in_specs, out_specs=out_specs, check_vma=False
    )
```

profile of v0, /device:TPU:0, one launch (start us, length us, event | category | flops | bytes accessed | tf_op | source)
XLA Modules:
  0.0 118.0 jit_solution(15064862504054637527)
XLA Ops:
  0.6 0.0 copy-start
  0.7 5.6 %all-gather.1 = s32[2,4,8]{2,1,0:T(4,128)S(1)} all-gather(s32[1,4,8]{2,1,0:T(4,128)} %bitcast.98), channel_id=1, replica_groups=mesh['groups'=1,'expert'=16,'dp'=2] {'dp'}, dimensions={0}, use_global_device_ids=true | all-gather | bytes 384 | tf_op jit(solution)/shard_map/all_gather | solution.py:82
  6.2 0.1 eq.15
  6.3 0.1 add.58
  6.4 0.1 add.59
  6.5 0.1 mul.81
  6.5 0.1 fusion.33
  6.6 0.1 reduce_window_sum.11
  6.7 0.2 select_reduce_fusion
  6.9 0.1 reduce_sum.30
  7.0 4.6 %all-gather.2 = bf16[2,4,2048]{2,1,0:T(4,128)(2,1)S(1)} all-gather(bf16[1,4,2048]{2,1,0:T(4,128)(2,1)} %bitcast.96), channel_id=1, replica_groups=mesh['groups'=1,'expert'=16,'dp'=2] {'dp'}, dimensions={0}, use_global_device_ids=true | all-gather | bytes 49152 | tf_op jit(solution)/shard_map/all_gather | solution.py:78
  11.6 1.8 %scatter_custom_fusion = bf16[128,2048]{1,0:T(8,128)(2,1)} fusion(s32[64]{0:T(128)S(1)} %fusion.34, bf16[]{:T(256)} %constant.9.clone.1, bf16[8,2048]{1,0:T(8,128)(2,1)S(1)} %reshape.225), kind=kCustom, calls=%fused_computation.39 | custom fusion | bytes 557058 | tf_op jit(solution)/shard_map/scatter | solution.py:28
  13.4 6.4 %all-to-all-start = ((bf16[16,8,2048]{2,1,0:T(8,128)(2,1)}), bf16[16,8,2048]{2,1,0:T(8,128)(2,1)S(1)}, u32[]{:S(2)}, u32[]{:S(2)}) async-start(bf16[16,8,2048]{2,1,0:T(8,128)(2,1)} %bitcast.6), calls=%async_computation | async-start | bytes 1048576 | tf_op jit(solution)/shard_map/all_to_all | solution.py:95
  19.8 4.5 %all-gather = s32[2,4,8]{2,1,0:T(4,128)S(1)} all-gather(s32[1,4,8]{2,1,0:T(4,128)} %bitcast.99), channel_id=1, replica_groups=mesh['groups'=1,'expert'=16,'dp'=2] {'dp'}, dimensions={0}, use_global_device_ids=true | all-gather | bytes 384 | tf_op jit(solution)/shard_map/all_gather | solution.py:83
  24.3 0.1 mul.87
  24.4 4.6 %all-gather.3 = bf16[2,4,2048]{2,1,0:T(4,128)(2,1)S(1)} all-gather(bf16[1,4,2048]{2,1,0:T(4,128)(2,1)} %bitcast.97), channel_id=1, replica_groups=mesh['groups'=1,'expert'=16,'dp'=2] {'dp'}, dimensions={0}, use_global_device_ids=true | all-gather | bytes 49152 | tf_op jit(solution)/shard_map/all_gather | solution.py:79
  29.1 1.9 %scatter_custom_fusion.1 = bf16[128,2048]{1,0:T(8,128)(2,1)} fusion(s32[64]{0:T(128)S(1)} %fusion.34, f32[8,2048]{1,0:T(8,128)S(1)} %reshape.229, f32[64]{0:T(128)S(1)} %mul.87, bf16[]{:T(256)} %constant.9.clone.1), kind=kCustom, calls=%fused_computation.38 | custom fusion | flops 262144 | bytes 590338 | tf_op jit(solution)/shard_map/scatter | solution.py:28
  30.9 3.4 %all-to-all-done = bf16[16,8,2048]{2,1,0:T(8,128)(2,1)S(1)} async-done(((bf16[16,8,2048]{2,1,0:T(8,128)(2,1)}), bf16[16,8,2048]{2,1,0:T(8,128)(2,1)S(1)}, u32[]{:S(2)}, u32[]{:S(2)}) %all-to-all-start) | async-done | bytes 524320 | tf_op jit(solution)/shard_map/all_to_all | solution.py:95
  34.3 4.1 %all-to-all-start.2 = ((bf16[16,8,2048]{2,1,0:T(8,128)(2,1)}), bf16[16,8,2048]{2,1,0:T(8,128)(2,1)S(1)}, u32[]{:S(2)}, u32[]{:S(2)}) async-start(bf16[16,8,2048]{2,1,0:T(8,128)(2,1)} %bitcast.15), calls=%async_computation.2 | async-start | bytes 1048576 | tf_op jit(solution)/shard_map/all_to_all | solution.py:96
  38.4 0.0 copy-start.1
  38.4 2.9 %fusion.10 = f32[128,512]{1,0:T(8,128)} fusion(bf16[1,2048,512]{2,1,0:T(8,128)(2,1)} %param.11, bf16[16,8,2048]{2,1,0:T(8,128)(2,1)S(1)} %all-to-all-done), kind=kOutput, calls=%fused_computation.19 | convolution fusion | flops 268435456 | bytes 2883584 | tf_op jit(solution)/shard_map/emd,edf->emf/dot_general | solution.py:33
  41.3 0.0 copy-done.1
  41.3 1.2 fusion.14
  42.5 10.4 %all-to-all-done.2 = bf16[16,8,2048]{2,1,0:T(8,128)(2,1)S(1)} async-done(((bf16[16,8,2048]{2,1,0:T(8,128)(2,1)}), bf16[16,8,2048]{2,1,0:T(8,128)(2,1)S(1)}, u32[]{:S(2)}, u32[]{:S(2)}) %all-to-all-start.2) | async-done | bytes 524320 | tf_op jit(solution)/shard_map/all_to_all | solution.py:96
  52.9 0.0 copy-done
  52.9 0.0 copy-start.3
  52.9 2.1 %multiply_convert_fusion = (bf16[128,512]{1,0:T(8,128)(2,1)S(1)}, bf16[128,512]{1,0:T(8,128)(2,1)S(1)}, bf16[128,512]{1,0:T(8,128)(2,1)S(1)}) fusion(f32[128,512]{1,0:T(8,128)} %fusion.14, f32[128,512]{1,0:T(8,128)} %fusion.10, bf16[1,512,2048]{2,1,0:T(8,128)(2,1)S(1)} %copy-done, bf16[16,8,2048]{2,1,0:T(8,128)(2,1)S(1)} %all-to-all-done.2), kind=kOutput, calls=%fused_computation.41 | convolution fusion | flops 269484032 | bytes 3538944 | tf_op jit(solution)/shard_map/emd,efd->emf/dot_general | solution.py:36
  55.0 0.4 fusion.4
  55.5 0.0 copy-done.3
  55.5 1.8 %copy.25 = bf16[1,128,2048]{2,0,1:T(2,128)(2,1)} copy(bf16[1,128,2048]{2,1,0:T(8,128)(2,1)S(1)} %fusion.4) | data formatting | bytes 1048576 | tf_op jit(solution)/shard_map/convert_element_type | solution.py:41
  57.2 0.5 broadcast.84
  57.8 4.8 %reduce = bf16[128,2048]{1,0:T(8,128)(2,1)S(1)} reduce(bf16[128,1,2048]{2,1,0:T(2,128)(2,1)} %bitcast.93, bf16[]{:T(256)} %broadcast.84), dimensions={1}, to_apply=%bitcast.86.reduce_sub_computation | reduce | bytes 1048578
  62.5 1.3 %reshape.243 = bf16[16,2,8192]{2,1,0:T(2,128)(2,1)} reshape(bf16[128,2048]{1,0:T(8,128)(2,1)S(1)} %reduce) | data formatting | bytes 1048576
  63.9 4.1 %all-to-all-start.1 = ((bf16[16,2,8192]{2,1,0:T(2,128)(2,1)}), bf16[16,2,8192]{2,1,0:T(2,128)(2,1)S(1)}, u32[]{:S(2)}, u32[]{:S(2)}) async-start(bf16[16,2,8192]{2,1,0:T(2,128)(2,1)} %reshape.243), calls=%async_computation.1 | async-start | bytes 1048576 | tf_op jit(solution)/shard_map/all_to_all | solution.py:102
  68.0 0.0 copy-start.2
  68.0 2.5 %fusion.12 = f32[128,2048]{1,0:T(8,128)S(1)} fusion(bf16[128,512]{1,0:T(8,128)(2,1)S(1)} %get-tuple-element.8, bf16[1,2048,512]{2,1,0:T(8,128)(2,1)} %param.10), kind=kOutput, calls=%fused_computation.21 | convolution fusion | flops 268435456 | bytes 3276800 | tf_op jit(solution)/shard_map/emf,edf->emd/dot_general | solution.py:43
  70.5 0.0 copy-done.2
  70.6 0.8 fusion.5
  71.4 1.8 %copy.24 = bf16[1,128,2048]{2,0,1:T(2,128)(2,1)} copy(bf16[1,128,2048]{2,1,0:T(8,128)(2,1)S(1)} %fusion.5) | data formatting | bytes 1048576 | tf_op jit(solution)/shard_map/convert_element_type | solution.py:45
  73.2 0.0 copy-start.4
  73.2 5.6 %reduce.1 = bf16[128,2048]{1,0:T(8,128)(2,1)} reduce(bf16[128,1,2048]{2,1,0:T(2,128)(2,1)} %bitcast.94, bf16[]{:T(256)} %broadcast.84), dimensions={1}, to_apply=%bitcast.85.reduce_sub_computation | reduce | bytes 1048578
  78.7 2.4 %reshape.245 = bf16[16,2,8192]{2,1,0:T(2,128)(2,1)} reshape(bf16[128,2048]{1,0:T(8,128)(2,1)} %reduce.1) | data formatting | bytes 1048576
  81.1 1.3 %all-to-all-done.1 = bf16[16,2,8192]{2,1,0:T(2,128)(2,1)S(1)} async-done(((bf16[16,2,8192]{2,1,0:T(2,128)(2,1)}), bf16[16,2,8192]{2,1,0:T(2,128)(2,1)S(1)}, u32[]{:S(2)}, u32[]{:S(2)}) %all-to-all-start.1) | async-done | bytes 524320 | tf_op jit(solution)/shard_map/all_to_all | solution.py:102
  82.4 4.7 %all-to-all-start.3 = ((bf16[16,2,8192]{2,1,0:T(2,128)(2,1)}), bf16[16,2,8192]{2,1,0:T(2,128)(2,1)}, u32[]{:S(2)}, u32[]{:S(2)}) async-start(bf16[16,2,8192]{2,1,0:T(2,128)(2,1)} %reshape.245), calls=%async_computation.3 | async-start | bytes 1048576 | tf_op jit(solution)/shard_map/all_to_all | solution.py:103
  87.2 0.0 copy-done.4
  87.2 0.6 dynamic-slice
  88.5 3.1 %fusion.2 = bf16[1,512,2048]{2,1,0:T(8,128)(2,1)} fusion(bf16[128,512]{1,0:T(8,128)(2,1)S(1)} %get-tuple-element.9, bf16[16,8,2048]{2,1,0:T(8,128)(2,1)} %copy-done.3), kind=kOutput, calls=%fused_computation.9 | convolution fusion | flops 269484032 | bytes 2752512 | tf_op jit(solution)/shard_map/emf,emd->efd/dot_general | solution.py:48
  91.5 2.0 %fusion.1 = bf16[1,2048,512]{2,1,0:T(8,128)(2,1)} fusion(bf16[128,512]{1,0:T(8,128)(2,1)S(1)} %get-tuple-element.7, bf16[16,8,2048]{2,1,0:T(8,128)(2,1)S(1)} %all-to-all-done), kind=kOutput, calls=%fused_computation.8 | convolution fusion | flops 269484032 | bytes 2752512 | tf_op jit(solution)/shard_map/emd,emf->edf/dot_general | solution.py:47
  93.6 2.0 %fusion = bf16[1,2048,512]{2,1,0:T(8,128)(2,1)} fusion(bf16[128,512]{1,0:T(8,128)(2,1)S(1)} %get-tuple-element.8, bf16[16,8,2048]{2,1,0:T(8,128)(2,1)S(1)} %all-to-all-done), kind=kOutput, calls=%fused_computation.7 | convolution fusion | flops 269484032 | bytes 2752512 | tf_op jit(solution)/shard_map/emd,emf->edf/dot_general | solution.py:46
  95.6 1.8 %reshape.244 = bf16[128,1,2048]{2,1,0:T(2,128)(2,1)} reshape(bf16[16,2,8192]{2,1,0:T(2,128)(2,1)S(1)} %all-to-all-done.1) | data formatting | bytes 1048576
  97.4 1.5 %copy.23 = bf16[1,128,2048]{2,1,0:T(8,128)(2,1)S(1)} copy(bf16[1,128,2048]{2,0,1:T(2,128)(2,1)} %bitcast.91) | data formatting | bytes 1048576
  98.9 0.7 gather_fusion
  99.7 0.2 fusion.16
  99.9 1.8 %all-to-all-done.3 = bf16[16,2,8192]{2,1,0:T(2,128)(2,1)} async-done(((bf16[16,2,8192]{2,1,0:T(2,128)(2,1)}), bf16[16,2,8192]{2,1,0:T(2,128)(2,1)}, u32[]{:S(2)}, u32[]{:S(2)}) %all-to-all-start.3) | async-done | bytes 524320 | tf_op jit(solution)/shard_map/all_to_all | solution.py:103
  101.7 3.5 %reshape.246 = bf16[128,1,2048]{2,1,0:T(2,128)(2,1)} reshape(bf16[16,2,8192]{2,1,0:T(2,128)(2,1)} %all-to-all-done.3) | data formatting | bytes 1048576
  105.2 1.5 %copy.22 = bf16[1,128,2048]{2,1,0:T(8,128)(2,1)S(1)} copy(bf16[1,128,2048]{2,0,1:T(2,128)(2,1)} %bitcast.92) | data formatting | bytes 1048576
  106.7 0.7 gather_fusion.1
  107.5 0.2 convert_reduce_fusion
  107.6 9.7 %all-reduce.4 = (bf16[8,2048]{1,0:T(8,128)(2,1)S(1)}, bf16[8,2048]{1,0:T(8,128)(2,1)S(1)}) all-reduce(f32[8,2048]{1,0:T(8,128)S(1)} %fusion.16, f32[8,2048]{1,0:T(8,128)S(1)} %convert_reduce_fusion), channel_id=2, replica_groups=mesh['groups'=1,'expert'=16,'dp'=2] {'dp'}, use_global_device_ids=true, to_apply=%region_4.5.clone | all-reduce | flops 32768 | bytes 196608
  117.4 0.6 dynamic-slice_convert_fusion
  (7 shorter events, 0.0 us)
Async XLA Ops:
  0.6 52.3 %copy-start = (bf16[1,512,2048]{2,1,0:T(8,128)(2,1)S(1)}, bf16[1,512,2048]{2,1,0:T(8,128)(2,1)}, u32[]{:S(2)}) copy-start(bf16[1,512,2048]{2,1,0:T(8,128)(2,1)} %param.12) | copy-start | bytes 6291460
  13.4 20.9 %all-to-all-start = ((bf16[16,8,2048]{2,1,0:T(8,128)(2,1)}), bf16[16,8,2048]{2,1,0:T(8,128)(2,1)S(1)}, u32[]{:S(2)}, u32[]{:S(2)}) async-start(bf16[16,8,2048]{2,1,0:T(8,128)(2,1)} %bitcast.6), calls=%async_computation | async-start | bytes 1048576 | tf_op jit(solution)/shard_map/all_to_all | solution.py:95
  34.3 18.6 %all-to-all-start.2 = ((bf16[16,8,2048]{2,1,0:T(8,128)(2,1)}), bf16[16,8,2048]{2,1,0:T(8,128)(2,1)S(1)}, u32[]{:S(2)}, u32[]{:S(2)}) async-start(bf16[16,8,2048]{2,1,0:T(8,128)(2,1)} %bitcast.15), calls=%async_computation.2 | async-start | bytes 1048576 | tf_op jit(solution)/shard_map/all_to_all | solution.py:96
  38.4 2.9 %copy-start.1 = (bf16[1,2048,512]{2,1,0:T(8,128)(2,1)S(1)}, bf16[1,2048,512]{2,1,0:T(8,128)(2,1)}, u32[]{:S(2)}) copy-start(bf16[1,2048,512]{2,1,0:T(8,128)(2,1)} %param.10) | copy-start | bytes 6291460
  52.9 2.6 %copy-start.3 = (bf16[16,8,2048]{2,1,0:T(8,128)(2,1)}, bf16[16,8,2048]{2,1,0:T(8,128)(2,1)S(1)}, u32[]{:S(2)}) copy-start(bf16[16,8,2048]{2,1,0:T(8,128)(2,1)S(1)} %all-to-all-done.2) | copy-start | bytes 1572868
  63.9 18.6 %all-to-all-start.1 = ((bf16[16,2,8192]{2,1,0:T(2,128)(2,1)}), bf16[16,2,8192]{2,1,0:T(2,128)(2,1)S(1)}, u32[]{:S(2)}, u32[]{:S(2)}) async-start(bf16[16,2,8192]{2,1,0:T(2,128)(2,1)} %reshape.243), calls=%async_computation.1 | async-start | bytes 1048576 | tf_op jit(solution)/shard_map/all_to_all | solution.py:102
  68.0 2.6 %copy-start.2 = (bf16[1,2048,512]{2,1,0:T(8,128)(2,1)S(1)}, bf16[1,2048,512]{2,1,0:T(8,128)(2,1)}, u32[]{:S(2)}) copy-start(bf16[1,2048,512]{2,1,0:T(8,128)(2,1)} %param.11) | copy-start | bytes 6291460
  73.2 14.0 %copy-start.4 = (u32[32]{0:T(128)S(1)}, u32[32]{0:T(128)}, u32[]{:S(2)}) copy-start(u32[32]{0:T(128)} %constant.31) | copy-start | bytes 388
  82.4 19.3 %all-to-all-start.3 = ((bf16[16,2,8192]{2,1,0:T(2,128)(2,1)}), bf16[16,2,8192]{2,1,0:T(2,128)(2,1)}, u32[]{:S(2)}, u32[]{:S(2)}) async-start(bf16[16,2,8192]{2,1,0:T(2,128)(2,1)} %reshape.245), calls=%async_computation.3 | async-start | bytes 1048576 | tf_op jit(solution)/shard_map/all_to_all | solution.py:103
where the time goes:
time: 119 us; the launch traced here: 118 us
  blocking collectives  29 us (24%)
  local copies, waits for them, and re-layouts  21.2 us (18%)
  starting transfers between devices  19.4 us (16%)
  matrix products  17.1 us (14%)
  waiting for transfers between devices  16.9 us (14%)
  other arithmetic  13 us (11%)
  between operations  1.47 us (1%)
    unnamed x19, local copies, waits for them, and re-layouts  13.2 us
    all_to_all x1, waiting for transfers between devices, on_device(): lax.all_to_all(send_grads, 'expert', split_axis=0, concat_axis=1, tiled=T...  10.4 us
    unnamed x2, other arithmetic  10.3 us
    unnamed x1, blocking collectives  9.73 us
    all_to_all x1, starting transfers between devices, on_device(): lax.all_to_all(send_tokens, 'expert', split_axis=0, concat_axis=1, tiled=...  6.43 us
    all_gather x1, blocking collectives, on_device(): lax.all_gather(route_ids, 'dp', axis=0, tiled=True)  5.57 us
    all_to_all x1, starting transfers between devices, on_device(): lax.all_to_all(part_back, 'expert', split_axis=1, concat_axis=0, tiled=True)  4.74 us
    all_gather x1, blocking collectives, on_device(): lax.all_gather(tokens, 'dp', axis=0, tiled=True)  4.62 us
  transfers between devices with their start and end apart: 4, of which 4 were waited for; matrix products, arithmetic and copies ran while one was open for 26% of the time, Pallas kernels for 0%

commit v1 on v0

v1 whole, which is shorter than its diff:
```python
import jax
import jax.numpy as jnp
from jax import lax
from jax.experimental import pallas as pl
from jax.experimental.pallas import tpu as pltpu
from jax.sharding import PartitionSpec as P

AXES = ("expert", "dp")
CHUNK = 32
VMEM_LIMIT = 48 * 1024 * 1024
F32 = jnp.float32
BF16 = jnp.bfloat16


def vmem():
    return pl.BlockSpec(memory_space=pltpu.VMEM)


def call(body, outs, *args, flops=0, out_specs=None, **kw):
    moved = sum(a.size * a.dtype.itemsize for a in args) + sum(o.size * o.dtype.itemsize for o in outs)
    return pl.pallas_call(
        body,
        out_shape=outs,
        in_specs=[vmem() for _ in args],
        out_specs=[vmem() for _ in outs] if out_specs is None else out_specs,
        compiler_params=pltpu.CompilerParams(vmem_limit_bytes=VMEM_LIMIT),
        cost_estimate=pl.CostEstimate(flops=flops, bytes_accessed=moved, transcendentals=0),
        **kw,
    )(*args)


def shape(*dims, dtype=BF16):
    return jax.ShapeDtypeStruct(dims, dtype)


def exchange(x, mask, total):
    return lax.ppermute(x, AXES, [(i, i ^ mask) for i in range(total)])


def stages(total, core):
    bits = [1 << b for b in reversed(range(total.bit_length() - 1)) if 1 << b != core]
    pairs = [bits[i : i + 2] for i in range(0, len(bits), 2)]
    return [[p[0] * a + (p[1] * b if len(p) > 1 else 0) for a in range(2) for b in range(2 if len(p) > 1 else 1)][1:] for p in pairs]


def pack(tokens, route_ids, route_weights, grad_out, experts):
    rows, width = tokens.shape
    lanes = -(-2 * experts // 128) * 128

    def body(t_ref, i_ref, w_ref, g_ref, o_ref):
        lane = lax.broadcasted_iota(jnp.int32, (rows, lanes), 1)
        ids, weights = i_ref[...], w_ref[...]
        coded = jnp.zeros((rows, lanes), jnp.int32)
        for k in range(ids.shape[1]):
            one, w = ids[:, k : k + 1], weights[:, k : k + 1]
            coded += jnp.where(lane == one, w >> 8, 0) + jnp.where(lane == one + experts, w & 255, 0)
        both = jnp.concatenate([t_ref[...].astype(F32), g_ref[...].astype(F32)], axis=0)
        side = jnp.concatenate([coded.astype(F32), jnp.zeros((rows, lanes), F32)], axis=0)
        o_ref[0] = jnp.concatenate([both, side], axis=1).astype(BF16)

    return call(body, [shape(1, 2 * rows, width + lanes)], tokens, route_ids, route_weights, grad_out)[0]


def selector(blocks, rows, offset):
    t = lax.broadcasted_iota(jnp.int32, (blocks * rows, 2 * blocks * rows), 0)
    s = lax.broadcasted_iota(jnp.int32, (blocks * rows, 2 * blocks * rows), 1)
    return (s == (t // rows) * 2 * rows + offset + t % rows).astype(BF16)


def dot(a, b, ca=1, cb=0):
    return lax.dot_general(a, b, (((ca,), (cb,)), ((), ())), preferred_element_type=F32)


def expert_math(pieces, me, w_gate, w_up, w_down, experts, splits):
    blocks = sum(p.shape[0] for p in pieces)
    rows = pieces[0].shape[1] // 2
    width, hid = w_gate.shape
    lanes = pieces[0].shape[2] - width
    m = blocks * rows
    count = len(pieces)

    def body(*refs):
        me_ref, wg_ref, wu_ref, wd_ref = refs[count : count + 4]
        outs = refs[count + 4 :]
        parts, (t_ref, do_ref, h_ref, dg_ref, du_ref) = outs[: len(splits)], outs[len(splits) :]
        x = jnp.concatenate([r[...].reshape(-1, width + lanes) for r in refs[:count]], axis=0)
        pick_t, pick_g = selector(blocks, rows, 0), selector(blocks, rows, rows)
        token = dot(pick_t, x[:, :width]).astype(BF16)
        t_ref[...] = token
        side = dot(pick_t, x[:, width:])
        lane = lax.broadcasted_iota(jnp.int32, (m, lanes), 1)
        mine = me_ref[0]
        scale = jnp.where(lane == mine, 1.0 / 256.0, 0.0) + jnp.where(lane == mine + experts, 1.0 / 65536.0, 0.0)
        coef = jnp.sum(side * scale, axis=1, keepdims=True)
        dout = (coef * dot(pick_g, x[:, :width])).astype(BF16)
        do_ref[...] = dout
        gate = dot(token, wg_ref[...])
        upper = dot(token, wu_ref[...])
        dact = dot(dout, wd_ref[...], 1, 1)
        sig = jax.nn.sigmoid(gate)
        swish = gate * sig
        hidden = (swish * upper).astype(BF16)
        dgate = (dact * upper * sig * (1.0 + gate * (1.0 - sig))).astype(BF16)
        dupper = (dact * swish).astype(BF16)
        h_ref[...], dg_ref[...], du_ref[...] = hidden, dgate, dupper
        part = (coef * dot(hidden, wd_ref[...])).astype(BF16)
        back = (dot(dgate, wg_ref[...], 1, 1) + dot(dupper, wu_ref[...], 1, 1)).astype(BF16)
        mixed = (dot(pick_t, part, 0, 0) + dot(pick_g, back, 0, 0)).astype(BF16)
        mixed = mixed.reshape(blocks, 2 * rows, width)
        at = 0
        for ref, n in zip(parts, splits):
            ref[...] = mixed[at : at + n]
            at += n

    outs = [shape(n, 2 * rows, width) for n in splits]
    outs += [shape(m, width), shape(m, width), shape(m, hid), shape(m, hid), shape(m, hid)]
    specs = [vmem()] * count + [pl.BlockSpec(memory_space=pltpu.SMEM)] + [vmem()] * 3
    args = [*pieces, me, w_gate, w_up, w_down]
    got = pl.pallas_call(
        body,
        out_shape=outs,
        in_specs=specs,
        out_specs=[vmem() for _ in outs],
        compiler_params=pltpu.CompilerParams(vmem_limit_bytes=VMEM_LIMIT),
        cost_estimate=pl.CostEstimate(flops=12 * m * width * hid, bytes_accessed=10 << 20, transcendentals=m * hid),
    )(*args)
    return list(got[: len(splits)]), got[len(splits) :]


def grad_pair(left, rights, steps):
    m, rows = left.shape
    cols = rights[0].shape[1]
    steps = steps if rows % (128 * steps) == 0 else 1
    tile = rows // steps

    def body(l_ref, *refs):
        for r_ref, o_ref in zip(refs[: len(rights)], refs[len(rights) :]):
            o_ref[...] = dot(l_ref[...], r_ref[...], 0, 0).astype(BF16)

    return pl.pallas_call(
        body,
        grid=(steps,),
        out_shape=[shape(rows, cols) for _ in rights],
        in_specs=[pl.BlockSpec((m, tile), lambda i: (0, i))] + [pl.BlockSpec((m, cols), lambda i: (0, 0)) for _ in rights],
        out_specs=[pl.BlockSpec((tile, cols), lambda i: (i, 0)) for _ in rights],
        compiler_params=pltpu.CompilerParams(vmem_limit_bytes=VMEM_LIMIT),
        cost_estimate=pl.CostEstimate(
            flops=2 * m * rows * cols * len(rights), bytes_accessed=2 * rows * cols * len(rights), transcendentals=0
        ),
    )(left, *rights)


def add_split(terms, splits, last):
    n, rows2, width = terms[0].shape
    rows = rows2 // 2

    def body(*refs):
        total = refs[0][...].astype(F32)
        for r in refs[1 : len(terms)]:
            total += r[...].astype(F32)
        outs = refs[len(terms) :]
        if last:
            outs[0][...] = total[0, :rows].astype(BF16)
            outs[1][...] = total[0, rows:].astype(BF16)
            return
        at = 0
        for ref, k in zip(outs, splits):
            ref[...] = total[at : at + k].astype(ref.dtype)
            at += k

    if last:
        outs = [shape(rows, width), shape(rows, width)]
    else:
        outs = [shape(k, rows2, width, dtype=F32 if i == 0 else BF16) for i, k in enumerate(splits)]
    return call(body, outs, *terms)


def on_device(tokens, route_ids, route_weights, w_gate, w_up, w_down, grad_out):
    experts = w_gate.shape[0] * lax.axis_size("expert")
    core = lax.axis_size("dp")
    total = lax.axis_size("expert") * core
    plan = stages(total, core)
    me = lax.axis_index("expert").astype(jnp.int32).reshape(1)
    wg, wu, wd = w_gate[0], w_up[0], w_down[0]

    held = [pack(tokens, route_ids, route_weights, grad_out, experts)]
    for masks in plan:
        block = held[0] if len(held) == 1 else jnp.concatenate(held, axis=0)
        held = [block] + [exchange(block, mask, total) for mask in masks]
    pieces = held + [exchange(h, core, total) for h in held]

    half = total // 2
    if total <= CHUNK:
        (keep, send), kept = expert_math(pieces, me, wg, wu, wd, experts, [half, half])
    else:
        whole = jnp.concatenate(pieces, axis=0)
        sums, saved = [], []
        for at in range(0, total, CHUNK):
            (got,), rest = expert_math([whole[at : at + CHUNK]], me, wg, wu, wd, experts, [CHUNK])
            sums.append(got)
            saved.append(rest)
        got = jnp.concatenate(sums, axis=0)
        keep, send = got[:half], got[half:]
        kept = [jnp.concatenate(parts, axis=0) for parts in zip(*saved)]
    token, dout, hidden, dgate, dupper = kept

    terms = [keep, exchange(send, core, total)]
    for masks in reversed(plan):
        n = terms[0].shape[0] // (len(masks) + 1)
        mine, *others = add_split(terms, [n] * (len(masks) + 1), False)
        terms = [mine] + [exchange(o, mask, total) for o, mask in zip(others, masks)]
    mixed, back = add_split(terms, None, True)

    gate_grad, up_grad = grad_pair(token, [dgate, dupper], 4)
    (down_grad,) = grad_pair(hidden, [dout], 4)
    return mixed, back, gate_grad[None], up_grad[None], down_grad[None]


def solution(mesh):
    rows = P(("groups", "expert", "dp"), None)
    in_specs = (rows, rows, rows, P("expert", None, "dp"), P("expert", None, "dp"), P("expert", "dp", None), rows)
    hidden = P(("groups", "expert"), None, "dp")
    out_specs = (rows, rows, hidden, hidden, P(("groups", "expert"), "dp", None))
    return jax.shard_map(on_device, mesh=mesh, in_specs=in_specs, out_specs=out_specs, check_vma=False)
```

time: 119 us -> 54.1 us (0.45)
  blocking collectives: 29 us -> 0 us
  matrix products: 17.1 us -> 0 us
  local copies, waits for them, and re-layouts: 21.2 us -> 4.38 us
  other arithmetic: 13 us -> 0.03 us
  Pallas kernels: 0 us -> 12.5 us
  starting transfers between devices: 19.4 us -> 18.2 us
    all_to_all x4 -> x0, starting transfers between devices: 19.4 us -> none  [the longest x1 6.43 us: on_device(): lax.all_to_all(send_tokens, 'expert', split_axis=0, concat_axis=1, tiled=...]
    all_gather x4 -> x0, blocking collectives: 19.3 us -> none  [the longest x1 5.57 us: on_device(): lax.all_gather(route_ids, 'dp', axis=0, tiled=True)]
    ppermute x0 -> x17, starting transfers between devices: none -> 18.2 us  [exchange(): return lax.ppermute(x, AXES, [(i, i ^ mask) for i in range(total)])]
    ppermute x0 -> x17, waiting for transfers between devices: none -> 17.9 us  [exchange(): return lax.ppermute(x, AXES, [(i, i ^ mask) for i in range(total)])]
    dot_general x9 -> x0, matrix products: 17.1 us -> none  [the longest x1 3.09 us: expert_math(): jnp.einsum('emf,emd->efd', hidden, grad_rows, preferred_element_type=jnp....]
    all_to_all x4 -> x0, waiting for transfers between devices: 16.9 us -> none  [the longest x1 10.4 us: on_device(): lax.all_to_all(send_grads, 'expert', split_axis=0, concat_axis=1, tiled=T...]
    pallas_call x0 -> x7, Pallas kernels: none -> 12.5 us  [the longest x1 5.82 us: expert_math(): pl.pallas_call(body, out_shape=outs, in_specs=specs, out_specs=[vmem() fo...]
    unnamed x2 -> x0, other arithmetic: 10.3 us -> none
  transfers between devices with their start and end apart: 4 -> 17, of which waited for: 4 -> 9; matrix products, arithmetic and copies ran while one was open for 26% -> 0% of each run, Pallas kernels for 0% -> 11%
where the time goes in v1:
time: 54.1 us; the launch traced here: 53.7 us
  starting transfers between devices  18.2 us (34%)
  waiting for transfers between devices  17.9 us (33%)
  Pallas kernels  12.5 us (23%)
  local copies, waits for them, and re-layouts  4.38 us (8%)
  between operations  0.69 us (1%)
    ppermute x17, starting transfers between devices, exchange(): return lax.ppermute(x, AXES, [(i, i ^ mask) for i in range(total)])  18.2 us
    ppermute x17, waiting for transfers between devices, exchange(): return lax.ppermute(x, AXES, [(i, i ^ mask) for i in range(total)])  17.9 us
    pallas_call x1, Pallas kernels, expert_math(): pl.pallas_call(body, out_shape=outs, in_specs=specs, out_specs=[vmem() fo...  5.82 us
    pallas_call x2, Pallas kernels, grad_pair(): pl.pallas_call(body, grid=(steps,), out_shape=[shape(rows, cols) for _ in...  5.71 us
    unnamed x10, local copies, waits for them, and re-layouts  4.38 us
  transfers between devices with their start and end apart: 17, of which 9 were waited for; matrix products, arithmetic and copies ran while one was open for 0% of the time, Pallas kernels for 11%

profile of v1, /device:TPU:0, one launch (start us, length us, event | category | flops | bytes accessed | tf_op | source)
XLA Modules:
  0.0 53.7 jit_solution(15129722280497518944)
XLA Ops:
  0.6 0.0 copy-start.1
  0.6 0.7 %copy-done.1 = bf16[4,2048]{1,0:T(4,128)(2,1)S(1)} copy-done((bf16[4,2048]{1,0:T(4,128)(2,1)S(1)}, bf16[4,2048]{1,0:T(4,128)(2,1)}, u32[]{:S(2)}) %copy-start.1) | copy-done | bytes 16408
  1.4 0.0 copy-start.2
  1.4 0.7 %copy-done.2 = bf16[4,2048]{1,0:T(4,128)(2,1)S(1)} copy-done((bf16[4,2048]{1,0:T(4,128)(2,1)S(1)}, bf16[4,2048]{1,0:T(4,128)(2,1)}, u32[]{:S(2)}) %copy-start.2) | copy-done | bytes 16408
  2.1 0.0 copy-start.3
  2.1 0.7 %copy-done.3 = s32[4,8]{1,0:T(4,128)S(1)} copy-done((s32[4,8]{1,0:T(4,128)S(1)}, s32[4,8]{1,0:T(4,128)}, u32[]{:S(2)}) %copy-start.3) | copy-done | bytes 152
  2.8 0.0 copy-start.4
  2.8 0.7 %copy-done.4 = s32[4,8]{1,0:T(4,128)S(1)} copy-done((s32[4,8]{1,0:T(4,128)S(1)}, s32[4,8]{1,0:T(4,128)}, u32[]{:S(2)}) %copy-start.4) | copy-done | bytes 152
  3.4 0.1 shard_map.110
  3.5 5.1 %collective-permute-start.2 = (bf16[1,8,2176]{2,1,0:T(8,128)(2,1)S(1)}, bf16[1,8,2176]{2,1,0:T(8,128)(2,1)S(1)}, u32[]{:S(2)}, u32[]{:S(2)}) collective-permute-start(bf16[1,8,2176]{2,1,0:T(8,128)(2,1)S(1)} %shard_map.110), channel_id=1, source_target_pairs={{0,24},{1,25},{2,26},{3,27},{4,28},{5,29},{6,30},{7,31},{8,16},{9,... | collective-permute-start | bytes 104456 | tf_op jit(solution)/shard_map/ppermute | solution.py:37
  8.7 0.0 collective-permute-start.1
  8.7 0.6 %collective-permute-start = (bf16[1,8,2176]{2,1,0:T(8,128)(2,1)S(1)}, bf16[1,8,2176]{2,1,0:T(8,128)(2,1)S(1)}, u32[]{:S(2)}, u32[]{:S(2)}) collective-permute-start(bf16[1,8,2176]{2,1,0:T(8,128)(2,1)S(1)} %shard_map.110), channel_id=1, source_target_pairs={{0,8},{1,9},{2,10},{3,11},{4,12},{5,13},{6,14},{7,15},{8,0},{9,1},... | collective-permute-start | bytes 104456 | tf_op jit(solution)/shard_map/ppermute | solution.py:37
  9.3 1.3 %collective-permute-done.2 = bf16[1,8,2176]{2,1,0:T(8,128)(2,1)S(1)} collective-permute-done((bf16[1,8,2176]{2,1,0:T(8,128)(2,1)S(1)}, bf16[1,8,2176]{2,1,0:T(8,128)(2,1)S(1)}, u32[]{:S(2)}, u32[]{:S(2)}) %collective-permute-start.2) | collective-permute-done | bytes 34848 | tf_op jit(solution)/shard_map/ppermute | solution.py:37
  10.6 2.9 %collective-permute-done.1 = bf16[1,8,2176]{2,1,0:T(8,128)(2,1)S(1)} collective-permute-done((bf16[1,8,2176]{2,1,0:T(8,128)(2,1)S(1)}, bf16[1,8,2176]{2,1,0:T(8,128)(2,1)S(1)}, u32[]{:S(2)}, u32[]{:S(2)}) %collective-permute-start.1) | collective-permute-done | bytes 34848 | tf_op jit(solution)/shard_map/ppermute | solution.py:37
  13.5 0.0 collective-permute-done
  13.5 1.6 %collective-permute-start.3 = (bf16[4,8,2176]{2,1,0:T(8,128)(2,1)S(1)}, bf16[4,8,2176]{2,1,0:T(8,128)(2,1)S(1)}, u32[]{:S(2)}, u32[]{:S(2)}) collective-permute-start(bf16[4,8,2176]{2,1,0:T(8,128)(2,1)S(1)} %pad_maximum_fusion.refs_0_), channel_id=1, source_target_pairs={{0,1},{1,0},{2,3},{3,2},{4,5},{5,4},{6,7},{7,6},{8,9},{9,8},{10,11... | collective-permute-start | bytes 417800 | tf_op jit(solution)/shard_map/ppermute | solution.py:37
  15.1 1.5 %collective-permute-start.4 = (bf16[4,8,2176]{2,1,0:T(8,128)(2,1)S(1)}, bf16[4,8,2176]{2,1,0:T(8,128)(2,1)S(1)}, u32[]{:S(2)}, u32[]{:S(2)}) collective-permute-start(bf16[4,8,2176]{2,1,0:T(8,128)(2,1)S(1)} %pad_maximum_fusion.refs_0_), channel_id=1, source_target_pairs={{0,4},{1,5},{2,6},{3,7},{4,0},{5,1},{6,2},{7,3},{8,12},{9,13},{10,... | collective-permute-start | bytes 417800 | tf_op jit(solution)/shard_map/ppermute | solution.py:37
  16.6 0.5 collective-permute-start.5
  17.1 0.0 collective-permute-start.6
  17.1 2.9 %collective-permute-done.3.refs_1_ = bf16[4,8,2176]{2,1,0:T(8,128)(2,1)S(1)} collective-permute-done((bf16[4,8,2176]{2,1,0:T(8,128)(2,1)S(1)}, bf16[4,8,2176]{2,1,0:T(8,128)(2,1)S(1)}, u32[]{:S(2)}, u32[]{:S(2)}) %collective-permute-start.3) | collective-permute-done | bytes 139296 | tf_op jit(solution)/shard_map/ppermute | solution.py:37
  20.0 0.0 collective-permute-start.7
  20.0 2.7 %collective-permute-done.4.refs_2_ = bf16[4,8,2176]{2,1,0:T(8,128)(2,1)S(1)} collective-permute-done((bf16[4,8,2176]{2,1,0:T(8,128)(2,1)S(1)}, bf16[4,8,2176]{2,1,0:T(8,128)(2,1)S(1)}, u32[]{:S(2)}, u32[]{:S(2)}) %collective-permute-start.4) | collective-permute-done | bytes 139296 | tf_op jit(solution)/shard_map/ppermute | solution.py:37
  22.7 0.0 collective-permute-start.8
  22.7 0.0 collective-permute-done.5.refs_3_
  22.7 0.5 collective-permute-start.9
  23.2 0.0 collective-permute-done.6.refs_4_
  23.2 0.0 collective-permute-done.7.refs_5_
  23.2 0.8 %collective-permute-done.8.refs_6_ = bf16[4,8,2176]{2,1,0:T(8,128)(2,1)S(1)} collective-permute-done((bf16[4,8,2176]{2,1,0:T(8,128)(2,1)S(1)}, bf16[4,8,2176]{2,1,0:T(8,128)(2,1)S(1)}, u32[]{:S(2)}, u32[]{:S(2)}) %collective-permute-start.8) | collective-permute-done | bytes 139296 | tf_op jit(solution)/shard_map/ppermute | solution.py:37
  24.1 0.2 collective-permute-done.9.refs_7_
  24.3 0.0 copy-start
  24.3 1.6 %copy-done = bf16[1,2048,512]{2,1,0:T(8,128)(2,1)S(1)} copy-done((bf16[1,2048,512]{2,1,0:T(8,128)(2,1)S(1)}, bf16[1,2048,512]{2,1,0:T(8,128)(2,1)}, u32[]{:S(2)}) %copy-start) | copy-done | bytes 2097176
  25.8 5.8 %shard_map.111 = (bf16[16,8,2048]{2,1,0:T(8,128)(2,1)S(1)}, bf16[16,8,2048]{2,1,0:T(8,128)(2,1)S(1)}, bf16[128,2048]{1,0:T(8,128)(2,1)S(1)}, bf16[128,2048]{1,0:...) custom-call(bf16[4,8,2176]{2,1,0:T(8,128)(2,1)S(1)} %pad_maximum_fusion., ...), custom_call_target="tpu_custom_call" | custom-call | flops 1610612736 | bytes 10485760 | tf_op jit(solution)/shard_map/pallas_call | solution.py:119
  31.7 0.4 collective-permute-start.10
  32.1 1.6 %collective-permute-done.10.refs_1_ = bf16[16,8,2048]{2,1,0:T(8,128)(2,1)S(1)} collective-permute-done((bf16[16,8,2048]{2,1,0:T(8,128)(2,1)S(1)}, bf16[16,8,2048]{2,1,0:T(8,128)(2,1)S(1)}, u32[]{:S(2)}, u32[]{:S(2)}) %collective-permute-start.10) | collective-permute-done | bytes 524320 | tf_op jit(solution)/shard_map/ppermute | solution.py:37
  33.6 0.1 shard_map.112
  33.8 0.3 collective-permute-start.11
  34.0 0.9 %collective-permute-start.12 = (bf16[4,8,2048]{2,1,0:T(8,128)(2,1)S(1)}, bf16[4,8,2048]{2,1,0:T(8,128)(2,1)S(1)}, u32[]{:S(2)}, u32[]{:S(2)}) collective-permute-start(bf16[4,8,2048]{2,1,0:T(8,128)(2,1)S(1)} %get-tuple-element.28), channel_id=1, source_target_pairs={{0,4},{1,5},{2,6},{3,7},{4,0},{5,1},{6,2},{7,3},{8,12},{9,13},{10,... | collective-permute-start | bytes 393224 | tf_op jit(solution)/shard_map/ppermute | solution.py:37
  35.0 2.3 %collective-permute-start.13 = (bf16[4,8,2048]{2,1,0:T(8,128)(2,1)S(1)}, bf16[4,8,2048]{2,1,0:T(8,128)(2,1)S(1)}, u32[]{:S(2)}, u32[]{:S(2)}) collective-permute-start(bf16[4,8,2048]{2,1,0:T(8,128)(2,1)S(1)} %get-tuple-element.29), channel_id=1, source_target_pairs={{0,5},{1,4},{2,7},{3,6},{4,1},{5,0},{6,3},{7,2},{8,13},{9,12},{10,... | collective-permute-start | bytes 393224 | tf_op jit(solution)/shard_map/ppermute | solution.py:37
  37.3 2.8 %collective-permute-done.11.refs_1_ = bf16[4,8,2048]{2,1,0:T(8,128)(2,1)S(1)} collective-permute-done((bf16[4,8,2048]{2,1,0:T(8,128)(2,1)S(1)}, bf16[4,8,2048]{2,1,0:T(8,128)(2,1)S(1)}, u32[]{:S(2)}, u32[]{:S(2)}) %collective-permute-start.11) | collective-permute-done | bytes 131104 | tf_op jit(solution)/shard_map/ppermute | solution.py:37
  40.2 0.0 collective-permute-done.12.refs_2_
  40.2 2.7 %collective-permute-done.13.refs_3_ = bf16[4,8,2048]{2,1,0:T(8,128)(2,1)S(1)} collective-permute-done((bf16[4,8,2048]{2,1,0:T(8,128)(2,1)S(1)}, bf16[4,8,2048]{2,1,0:T(8,128)(2,1)S(1)}, u32[]{:S(2)}, u32[]{:S(2)}) %collective-permute-start.13) | collective-permute-done | bytes 131104 | tf_op jit(solution)/shard_map/ppermute | solution.py:37
  42.8 0.1 shard_map.113
  42.9 0.1 collective-permute-start.14
  43.0 2.2 %collective-permute-start.15 = (bf16[1,8,2048]{2,1,0:T(8,128)(2,1)S(1)}, bf16[1,8,2048]{2,1,0:T(8,128)(2,1)S(1)}, u32[]{:S(2)}, u32[]{:S(2)}) collective-permute-start(bf16[1,8,2048]{2,1,0:T(8,128)(2,1)S(1)} %get-tuple-element.32), channel_id=1, source_target_pairs={{0,16},{1,17},{2,18},{3,19},{4,20},{5,21},{6,22},{7,23},{8,24},{9,... | collective-permute-start | bytes 98312 | tf_op jit(solution)/shard_map/ppermute | solution.py:37
  45.3 2.1 %collective-permute-start.16 = (bf16[1,8,2048]{2,1,0:T(8,128)(2,1)S(1)}, bf16[1,8,2048]{2,1,0:T(8,128)(2,1)S(1)}, u32[]{:S(2)}, u32[]{:S(2)}) collective-permute-start(bf16[1,8,2048]{2,1,0:T(8,128)(2,1)S(1)} %get-tuple-element.33), channel_id=1, source_target_pairs={{0,24},{1,25},{2,26},{3,27},{4,28},{5,29},{6,30},{7,31},{8,16},{9,... | collective-permute-start | bytes 98312 | tf_op jit(solution)/shard_map/ppermute | solution.py:37
  47.3 3.1 %shard_map.115 = (bf16[2048,512]{1,0:T(8,128)(2,1)}, bf16[2048,512]{1,0:T(8,128)(2,1)}) custom-call(bf16[128,2048]{1,0:T(8,128)(2,1)S(1)} %get-tuple-element.36.l_ref, bf16[128,512]{1,0:T(8,128)(2,1)S(1)} %get-tuple-element.37.refs_0_, bf16[128,512]{1,0:T(8,128)(2,1)S(1)} %get-tuple-element.38.refs_1_), custom_call_target="tpu_custom_call" | custom-call | flops 536870912 | bytes 4194304 | tf_op jit(solution)/shard_map/pallas_call | solution.py:140
  50.4 2.6 %shard_map.116 = bf16[512,2048]{1,0:T(8,128)(2,1)} custom-call(bf16[128,512]{1,0:T(8,128)(2,1)S(1)} %get-tuple-element.41.l_ref, bf16[128,2048]{1,0:T(8,128)(2,1)S(1)} %get-tuple-element.42.refs_0_), custom_call_target="tpu_custom_call" | custom-call | flops 268435456 | bytes 2097152 | tf_op jit(solution)/shard_map/pallas_call | solution.py:140
  53.0 0.0 collective-permute-done.14.refs_1_
  53.0 0.0 collective-permute-done.15.refs_2_
  53.1 0.0 collective-permute-done.16.refs_3_
  53.1 0.6 %shard_map.114 = (bf16[4,2048]{1,0:T(4,128)(2,1)}, bf16[4,2048]{1,0:T(4,128)(2,1)}) custom-call(f32[1,8,2048]{2,1,0:T(8,128)S(1)} %get-tuple-element.30.refs_0_, bf16[1,8,2048]{2,1,0:T(8,128)(2,1)S(1)} %collective-permute-done.14.refs_1_, bf16[1,8,2048]{2,1,0:T(8,128)(2,1)S(1)} %collective-permute-done.15.refs_2_, ...), custom_call_target="tpu_custom_call" | custom-call | bytes 196608 | tf_op jit(solution)/shard_map/pallas_call | solution.py:21
  (1 shorter events, 0.0 us)
Async XLA Ops:
  0.6 0.7 %copy-start.1 = (bf16[4,2048]{1,0:T(4,128)(2,1)S(1)}, bf16[4,2048]{1,0:T(4,128)(2,1)}, u32[]{:S(2)}) copy-start(bf16[4,2048]{1,0:T(4,128)(2,1)} %t_ref.1) | copy-start | bytes 49156
  1.4 0.7 %copy-start.2 = (bf16[4,2048]{1,0:T(4,128)(2,1)S(1)}, bf16[4,2048]{1,0:T(4,128)(2,1)}, u32[]{:S(2)}) copy-start(bf16[4,2048]{1,0:T(4,128)(2,1)} %g_ref.1) | copy-start | bytes 49156
  2.1 0.7 %copy-start.3 = (s32[4,8]{1,0:T(4,128)S(1)}, s32[4,8]{1,0:T(4,128)}, u32[]{:S(2)}) copy-start(s32[4,8]{1,0:T(4,128)} %i_ref.1) | copy-start | bytes 388
  2.8 0.7 %copy-start.4 = (s32[4,8]{1,0:T(4,128)S(1)}, s32[4,8]{1,0:T(4,128)}, u32[]{:S(2)}) copy-start(s32[4,8]{1,0:T(4,128)} %w_ref.1) | copy-start | bytes 388
  3.5 7.0 %collective-permute-start.2 = (bf16[1,8,2176]{2,1,0:T(8,128)(2,1)S(1)}, bf16[1,8,2176]{2,1,0:T(8,128)(2,1)S(1)}, u32[]{:S(2)}, u32[]{:S(2)}) collective-permute-start(bf16[1,8,2176]{2,1,0:T(8,128)(2,1)S(1)} %shard_map.110), channel_id=1, source_target_pairs={{0,24},{1,25},{2,26},{3,27},{4,28},{5,29},{6,30},{7,31},{8,16},{9,... | collective-permute-start | bytes 104456 | tf_op jit(solution)/shard_map/ppermute | solution.py:37
  8.7 4.8 %collective-permute-start.1 = (bf16[1,8,2176]{2,1,0:T(8,128)(2,1)S(1)}, bf16[1,8,2176]{2,1,0:T(8,128)(2,1)S(1)}, u32[]{:S(2)}, u32[]{:S(2)}) collective-permute-start(bf16[1,8,2176]{2,1,0:T(8,128)(2,1)S(1)} %shard_map.110), channel_id=1, source_target_pairs={{0,16},{1,17},{2,18},{3,19},{4,20},{5,21},{6,22},{7,23},{8,24},{9,... | collective-permute-start | bytes 104456 | tf_op jit(solution)/shard_map/ppermute | solution.py:37
  8.7 4.8 %collective-permute-start = (bf16[1,8,2176]{2,1,0:T(8,128)(2,1)S(1)}, bf16[1,8,2176]{2,1,0:T(8,128)(2,1)S(1)}, u32[]{:S(2)}, u32[]{:S(2)}) collective-permute-start(bf16[1,8,2176]{2,1,0:T(8,128)(2,1)S(1)} %shard_map.110), channel_id=1, source_target_pairs={{0,8},{1,9},{2,10},{3,11},{4,12},{5,13},{6,14},{7,15},{8,0},{9,1},... | collective-permute-start | bytes 104456 | tf_op jit(solution)/shard_map/ppermute | solution.py:37
  13.5 6.4 %collective-permute-start.3 = (bf16[4,8,2176]{2,1,0:T(8,128)(2,1)S(1)}, bf16[4,8,2176]{2,1,0:T(8,128)(2,1)S(1)}, u32[]{:S(2)}, u32[]{:S(2)}) collective-permute-start(bf16[4,8,2176]{2,1,0:T(8,128)(2,1)S(1)} %pad_maximum_fusion.refs_0_), channel_id=1, source_target_pairs={{0,1},{1,0},{2,3},{3,2},{4,5},{5,4},{6,7},{7,6},{8,9},{9,8},{10,11... | collective-permute-start | bytes 417800 | tf_op jit(solution)/shard_map/ppermute | solution.py:37
  15.1 7.6 %collective-permute-start.4 = (bf16[4,8,2176]{2,1,0:T(8,128)(2,1)S(1)}, bf16[4,8,2176]{2,1,0:T(8,128)(2,1)S(1)}, u32[]{:S(2)}, u32[]{:S(2)}) collective-permute-start(bf16[4,8,2176]{2,1,0:T(8,128)(2,1)S(1)} %pad_maximum_fusion.refs_0_), channel_id=1, source_target_pairs={{0,4},{1,5},{2,6},{3,7},{4,0},{5,1},{6,2},{7,3},{8,12},{9,13},{10,... | collective-permute-start | bytes 417800 | tf_op jit(solution)/shard_map/ppermute | solution.py:37
  16.6 6.1 %collective-permute-start.5 = (bf16[4,8,2176]{2,1,0:T(8,128)(2,1)S(1)}, bf16[4,8,2176]{2,1,0:T(8,128)(2,1)S(1)}, u32[]{:S(2)}, u32[]{:S(2)}) collective-permute-start(bf16[4,8,2176]{2,1,0:T(8,128)(2,1)S(1)} %pad_maximum_fusion.refs_0_), channel_id=1, source_target_pairs={{0,5},{1,4},{2,7},{3,6},{4,1},{5,0},{6,3},{7,2},{8,13},{9,12},{10,... | collective-permute-start | bytes 417800 | tf_op jit(solution)/shard_map/ppermute | solution.py:37
  17.1 6.1 %collective-permute-start.6 = (bf16[4,8,2176]{2,1,0:T(8,128)(2,1)S(1)}, bf16[4,8,2176]{2,1,0:T(8,128)(2,1)S(1)}, u32[]{:S(2)}, u32[]{:S(2)}) collective-permute-start(bf16[4,8,2176]{2,1,0:T(8,128)(2,1)S(1)} %pad_maximum_fusion.refs_0_), channel_id=1, source_target_pairs={{0,2},{1,3},{2,0},{3,1},{4,6},{5,7},{6,4},{7,5},{8,10},{9,11},{10,... | collective-permute-start | bytes 417800 | tf_op jit(solution)/shard_map/ppermute | solution.py:37
  20.0 3.2 %collective-permute-start.7 = (bf16[4,8,2176]{2,1,0:T(8,128)(2,1)S(1)}, bf16[4,8,2176]{2,1,0:T(8,128)(2,1)S(1)}, u32[]{:S(2)}, u32[]{:S(2)}) collective-permute-start(bf16[4,8,2176]{2,1,0:T(8,128)(2,1)S(1)} %collective-permute-done.3.refs_1_), channel_id=1, source_target_pairs={{0,2},{1,3},{2,0},{3,1},{4,6},{5,7},{6,4},{7,5},{8,10},{9,11},{10,... | collective-permute-start | bytes 417800 | tf_op jit(solution)/shard_map/ppermute | solution.py:37
  22.7 1.4 %collective-permute-start.8 = (bf16[4,8,2176]{2,1,0:T(8,128)(2,1)S(1)}, bf16[4,8,2176]{2,1,0:T(8,128)(2,1)S(1)}, u32[]{:S(2)}, u32[]{:S(2)}) collective-permute-start(bf16[4,8,2176]{2,1,0:T(8,128)(2,1)S(1)} %collective-permute-done.4.refs_2_), channel_id=1, source_target_pairs={{0,2},{1,3},{2,0},{3,1},{4,6},{5,7},{6,4},{7,5},{8,10},{9,11},{10,... | collective-permute-start | bytes 417800 | tf_op jit(solution)/shard_map/ppermute | solution.py:37
  22.7 1.6 %collective-permute-start.9 = (bf16[4,8,2176]{2,1,0:T(8,128)(2,1)S(1)}, bf16[4,8,2176]{2,1,0:T(8,128)(2,1)S(1)}, u32[]{:S(2)}, u32[]{:S(2)}) collective-permute-start(bf16[4,8,2176]{2,1,0:T(8,128)(2,1)S(1)} %collective-permute-done.5.refs_3_), channel_id=1, source_target_pairs={{0,2},{1,3},{2,0},{3,1},{4,6},{5,7},{6,4},{7,5},{8,10},{9,11},{10,... | collective-permute-start | bytes 417800 | tf_op jit(solution)/shard_map/ppermute | solution.py:37
  24.3 1.6 %copy-start = (bf16[1,2048,512]{2,1,0:T(8,128)(2,1)S(1)}, bf16[1,2048,512]{2,1,0:T(8,128)(2,1)}, u32[]{:S(2)}) copy-start(bf16[1,2048,512]{2,1,0:T(8,128)(2,1)} %param.10) | copy-start | bytes 6291460
  31.7 2.0 %collective-permute-start.10 = (bf16[16,8,2048]{2,1,0:T(8,128)(2,1)S(1)}, bf16[16,8,2048]{2,1,0:T(8,128)(2,1)S(1)}, u32[]{:S(2)}, u32[]{:S(2)}) collective-permute-start(bf16[16,8,2048]{2,1,0:T(8,128)(2,1)S(1)} %get-tuple-element.25), channel_id=1, source_target_pairs={{0,2},{1,3},{2,0},{3,1},{4,6},{5,7},{6,4},{7,5},{8,10},{9,11},{10,... | collective-permute-start | bytes 1572872 | tf_op jit(solution)/shard_map/ppermute | solution.py:37
  33.8 6.4 %collective-permute-start.11 = (bf16[4,8,2048]{2,1,0:T(8,128)(2,1)S(1)}, bf16[4,8,2048]{2,1,0:T(8,128)(2,1)S(1)}, u32[]{:S(2)}, u32[]{:S(2)}) collective-permute-start(bf16[4,8,2048]{2,1,0:T(8,128)(2,1)S(1)} %get-tuple-element.27), channel_id=1, source_target_pairs={{0,1},{1,0},{2,3},{3,2},{4,5},{5,4},{6,7},{7,6},{8,9},{9,8},{10,11... | collective-permute-start | bytes 393224 | tf_op jit(solution)/shard_map/ppermute | solution.py:37
  34.0 6.1 %collective-permute-start.12 = (bf16[4,8,2048]{2,1,0:T(8,128)(2,1)S(1)}, bf16[4,8,2048]{2,1,0:T(8,128)(2,1)S(1)}, u32[]{:S(2)}, u32[]{:S(2)}) collective-permute-start(bf16[4,8,2048]{2,1,0:T(8,128)(2,1)S(1)} %get-tuple-element.28), channel_id=1, source_target_pairs={{0,4},{1,5},{2,6},{3,7},{4,0},{5,1},{6,2},{7,3},{8,12},{9,13},{10,... | collective-permute-start | bytes 393224 | tf_op jit(solution)/shard_map/ppermute | solution.py:37
  35.0 7.8 %collective-permute-start.13 = (bf16[4,8,2048]{2,1,0:T(8,128)(2,1)S(1)}, bf16[4,8,2048]{2,1,0:T(8,128)(2,1)S(1)}, u32[]{:S(2)}, u32[]{:S(2)}) collective-permute-start(bf16[4,8,2048]{2,1,0:T(8,128)(2,1)S(1)} %get-tuple-element.29), channel_id=1, source_target_pairs={{0,5},{1,4},{2,7},{3,6},{4,1},{5,0},{6,3},{7,2},{8,13},{9,12},{10,... | collective-permute-start | bytes 393224 | tf_op jit(solution)/shard_map/ppermute | solution.py:37
  42.9 10.2 %collective-permute-start.14 = (bf16[1,8,2048]{2,1,0:T(8,128)(2,1)S(1)}, bf16[1,8,2048]{2,1,0:T(8,128)(2,1)S(1)}, u32[]{:S(2)}, u32[]{:S(2)}) collective-permute-start(bf16[1,8,2048]{2,1,0:T(8,128)(2,1)S(1)} %get-tuple-element.31), channel_id=1, source_target_pairs={{0,8},{1,9},{2,10},{3,11},{4,12},{5,13},{6,14},{7,15},{8,0},{9,1},... | collective-permute-start | bytes 98312 | tf_op jit(solution)/shard_map/ppermute | solution.py:37
  43.0 10.0 %collective-permute-start.15 = (bf16[1,8,2048]{2,1,0:T(8,128)(2,1)S(1)}, bf16[1,8,2048]{2,1,0:T(8,128)(2,1)S(1)}, u32[]{:S(2)}, u32[]{:S(2)}) collective-permute-start(bf16[1,8,2048]{2,1,0:T(8,128)(2,1)S(1)} %get-tuple-element.32), channel_id=1, source_target_pairs={{0,16},{1,17},{2,18},{3,19},{4,20},{5,21},{6,22},{7,23},{8,24},{9,... | collective-permute-start | bytes 98312 | tf_op jit(solution)/shard_map/ppermute | solution.py:37
  45.3 7.8 %collective-permute-start.16 = (bf16[1,8,2048]{2,1,0:T(8,128)(2,1)S(1)}, bf16[1,8,2048]{2,1,0:T(8,128)(2,1)S(1)}, u32[]{:S(2)}, u32[]{:S(2)}) collective-permute-start(bf16[1,8,2048]{2,1,0:T(8,128)(2,1)S(1)} %get-tuple-element.33), channel_id=1, source_target_pairs={{0,24},{1,25},{2,26},{3,27},{4,28},{5,29},{6,30},{7,31},{8,16},{9,... | collective-permute-start | bytes 98312 | tf_op jit(solution)/shard_map/ppermute | solution.py:37

commit v2 on v1

v2 whole, which is shorter than its diff:
```python
import jax
import jax.numpy as jnp
from jax import lax
from jax.experimental import pallas as pl
from jax.experimental.pallas import tpu as pltpu
from jax.sharding import PartitionSpec as P

AXES = ("expert", "dp")
CHUNK = 32
ROWS = 4
VMEM_LIMIT = 16 * 1024 * 1024
F32 = jnp.float32
BF16 = jnp.bfloat16


def vmem():
    return pl.BlockSpec(memory_space=pltpu.VMEM)


def hbm():
    return pl.BlockSpec(memory_space=pltpu.HBM)


def outside(arrays):
    return [pltpu.with_memory_space_constraint(a, pltpu.HBM) for a in arrays]


def shape(*dims, dtype=BF16):
    return jax.ShapeDtypeStruct(dims, dtype)


def params():
    return pltpu.CompilerParams(vmem_limit_bytes=VMEM_LIMIT)


def cost(flops, moved):
    return pl.CostEstimate(flops=flops, bytes_accessed=moved, transcendentals=0)


def dot(a, b, ca=1, cb=0):
    return lax.dot_general(a, b, (((ca,), (cb,)), ((), ())), preferred_element_type=F32)


def exchange(x, masks, total, core):
    return lax.ppermute(x, AXES, [(i, i ^ masks[i // core % 2]) for i in range(total)])


def stages(total, core):
    bits = [1 << b for b in reversed(range(total.bit_length() - 1)) if 1 << b != core]
    plan = []
    while bits:
        a, bits = bits[0], bits[1:]
        if not bits:
            plan.append([(a, a)])
            continue
        b, bits = bits[0], bits[1:]
        if (a > core) == (b > core) and b > 2 * core:
            plan.append([(b, b), (a, a), (a + b, a + b)])
        else:
            plan.append([(b, a), (a, b), (a + b, a + b)])
    return plan


def pack(tokens, route_ids, route_weights, grad_out, experts):
    rows, width = tokens.shape
    lanes = -(-2 * experts // 128) * 128

    def body(t_in, i_in, w_in, g_in, o_ref, t_ref, i_ref, w_ref, g_ref, sems):
        pairs = ((t_in, t_ref), (i_in, i_ref), (w_in, w_ref), (g_in, g_ref))
        copies = [pltpu.make_async_copy(a, b, sems.at[k]) for k, (a, b) in enumerate(pairs)]
        for c in copies:
            c.start()
        for c in copies:
            c.wait()
        lane = lax.broadcasted_iota(jnp.int32, (rows, lanes), 1)
        ids, weights = i_ref[...], w_ref[...]
        coded = jnp.zeros((rows, lanes), jnp.int32)
        for k in range(ids.shape[1]):
            one, w = ids[:, k : k + 1], weights[:, k : k + 1]
            coded += jnp.where(lane == one, w >> 8, 0) + jnp.where(lane == one + experts, w & 255, 0)
        both = jnp.concatenate([t_ref[...].astype(F32), g_ref[...].astype(F32)], axis=0)
        side = jnp.concatenate([coded.astype(F32), jnp.zeros((rows, lanes), F32)], axis=0)
        o_ref[0] = jnp.concatenate([both, side], axis=1).astype(BF16)

    args = (tokens, route_ids, route_weights, grad_out)
    return pl.pallas_call(
        body,
        out_shape=shape(1, 2 * rows, width + lanes),
        in_specs=[hbm() for _ in args],
        out_specs=vmem(),
        scratch_shapes=[pltpu.VMEM(a.shape, a.dtype) for a in args] + [pltpu.SemaphoreType.DMA((len(args),))],
        compiler_params=params(),
        cost_estimate=cost(0, 80 << 10),
    )(*outside(args))


def fetch(arrays, after):
    def body(*refs):
        n = len(arrays)
        copies = [pltpu.make_async_copy(refs[k], refs[n + 1 + k], refs[-1].at[k]) for k in range(n)]
        for c in copies:
            c.start()
        for c in copies:
            c.wait()

    return pl.pallas_call(
        body,
        out_shape=[shape(*a.shape, dtype=a.dtype) for a in arrays],
        in_specs=[hbm() for _ in arrays] + [pl.BlockSpec(memory_space=pl.ANY)],
        out_specs=[vmem() for _ in arrays],
        scratch_shapes=[pltpu.SemaphoreType.DMA((len(arrays),))],
        compiler_params=params(),
        cost_estimate=cost(0, 12 << 20),
    )(*outside(arrays), after)


def shifted(x):
    return pltpu.roll(x, ROWS, 1)


def expert_math(pieces, me, w_gate, w_up, w_down, experts, splits):
    blocks = sum(p.shape[0] for p in pieces)
    width, hid = w_gate.shape
    lanes = pieces[0].shape[2] - width
    m = blocks * ROWS
    count = len(pieces)

    def body(*refs):
        me_ref, wg_ref, wu_ref, wd_ref = refs[count : count + 4]
        outs = refs[count + 4 :]
        parts, (t_ref, do_ref, h_ref, dg_ref, du_ref) = outs[: len(splits)], outs[len(splits) :]
        x = jnp.concatenate([r[...] for r in refs[:count]], axis=0).astype(F32)
        x = x.reshape(blocks // 2, 2, 2 * ROWS, width + lanes)
        even, odd = x[:, 0], x[:, 1]
        low = lax.broadcasted_iota(jnp.int32, (1, 2 * ROWS, 1), 1) < ROWS
        wide = jnp.where(low, even, shifted(odd)).reshape(m, width + lanes)
        token = wide[:, :width].astype(BF16)
        t_ref[...] = token
        lane = lax.broadcasted_iota(jnp.int32, (1, lanes), 1)
        mine = me_ref[0]
        scale = jnp.where(lane == mine, 1.0 / 256.0, 0.0) + jnp.where(lane == mine + experts, 1.0 / 65536.0, 0.0)
        coef = jnp.sum(wide[:, width:] * scale, axis=1, keepdims=True)
        grads = jnp.where(low, shifted(even[..., :width]), odd[..., :width]).reshape(m, width)
        dout = (coef * grads).astype(BF16)
        do_ref[...] = dout
        gate = dot(token, wg_ref[...])
        upper = dot(token, wu_ref[...])
        dact = dot(dout, wd_ref[...], 1, 1)
        sig = jax.nn.sigmoid(gate)
        swish = gate * sig
        hidden = (swish * upper).astype(BF16)
        dgate = (dact * upper * sig * (1.0 + gate * (1.0 - sig))).astype(BF16)
        dupper = (dact * swish).astype(BF16)
        h_ref[...], dg_ref[...], du_ref[...] = hidden, dgate, dupper
        part = (coef * dot(hidden, wd_ref[...])).reshape(blocks // 2, 2 * ROWS, width)
        back = (dot(dgate, wg_ref[...], 1, 1) + dot(dupper, wu_ref[...], 1, 1)).reshape(blocks // 2, 2 * ROWS, width)
        first = jnp.where(low, part, shifted(back)).astype(BF16)
        second = jnp.where(low, shifted(part), back).astype(BF16)
        mixed = jnp.stack([first, second], axis=1).reshape(blocks, 2 * ROWS, width)
        at = 0
        for ref, n in zip(parts, splits):
            ref[...] = mixed[at : at + n]
            at += n

    outs = [shape(n, 2 * ROWS, width) for n in splits]
    outs += [shape(m, width), shape(m, width), shape(m, hid), shape(m, hid), shape(m, hid)]
    got = pl.pallas_call(
        body,
        out_shape=outs,
        in_specs=[vmem()] * count + [pl.BlockSpec(memory_space=pltpu.SMEM)] + [vmem()] * 3,
        out_specs=[vmem() for _ in outs],
        compiler_params=params(),
        cost_estimate=cost(12 * m * width * hid, 10 << 20),
    )(*pieces, me, w_gate, w_up, w_down)
    return list(got[: len(splits)]), got[len(splits) :]


def weight_grads(left, rights, steps):
    m, rows = left.shape
    cols = rights[0].shape[1]
    steps = steps if rows % (128 * steps) == 0 else 1
    tile = rows // steps

    def body(l_ref, *refs):
        for r_ref, o_ref in zip(refs[: len(rights)], refs[len(rights) :]):
            o_ref[...] = dot(l_ref[...], r_ref[...], 0, 0).astype(BF16)

    return pl.pallas_call(
        body,
        grid=(steps,),
        out_shape=[shape(rows, cols) for _ in rights],
        in_specs=[pl.BlockSpec((m, tile), lambda i: (0, i))] + [pl.BlockSpec((m, cols), lambda i: (0, 0)) for _ in rights],
        out_specs=[pl.BlockSpec((tile, cols), lambda i: (i, 0)) for _ in rights],
        compiler_params=params(),
        cost_estimate=cost(2 * m * rows * cols * len(rights), 2 * rows * cols * len(rights)),
    )(left, *rights)


def add(terms, splits, after=()):
    outs = [shape(n, *terms[0].shape[1:], dtype=BF16 if i else F32) for i, n in enumerate(splits)]

    def body(*refs):
        total = refs[0][...].astype(F32)
        for r in refs[1 : len(terms)]:
            total += r[...].astype(F32)
        at = 0
        for ref, n in zip(refs[len(terms) + len(after) :], splits):
            ref[...] = total[at : at + n].astype(ref.dtype)
            at += n

    return pl.pallas_call(
        body,
        out_shape=outs,
        in_specs=[vmem() for _ in terms] + [hbm() for _ in after],
        out_specs=[vmem() for _ in outs],
        compiler_params=params(),
        cost_estimate=cost(0, 64 << 10),
    )(*terms, *outside(after))


def add_pair(one, two):
    def body(a_ref, b_ref, o_ref):
        o_ref[...] = (a_ref[...].astype(F32) + b_ref[...].astype(F32)).astype(BF16)

    return pl.pallas_call(
        body,
        out_shape=shape(*one.shape),
        in_specs=[vmem(), vmem()],
        out_specs=vmem(),
        compiler_params=params(),
        cost_estimate=cost(0, 64 << 10),
    )(one, two)


def finish(terms, after=()):
    _, _, width = terms[0].shape

    def body(*refs):
        total = refs[0][...].astype(F32)
        for r in refs[1 : len(terms)]:
            total += r[...].astype(F32)
        out_ref, back_ref = refs[len(terms) + len(after) :]
        out_ref[...] = total[0, :ROWS].astype(BF16)
        back_ref[...] = total[0, ROWS:].astype(BF16)

    return pl.pallas_call(
        body,
        out_shape=[shape(ROWS, width)] * 2,
        in_specs=[vmem() for _ in terms] + [hbm() for _ in after],
        out_specs=[vmem(), vmem()],
        compiler_params=params(),
        cost_estimate=cost(0, 64 << 10),
    )(*terms, *outside(after))


def on_device(tokens, route_ids, route_weights, w_gate, w_up, w_down, grad_out):
    experts = w_gate.shape[0] * lax.axis_size("expert")
    core = lax.axis_size("dp")
    total = lax.axis_size("expert") * core
    plan = stages(total, core)
    me = lax.axis_index("expert").astype(jnp.int32).reshape(1)
    wg, wu, wd = w_gate[0], w_up[0], w_down[0]

    held = [pack(tokens, route_ids, route_weights, grad_out, experts)]
    for masks in plan:
        block = held[0] if len(held) == 1 else jnp.concatenate(held, axis=0)
        held = [block] + [exchange(block, mask, total, core) for mask in masks]
    wg, wu, wd = fetch((wg, wu, wd), held[1])
    pieces = held + [exchange(h, (core, core), total, core) for h in held]

    ways = len(held)
    size = total // 2 // ways
    if total <= CHUNK:
        parts, kept = expert_math(pieces, me, wg, wu, wd, experts, [size] * (2 * ways))
    else:
        whole = jnp.concatenate(pieces, axis=0)
        sums, saved = [], []
        for at in range(0, total, CHUNK):
            (got,), rest = expert_math([whole[at : at + CHUNK]], me, wg, wu, wd, experts, [CHUNK])
            sums.append(got)
            saved.append(rest)
        got = jnp.concatenate(sums, axis=0)
        parts = [got[at : at + size] for at in range(0, total, size)]
        kept = [jnp.concatenate(p, axis=0) for p in zip(*saved)]
    token, dout, hidden, dgate, dupper = kept

    gate_grad, up_grad = weight_grads(token, [dgate, dupper], 2)
    (down_grad,) = weight_grads(hidden, [dout], 2)

    keep, send = parts[:ways], parts[ways:]
    arrived = [exchange(p, (core, core), total, core) for p in send]
    terms = [keep[0], arrived[0]]
    for at, mask in enumerate(plan[-1]):
        terms.append(exchange(add_pair(keep[at + 1], arrived[at + 1]), mask, total, core))
    after = (gate_grad,)
    for masks in reversed(plan[:-1]):
        mine, *others = add(terms, [terms[0].shape[0] // (len(masks) + 1)] * (len(masks) + 1), after)
        terms = [mine] + [exchange(o, mask, total, core) for o, mask in zip(others, masks)]
        after = ()
    mixed, back = finish(terms, (down_grad,))
    return mixed, back, gate_grad[None], up_grad[None], down_grad[None]


def solution(mesh):
    rows = P(("groups", "expert", "dp"), None)
    in_specs = (rows, rows, rows, P("expert", None, "dp"), P("expert", None, "dp"), P("expert", "dp", None), rows)
    hidden = P(("groups", "expert"), None, "dp")
    out_specs = (rows, rows, hidden, hidden, P(("groups", "expert"), "dp", None))
    return jax.shard_map(on_device, mesh=mesh, in_specs=in_specs, out_specs=out_specs, check_vma=False)
```

time: 54.1 us -> 46.7 us (0.86)
  local copies, waits for them, and re-layouts: 4.38 us -> 0 us
  waiting for transfers between devices: 17.9 us -> 14.3 us
  starting transfers between devices: 18.2 us -> 18.9 us
    unnamed x10 -> x0, local copies, waits for them, and re-layouts: 4.38 us -> none
    ppermute x17 -> x20, waiting for transfers between devices: 17.9 us -> 14.3 us  [exchange(): lax.ppermute(x, AXES, [(i, i ^ masks[i // core % 2]) for i in range(total)])]
    ppermute x17 -> x20, starting transfers between devices: 18.2 us -> 18.9 us  [exchange(): lax.ppermute(x, AXES, [(i, i ^ masks[i // core % 2]) for i in range(total)])]
    pallas_call x7 -> x10, Pallas kernels: 12.5 us -> 12.4 us  [the longest x2 4.5 us: weight_grads(): pl.pallas_call(body, grid=(steps,), out_shape=[shape(rows, cols) for _ in...]
  transfers between devices with their start and end apart: 17 -> 20, of which waited for: 9 -> 9; matrix products, arithmetic and copies ran while one was open for 0% -> 0% of each run, Pallas kernels for 11% -> 16%
where the time goes in v2:
time: 46.7 us; the launch traced here: 46.3 us
  starting transfers between devices  18.9 us (40%)
  waiting for transfers between devices  14.3 us (31%)
  Pallas kernels  12.4 us (27%)
  between operations  0.72 us (2%)
    ppermute x20, starting transfers between devices, exchange(): lax.ppermute(x, AXES, [(i, i ^ masks[i // core % 2]) for i in range(total)])  18.9 us
    ppermute x20, waiting for transfers between devices, exchange(): lax.ppermute(x, AXES, [(i, i ^ masks[i // core % 2]) for i in range(total)])  14.3 us
    pallas_call x2, Pallas kernels, weight_grads(): pl.pallas_call(body, grid=(steps,), out_shape=[shape(rows, cols) for _ in...  4.5 us
    pallas_call x1, Pallas kernels, expert_math(): pl.pallas_call(body, out_shape=outs, in_specs=[vmem()] * count + [pl.Bloc...  3.28 us
    pallas_call x1, Pallas kernels, fetch(): pl.pallas_call(body, out_shape=[shape(*a.shape, dtype=a.dtype) for a in a...  2.88 us
  transfers between devices with their start and end apart: 20, of which 9 were waited for; matrix products, arithmetic and copies ran while one was open for 0% of the time, Pallas kernels for 16%

profile of v2, /device:TPU:0, one launch (start us, length us, event | category | flops | bytes accessed | tf_op | source)
XLA Modules:
  0.0 46.3 jit_solution(14255233873545702364)
XLA Ops:
  0.6 0.9 %shard_map.110 = bf16[1,8,2176]{2,1,0:T(8,128)(2,1)S(1)} custom-call(bf16[4,2048]{1,0:T(4,128)(2,1)} %t_in.1, s32[4,8]{1,0:T(4,128)} %i_in.1, s32[4,8]{1,0:T(4,128)} %w_in.1, bf16[4,2048]{1,0:T(4,128)(2,1)} %g_in.1), custom_call_target="tpu_custom_call" | custom-call | bytes 81920 | tf_op jit(solution)/shard_map/pallas_call | solution.py:86
  1.6 5.1 %collective-permute-start.2 = (bf16[1,8,2176]{2,1,0:T(8,128)(2,1)S(1)}, bf16[1,8,2176]{2,1,0:T(8,128)(2,1)S(1)}, u32[]{:S(2)}, u32[]{:S(2)}) collective-permute-start(bf16[1,8,2176]{2,1,0:T(8,128)(2,1)S(1)} %shard_map.110), channel_id=1, source_target_pairs={{0,24},{1,25},{2,26},{3,27},{4,28},{5,29},{6,30},{7,31},{8,16},{9,... | collective-permute-start | bytes 104456 | tf_op jit(solution)/shard_map/ppermute | solution.py:45
  6.7 0.0 collective-permute-start.1
  6.7 0.6 %collective-permute-start = (bf16[1,8,2176]{2,1,0:T(8,128)(2,1)S(1)}, bf16[1,8,2176]{2,1,0:T(8,128)(2,1)S(1)}, u32[]{:S(2)}, u32[]{:S(2)}) collective-permute-start(bf16[1,8,2176]{2,1,0:T(8,128)(2,1)S(1)} %shard_map.110), channel_id=1, source_target_pairs={{0,8},{1,9},{2,10},{3,11},{4,12},{5,13},{6,14},{7,15},{8,0},{9,1},... | collective-permute-start | bytes 104456 | tf_op jit(solution)/shard_map/ppermute | solution.py:45
  7.3 1.3 %collective-permute-done.2 = bf16[1,8,2176]{2,1,0:T(8,128)(2,1)S(1)} collective-permute-done((bf16[1,8,2176]{2,1,0:T(8,128)(2,1)S(1)}, bf16[1,8,2176]{2,1,0:T(8,128)(2,1)S(1)}, u32[]{:S(2)}, u32[]{:S(2)}) %collective-permute-start.2) | collective-permute-done | bytes 34848 | tf_op jit(solution)/shard_map/ppermute | solution.py:45
  8.6 2.9 %collective-permute-done.1 = bf16[1,8,2176]{2,1,0:T(8,128)(2,1)S(1)} collective-permute-done((bf16[1,8,2176]{2,1,0:T(8,128)(2,1)S(1)}, bf16[1,8,2176]{2,1,0:T(8,128)(2,1)S(1)}, u32[]{:S(2)}, u32[]{:S(2)}) %collective-permute-start.1) | collective-permute-done | bytes 34848 | tf_op jit(solution)/shard_map/ppermute | solution.py:45
  11.5 0.0 collective-permute-done
  11.5 2.5 %collective-permute-start.5 = (bf16[4,8,2176]{2,1,0:T(8,128)(2,1)S(1)}, bf16[4,8,2176]{2,1,0:T(8,128)(2,1)S(1)}, u32[]{:S(2)}, u32[]{:S(2)}) collective-permute-start(bf16[4,8,2176]{2,1,0:T(8,128)(2,1)S(1)} %pad_maximum_fusion.refs_0_), channel_id=1, source_target_pairs={{0,5},{1,4},{2,7},{3,6},{4,1},{5,0},{6,3},{7,2},{8,13},{9,12},{10,... | collective-permute-start | bytes 417800 | tf_op jit(solution)/shard_map/ppermute | solution.py:45
  14.1 0.5 %collective-permute-start.4 = (bf16[4,8,2176]{2,1,0:T(8,128)(2,1)S(1)}, bf16[4,8,2176]{2,1,0:T(8,128)(2,1)S(1)}, u32[]{:S(2)}, u32[]{:S(2)}) collective-permute-start(bf16[4,8,2176]{2,1,0:T(8,128)(2,1)S(1)} %pad_maximum_fusion.refs_0_), channel_id=1, source_target_pairs={{0,4},{1,5},{2,3},{3,2},{4,0},{5,1},{6,7},{7,6},{8,12},{9,13},{10,... | collective-permute-start | bytes 417800 | tf_op jit(solution)/shard_map/ppermute | solution.py:45
  14.6 0.5 %collective-permute-start.3 = (bf16[4,8,2176]{2,1,0:T(8,128)(2,1)S(1)}, bf16[4,8,2176]{2,1,0:T(8,128)(2,1)S(1)}, u32[]{:S(2)}, u32[]{:S(2)}) collective-permute-start(bf16[4,8,2176]{2,1,0:T(8,128)(2,1)S(1)} %pad_maximum_fusion.refs_0_), channel_id=1, source_target_pairs={{0,1},{1,0},{2,6},{3,7},{4,5},{5,4},{6,2},{7,3},{8,9},{9,8},{10,14... | collective-permute-start | bytes 417800 | tf_op jit(solution)/shard_map/ppermute | solution.py:45
  15.1 0.0 collective-permute-start.6
  15.1 3.0 %collective-permute-done.5.refs_3_ = bf16[4,8,2176]{2,1,0:T(8,128)(2,1)S(1)} collective-permute-done((bf16[4,8,2176]{2,1,0:T(8,128)(2,1)S(1)}, bf16[4,8,2176]{2,1,0:T(8,128)(2,1)S(1)}, u32[]{:S(2)}, u32[]{:S(2)}) %collective-permute-start.5) | collective-permute-done | bytes 139296 | tf_op jit(solution)/shard_map/ppermute | solution.py:45
  18.1 0.0 collective-permute-start.9
  18.1 1.4 %collective-permute-done.4.refs_2_ = bf16[4,8,2176]{2,1,0:T(8,128)(2,1)S(1)} collective-permute-done((bf16[4,8,2176]{2,1,0:T(8,128)(2,1)S(1)}, bf16[4,8,2176]{2,1,0:T(8,128)(2,1)S(1)}, u32[]{:S(2)}, u32[]{:S(2)}) %collective-permute-start.4) | collective-permute-done | bytes 139296 | tf_op jit(solution)/shard_map/ppermute | solution.py:45
  19.5 0.0 collective-permute-start.8
  19.5 0.1 collective-permute-done.3.refs_3_.refs_1_
  19.6 0.4 collective-permute-start.7
  20.0 2.9 %shard_map.111 = (bf16[2048,512]{1,0:T(8,128)(2,1)S(1)}, bf16[2048,512]{1,0:T(8,128)(2,1)S(1)}, bf16[512,2048]{1,0:T(8,128)(2,1)S(1)}) custom-call(bf16[2048,512]{1,0:T(8,128)(2,1)} %bitcast.8, bf16[2048,512]{1,0:T(8,128)(2,1)} %bitcast.9, bf16[512,2048]{1,0:T(8,128)(2,1)} %bitcast.10, bf16[4,8,2176]{2,1,0:T(8,128)(2,1)S(1)} %collective-permute-done.3.refs_3_.refs_1_), custom_call_target="tpu_custom_call" | custom-call | bytes 12582912 | tf_op jit(solution)/shard_map/pallas_call | solution.py:106
  22.9 0.0 collective-permute-done.6.refs_4_
  22.9 0.0 collective-permute-done.9.refs_7_
  22.9 0.0 collective-permute-done.8.refs_6_
  22.9 0.0 collective-permute-done.7.refs_5_
  23.0 3.3 %shard_map.112 = (bf16[4,8,2048]{2,1,0:T(8,128)(2,1)S(1)}, bf16[4,8,2048]{2,1,0:T(8,128)(2,1)S(1)}, bf16[4,8,2048]{2,1,0:T(8,128)(2,1)S(1)}, bf16[4,8,2048]{2,1,...) custom-call(bf16[4,8,2176]{2,1,0:T(8,128)(2,1)S(1)} %pad_maximum_fus, ...), custom_call_target="tpu_custom_call" | custom-call | flops 1610612736 | bytes 10485760 | tf_op jit(solution)/shard_map/pallas_call | solution.py:167
  26.2 0.2 collective-permute-start.11
  26.4 0.4 collective-permute-start.13
  26.8 0.1 collective-permute-start.15
  26.9 0.4 collective-permute-start.10
  27.3 0.3 collective-permute-done.11.b_ref
  27.7 1.5 %collective-permute-start.12 = (bf16[4,8,2048]{2,1,0:T(8,128)(2,1)S(1)}, bf16[4,8,2048]{2,1,0:T(8,128)(2,1)S(1)}, u32[]{:S(2)}, u32[]{:S(2)}) collective-permute-start(bf16[4,8,2048]{2,1,0:T(8,128)(2,1)S(1)} %shard_map.113), channel_id=1, source_target_pairs={{0,1},{1,0},{2,6},{3,7},{4,5},{5,4},{6,2},{7,3},{8,9},{9,8},{10,14... | collective-permute-start | bytes 393224 | tf_op jit(solution)/shard_map/ppermute | solution.py:45
  29.2 0.0 collective-permute-done.13.b_ref
  29.3 1.6 %collective-permute-start.14 = (bf16[4,8,2048]{2,1,0:T(8,128)(2,1)S(1)}, bf16[4,8,2048]{2,1,0:T(8,128)(2,1)S(1)}, u32[]{:S(2)}, u32[]{:S(2)}) collective-permute-start(bf16[4,8,2048]{2,1,0:T(8,128)(2,1)S(1)} %shard_map.114), channel_id=1, source_target_pairs={{0,4},{1,5},{2,3},{3,2},{4,0},{5,1},{6,7},{7,6},{8,12},{9,13},{10,... | collective-permute-start | bytes 393224 | tf_op jit(solution)/shard_map/ppermute | solution.py:45
  30.8 0.0 collective-permute-done.15.b_ref
  30.9 0.6 %collective-permute-start.16 = (bf16[4,8,2048]{2,1,0:T(8,128)(2,1)S(1)}, bf16[4,8,2048]{2,1,0:T(8,128)(2,1)S(1)}, u32[]{:S(2)}, u32[]{:S(2)}) collective-permute-start(bf16[4,8,2048]{2,1,0:T(8,128)(2,1)S(1)} %shard_map.115), channel_id=1, source_target_pairs={{0,5},{1,4},{2,7},{3,6},{4,1},{5,0},{6,3},{7,2},{8,13},{9,12},{10,... | collective-permute-start | bytes 393224 | tf_op jit(solution)/shard_map/ppermute | solution.py:45
  31.5 2.6 %shard_map.116 = (bf16[2048,512]{1,0:T(8,128)(2,1)}, bf16[2048,512]{1,0:T(8,128)(2,1)}) custom-call(bf16[128,2048]{1,0:T(8,128)(2,1)S(1)} %get-tuple-element.40.l_ref, bf16[128,512]{1,0:T(8,128)(2,1)S(1)} %get-tuple-element.41.refs_0_, bf16[128,512]{1,0:T(8,128)(2,1)S(1)} %get-tuple-element.42.refs_1_), custom_call_target="tpu_custom_call" | custom-call | flops 536870912 | bytes 4194304 | tf_op jit(solution)/shard_map/pallas_call | solution.py:188
  34.0 0.0 collective-permute-done.10.refs_1_
  34.0 0.0 collective-permute-done.12.refs_2_
  34.0 0.4 collective-permute-done.14.refs_3_
  34.4 3.0 %collective-permute-done.16.refs_4_ = bf16[4,8,2048]{2,1,0:T(8,128)(2,1)S(1)} collective-permute-done((bf16[4,8,2048]{2,1,0:T(8,128)(2,1)S(1)}, bf16[4,8,2048]{2,1,0:T(8,128)(2,1)S(1)}, u32[]{:S(2)}, u32[]{:S(2)}) %collective-permute-start.16) | collective-permute-done | bytes 131104 | tf_op jit(solution)/shard_map/ppermute | solution.py:45
  37.4 0.1 shard_map.117
  37.5 0.2 collective-permute-start.17
  37.7 2.3 %collective-permute-start.18 = (bf16[1,8,2048]{2,1,0:T(8,128)(2,1)S(1)}, bf16[1,8,2048]{2,1,0:T(8,128)(2,1)S(1)}, u32[]{:S(2)}, u32[]{:S(2)}) collective-permute-start(bf16[1,8,2048]{2,1,0:T(8,128)(2,1)S(1)} %get-tuple-element.46), channel_id=1, source_target_pairs={{0,16},{1,17},{2,18},{3,19},{4,20},{5,21},{6,22},{7,23},{8,24},{9,... | collective-permute-start | bytes 98312 | tf_op jit(solution)/shard_map/ppermute | solution.py:45
  40.0 2.0 %collective-permute-start.19 = (bf16[1,8,2048]{2,1,0:T(8,128)(2,1)S(1)}, bf16[1,8,2048]{2,1,0:T(8,128)(2,1)S(1)}, u32[]{:S(2)}, u32[]{:S(2)}) collective-permute-start(bf16[1,8,2048]{2,1,0:T(8,128)(2,1)S(1)} %get-tuple-element.47), channel_id=1, source_target_pairs={{0,24},{1,25},{2,26},{3,27},{4,28},{5,29},{6,30},{7,31},{8,16},{9,... | collective-permute-start | bytes 98312 | tf_op jit(solution)/shard_map/ppermute | solution.py:45
  41.9 1.9 %shard_map.118.refs_4_ = bf16[512,2048]{1,0:T(8,128)(2,1)} custom-call(bf16[128,512]{1,0:T(8,128)(2,1)S(1)} %get-tuple-element.48.l_ref, bf16[128,2048]{1,0:T(8,128)(2,1)S(1)} %get-tuple-element.49.refs_0_), custom_call_target="tpu_custom_call" | custom-call | flops 268435456 | bytes 2097152 | tf_op jit(solution)/shard_map/pallas_call | solution.py:188
  43.9 0.0 collective-permute-done.17.refs_1_
  43.9 0.0 collective-permute-done.18.refs_2_
  43.9 1.8 %collective-permute-done.19.refs_3_ = bf16[1,8,2048]{2,1,0:T(8,128)(2,1)S(1)} collective-permute-done((bf16[1,8,2048]{2,1,0:T(8,128)(2,1)S(1)}, bf16[1,8,2048]{2,1,0:T(8,128)(2,1)S(1)}, u32[]{:S(2)}, u32[]{:S(2)}) %collective-permute-start.19) | collective-permute-done | bytes 32800 | tf_op jit(solution)/shard_map/ppermute | solution.py:45
  45.7 0.6 %shard_map.119 = (bf16[4,2048]{1,0:T(4,128)(2,1)}, bf16[4,2048]{1,0:T(4,128)(2,1)}) custom-call(f32[1,8,2048]{2,1,0:T(8,128)S(1)} %get-tuple-element.44.refs_0_, bf16[1,8,2048]{2,1,0:T(8,128)(2,1)S(1)} %collective-permute-done.17.refs_1_, bf16[1,8,2048]{2,1,0:T(8,128)(2,1)S(1)} %collective-permute-done.18.refs_2_, ...), custom_call_target="tpu_custom_call" | custom-call | bytes 65536 | tf_op jit(solution)/shard_map/pallas_call | solution.py:246
  (4 shorter events, 0.1 us)
Async XLA Ops:
  1.6 7.0 %collective-permute-start.2 = (bf16[1,8,2176]{2,1,0:T(8,128)(2,1)S(1)}, bf16[1,8,2176]{2,1,0:T(8,128)(2,1)S(1)}, u32[]{:S(2)}, u32[]{:S(2)}) collective-permute-start(bf16[1,8,2176]{2,1,0:T(8,128)(2,1)S(1)} %shard_map.110), channel_id=1, source_target_pairs={{0,24},{1,25},{2,26},{3,27},{4,28},{5,29},{6,30},{7,31},{8,16},{9,... | collective-permute-start | bytes 104456 | tf_op jit(solution)/shard_map/ppermute | solution.py:45
  6.7 4.8 %collective-permute-start.1 = (bf16[1,8,2176]{2,1,0:T(8,128)(2,1)S(1)}, bf16[1,8,2176]{2,1,0:T(8,128)(2,1)S(1)}, u32[]{:S(2)}, u32[]{:S(2)}) collective-permute-start(bf16[1,8,2176]{2,1,0:T(8,128)(2,1)S(1)} %shard_map.110), channel_id=1, source_target_pairs={{0,16},{1,17},{2,18},{3,19},{4,20},{5,21},{6,22},{7,23},{8,24},{9,... | collective-permute-start | bytes 104456 | tf_op jit(solution)/shard_map/ppermute | solution.py:45
  6.7 4.8 %collective-permute-start = (bf16[1,8,2176]{2,1,0:T(8,128)(2,1)S(1)}, bf16[1,8,2176]{2,1,0:T(8,128)(2,1)S(1)}, u32[]{:S(2)}, u32[]{:S(2)}) collective-permute-start(bf16[1,8,2176]{2,1,0:T(8,128)(2,1)S(1)} %shard_map.110), channel_id=1, source_target_pairs={{0,8},{1,9},{2,10},{3,11},{4,12},{5,13},{6,14},{7,15},{8,0},{9,1},... | collective-permute-start | bytes 104456 | tf_op jit(solution)/shard_map/ppermute | solution.py:45
  11.5 6.5 %collective-permute-start.5 = (bf16[4,8,2176]{2,1,0:T(8,128)(2,1)S(1)}, bf16[4,8,2176]{2,1,0:T(8,128)(2,1)S(1)}, u32[]{:S(2)}, u32[]{:S(2)}) collective-permute-start(bf16[4,8,2176]{2,1,0:T(8,128)(2,1)S(1)} %pad_maximum_fusion.refs_0_), channel_id=1, source_target_pairs={{0,5},{1,4},{2,7},{3,6},{4,1},{5,0},{6,3},{7,2},{8,13},{9,12},{10,... | collective-permute-start | bytes 417800 | tf_op jit(solution)/shard_map/ppermute | solution.py:45
  14.1 5.5 %collective-permute-start.4 = (bf16[4,8,2176]{2,1,0:T(8,128)(2,1)S(1)}, bf16[4,8,2176]{2,1,0:T(8,128)(2,1)S(1)}, u32[]{:S(2)}, u32[]{:S(2)}) collective-permute-start(bf16[4,8,2176]{2,1,0:T(8,128)(2,1)S(1)} %pad_maximum_fusion.refs_0_), channel_id=1, source_target_pairs={{0,4},{1,5},{2,3},{3,2},{4,0},{5,1},{6,7},{7,6},{8,12},{9,13},{10,... | collective-permute-start | bytes 417800 | tf_op jit(solution)/shard_map/ppermute | solution.py:45
  14.6 5.1 %collective-permute-start.3 = (bf16[4,8,2176]{2,1,0:T(8,128)(2,1)S(1)}, bf16[4,8,2176]{2,1,0:T(8,128)(2,1)S(1)}, u32[]{:S(2)}, u32[]{:S(2)}) collective-permute-start(bf16[4,8,2176]{2,1,0:T(8,128)(2,1)S(1)} %pad_maximum_fusion.refs_0_), channel_id=1, source_target_pairs={{0,1},{1,0},{2,6},{3,7},{4,5},{5,4},{6,2},{7,3},{8,9},{9,8},{10,14... | collective-permute-start | bytes 417800 | tf_op jit(solution)/shard_map/ppermute | solution.py:45
  15.1 7.8 %collective-permute-start.6 = (bf16[4,8,2176]{2,1,0:T(8,128)(2,1)S(1)}, bf16[4,8,2176]{2,1,0:T(8,128)(2,1)S(1)}, u32[]{:S(2)}, u32[]{:S(2)}) collective-permute-start(bf16[4,8,2176]{2,1,0:T(8,128)(2,1)S(1)} %pad_maximum_fusion.refs_0_), channel_id=1, source_target_pairs={{0,2},{1,3},{2,0},{3,1},{4,6},{5,7},{6,4},{7,5},{8,10},{9,11},{10,... | collective-permute-start | bytes 417800 | tf_op jit(solution)/shard_map/ppermute | solution.py:45
  18.1 4.9 %collective-permute-start.9 = (bf16[4,8,2176]{2,1,0:T(8,128)(2,1)S(1)}, bf16[4,8,2176]{2,1,0:T(8,128)(2,1)S(1)}, u32[]{:S(2)}, u32[]{:S(2)}) collective-permute-start(bf16[4,8,2176]{2,1,0:T(8,128)(2,1)S(1)} %collective-permute-done.5.refs_3_), channel_id=1, source_target_pairs={{0,2},{1,3},{2,0},{3,1},{4,6},{5,7},{6,4},{7,5},{8,10},{9,11},{10,... | collective-permute-start | bytes 417800 | tf_op jit(solution)/shard_map/ppermute | solution.py:45
  19.5 3.4 %collective-permute-start.8 = (bf16[4,8,2176]{2,1,0:T(8,128)(2,1)S(1)}, bf16[4,8,2176]{2,1,0:T(8,128)(2,1)S(1)}, u32[]{:S(2)}, u32[]{:S(2)}) collective-permute-start(bf16[4,8,2176]{2,1,0:T(8,128)(2,1)S(1)} %collective-permute-done.4.refs_2_), channel_id=1, source_target_pairs={{0,2},{1,3},{2,0},{3,1},{4,6},{5,7},{6,4},{7,5},{8,10},{9,11},{10,... | collective-permute-start | bytes 417800 | tf_op jit(solution)/shard_map/ppermute | solution.py:45
  19.6 3.3 %collective-permute-start.7 = (bf16[4,8,2176]{2,1,0:T(8,128)(2,1)S(1)}, bf16[4,8,2176]{2,1,0:T(8,128)(2,1)S(1)}, u32[]{:S(2)}, u32[]{:S(2)}) collective-permute-start(bf16[4,8,2176]{2,1,0:T(8,128)(2,1)S(1)} %collective-permute-done.3.refs_3_.refs_1_), channel_id=1, source_target_pairs={{0,2},{1,3},{2,0},{3,1},{4,6},{5,7},{6,4},{7,5},{8,10},{9,11},{10,... | collective-permute-start | bytes 417800 | tf_op jit(solution)/shard_map/ppermute | solution.py:45
  26.2 1.4 %collective-permute-start.11 = (bf16[4,8,2048]{2,1,0:T(8,128)(2,1)S(1)}, bf16[4,8,2048]{2,1,0:T(8,128)(2,1)S(1)}, u32[]{:S(2)}, u32[]{:S(2)}) collective-permute-start(bf16[4,8,2048]{2,1,0:T(8,128)(2,1)S(1)} %get-tuple-element.35), channel_id=1, source_target_pairs={{0,2},{1,3},{2,0},{3,1},{4,6},{5,7},{6,4},{7,5},{8,10},{9,11},{10,... | collective-permute-start | bytes 393224 | tf_op jit(solution)/shard_map/ppermute | solution.py:45
  26.4 2.8 %collective-permute-start.13 = (bf16[4,8,2048]{2,1,0:T(8,128)(2,1)S(1)}, bf16[4,8,2048]{2,1,0:T(8,128)(2,1)S(1)}, u32[]{:S(2)}, u32[]{:S(2)}) collective-permute-start(bf16[4,8,2048]{2,1,0:T(8,128)(2,1)S(1)} %get-tuple-element.37), channel_id=1, source_target_pairs={{0,2},{1,3},{2,0},{3,1},{4,6},{5,7},{6,4},{7,5},{8,10},{9,11},{10,... | collective-permute-start | bytes 393224 | tf_op jit(solution)/shard_map/ppermute | solution.py:45
  26.8 4.0 %collective-permute-start.15 = (bf16[4,8,2048]{2,1,0:T(8,128)(2,1)S(1)}, bf16[4,8,2048]{2,1,0:T(8,128)(2,1)S(1)}, u32[]{:S(2)}, u32[]{:S(2)}) collective-permute-start(bf16[4,8,2048]{2,1,0:T(8,128)(2,1)S(1)} %get-tuple-element.39), channel_id=1, source_target_pairs={{0,2},{1,3},{2,0},{3,1},{4,6},{5,7},{6,4},{7,5},{8,10},{9,11},{10,... | collective-permute-start | bytes 393224 | tf_op jit(solution)/shard_map/ppermute | solution.py:45
  26.9 7.1 %collective-permute-start.10 = (bf16[4,8,2048]{2,1,0:T(8,128)(2,1)S(1)}, bf16[4,8,2048]{2,1,0:T(8,128)(2,1)S(1)}, u32[]{:S(2)}, u32[]{:S(2)}) collective-permute-start(bf16[4,8,2048]{2,1,0:T(8,128)(2,1)S(1)} %get-tuple-element.33), channel_id=1, source_target_pairs={{0,2},{1,3},{2,0},{3,1},{4,6},{5,7},{6,4},{7,5},{8,10},{9,11},{10,... | collective-permute-start | bytes 393224 | tf_op jit(solution)/shard_map/ppermute | solution.py:45
  27.7 6.4 %collective-permute-start.12 = (bf16[4,8,2048]{2,1,0:T(8,128)(2,1)S(1)}, bf16[4,8,2048]{2,1,0:T(8,128)(2,1)S(1)}, u32[]{:S(2)}, u32[]{:S(2)}) collective-permute-start(bf16[4,8,2048]{2,1,0:T(8,128)(2,1)S(1)} %shard_map.113), channel_id=1, source_target_pairs={{0,1},{1,0},{2,6},{3,7},{4,5},{5,4},{6,2},{7,3},{8,9},{9,8},{10,14... | collective-permute-start | bytes 393224 | tf_op jit(solution)/shard_map/ppermute | solution.py:45
  29.3 5.1 %collective-permute-start.14 = (bf16[4,8,2048]{2,1,0:T(8,128)(2,1)S(1)}, bf16[4,8,2048]{2,1,0:T(8,128)(2,1)S(1)}, u32[]{:S(2)}, u32[]{:S(2)}) collective-permute-start(bf16[4,8,2048]{2,1,0:T(8,128)(2,1)S(1)} %shard_map.114), channel_id=1, source_target_pairs={{0,4},{1,5},{2,3},{3,2},{4,0},{5,1},{6,7},{7,6},{8,12},{9,13},{10,... | collective-permute-start | bytes 393224 | tf_op jit(solution)/shard_map/ppermute | solution.py:45
  30.9 6.5 %collective-permute-start.16 = (bf16[4,8,2048]{2,1,0:T(8,128)(2,1)S(1)}, bf16[4,8,2048]{2,1,0:T(8,128)(2,1)S(1)}, u32[]{:S(2)}, u32[]{:S(2)}) collective-permute-start(bf16[4,8,2048]{2,1,0:T(8,128)(2,1)S(1)} %shard_map.115), channel_id=1, source_target_pairs={{0,5},{1,4},{2,7},{3,6},{4,1},{5,0},{6,3},{7,2},{8,13},{9,12},{10,... | collective-permute-start | bytes 393224 | tf_op jit(solution)/shard_map/ppermute | solution.py:45
  37.5 6.4 %collective-permute-start.17 = (bf16[1,8,2048]{2,1,0:T(8,128)(2,1)S(1)}, bf16[1,8,2048]{2,1,0:T(8,128)(2,1)S(1)}, u32[]{:S(2)}, u32[]{:S(2)}) collective-permute-start(bf16[1,8,2048]{2,1,0:T(8,128)(2,1)S(1)} %get-tuple-element.45), channel_id=1, source_target_pairs={{0,8},{1,9},{2,10},{3,11},{4,12},{5,13},{6,14},{7,15},{8,0},{9,1},... | collective-permute-start | bytes 98312 | tf_op jit(solution)/shard_map/ppermute | solution.py:45
  37.7 6.2 %collective-permute-start.18 = (bf16[1,8,2048]{2,1,0:T(8,128)(2,1)S(1)}, bf16[1,8,2048]{2,1,0:T(8,128)(2,1)S(1)}, u32[]{:S(2)}, u32[]{:S(2)}) collective-permute-start(bf16[1,8,2048]{2,1,0:T(8,128)(2,1)S(1)} %get-tuple-element.46), channel_id=1, source_target_pairs={{0,16},{1,17},{2,18},{3,19},{4,20},{5,21},{6,22},{7,23},{8,24},{9,... | collective-permute-start | bytes 98312 | tf_op jit(solution)/shard_map/ppermute | solution.py:45
  40.0 5.7 %collective-permute-start.19 = (bf16[1,8,2048]{2,1,0:T(8,128)(2,1)S(1)}, bf16[1,8,2048]{2,1,0:T(8,128)(2,1)S(1)}, u32[]{:S(2)}, u32[]{:S(2)}) collective-permute-start(bf16[1,8,2048]{2,1,0:T(8,128)(2,1)S(1)} %get-tuple-element.47), channel_id=1, source_target_pairs={{0,24},{1,25},{2,26},{3,27},{4,28},{5,29},{6,30},{7,31},{8,16},{9,... | collective-permute-start | bytes 98312 | tf_op jit(solution)/shard_map/ppermute | solution.py:45

commit v3 on v2

--- a/solution.py
+++ b/solution.py
@@ -6,8 +6,9 @@
 from jax.sharding import PartitionSpec as P
 
 AXES = ("expert", "dp")
-CHUNK = 32
 ROWS = 4
+GROUP = 4
+CHUNK = 8
 VMEM_LIMIT = 16 * 1024 * 1024
 F32 = jnp.float32
 BF16 = jnp.bfloat16
@@ -114,34 +115,49 @@
     )(*outside(arrays), after)
 
 
-def shifted(x):
-    return pltpu.roll(x, ROWS, 1)
+def regroup(blocks):
+    _, rows, width = blocks[0].shape
+
+    def body(*refs):
+        x = [r[0].astype(F32) for r in refs[:-1]]
+        low = lax.broadcasted_iota(jnp.int32, (rows, 1), 0) < ROWS
+        pairs = list(zip(x[::2], x[1::2]))
+        token = [jnp.where(low, a, pltpu.roll(b, ROWS, 0)) for a, b in pairs]
+        grads = [jnp.where(low, pltpu.roll(a, ROWS, 0), b) for a, b in pairs]
+        refs[-1][0] = jnp.concatenate(token + grads, axis=0).astype(BF16)
+
+    return pl.pallas_call(
+        body,
+        out_shape=shape(1, rows * len(blocks), width),
+        in_specs=[vmem() for _ in blocks],
+        out_specs=vmem(),
+        compiler_params=params(),
+        cost_estimate=cost(0, 64 << 10),
+    )(*blocks)
 
 
 def expert_math(pieces, me, w_gate, w_up, w_down, experts, splits):
     blocks = sum(p.shape[0] for p in pieces)
     width, hid = w_gate.shape
-    lanes = pieces[0].shape[2] - width
-    m = blocks * ROWS
+    _, rows, full = pieces[0].shape
+    lanes = full - width
+    half = rows // 2
+    m = blocks * half
     count = len(pieces)
 
     def body(*refs):
         me_ref, wg_ref, wu_ref, wd_ref = refs[count : count + 4]
         outs = refs[count + 4 :]
         parts, (t_ref, do_ref, h_ref, dg_ref, du_ref) = outs[: len(splits)], outs[len(splits) :]
-        x = jnp.concatenate([r[...] for r in refs[:count]], axis=0).astype(F32)
-        x = x.reshape(blocks // 2, 2, 2 * ROWS, width + lanes)
-        even, odd = x[:, 0], x[:, 1]
-        low = lax.broadcasted_iota(jnp.int32, (1, 2 * ROWS, 1), 1) < ROWS
-        wide = jnp.where(low, even, shifted(odd)).reshape(m, width + lanes)
-        token = wide[:, :width].astype(BF16)
+        x = jnp.concatenate([r[...] for r in refs[:count]], axis=0)
+        token = x[:, :half, :width].reshape(m, width)
         t_ref[...] = token
+        side = x[:, :half, width:].reshape(m, lanes).astype(F32)
         lane = lax.broadcasted_iota(jnp.int32, (1, lanes), 1)
         mine = me_ref[0]
         scale = jnp.where(lane == mine, 1.0 / 256.0, 0.0) + jnp.where(lane == mine + experts, 1.0 / 65536.0, 0.0)
-        coef = jnp.sum(wide[:, width:] * scale, axis=1, keepdims=True)
-        grads = jnp.where(low, shifted(even[..., :width]), odd[..., :width]).reshape(m, width)
-        dout = (coef * grads).astype(BF16)
+        coef = jnp.sum(side * scale, axis=1, keepdims=True)
+        dout = (coef * x[:, half:, :width].reshape(m, width).astype(F32)).astype(BF16)
         do_ref[...] = dout
         gate = dot(token, wg_ref[...])
         upper = dot(token, wu_ref[...])
@@ -152,17 +168,16 @@
         dgate = (dact * upper * sig * (1.0 + gate * (1.0 - sig))).astype(BF16)
         dupper = (dact * swish).astype(BF16)
         h_ref[...], dg_ref[...], du_ref[...] = hidden, dgate, dupper
-        part = (coef * dot(hidden, wd_ref[...])).reshape(blocks // 2, 2 * ROWS, width)
-        back = (dot(dgate, wg_ref[...], 1, 1) + dot(dupper, wu_ref[...], 1, 1)).reshape(blocks // 2, 2 * ROWS, width)
-        first = jnp.where(low, part, shifted(back)).astype(BF16)
-        second = jnp.where(low, shifted(part), back).astype(BF16)
-        mixed = jnp.stack([first, second], axis=1).reshape(blocks, 2 * ROWS, width)
+        part = (coef * dot(hidden, wd_ref[...])).astype(BF16).reshape(blocks, half, width)
+        back = dot(dgate, wg_ref[...], 1, 1) + dot(dupper, wu_ref[...], 1, 1)
+        back = back.astype(BF16).reshape(blocks, half, width)
         at = 0
         for ref, n in zip(parts, splits):
-            ref[...] = mixed[at : at + n]
+            ref[:, :half] = part[at : at + n]
+            ref[:, half:] = back[at : at + n]
             at += n
 
-    outs = [shape(n, 2 * ROWS, width) for n in splits]
+    outs = [shape(n, rows, width) for n in splits]
     outs += [shape(m, width), shape(m, width), shape(m, hid), shape(m, hid), shape(m, hid)]
     got = pl.pallas_call(
         body,
@@ -196,17 +211,41 @@
     )(left, *rights)
 
 
-def add(terms, splits, after=()):
+def add(terms, splits):
     outs = [shape(n, *terms[0].shape[1:], dtype=BF16 if i else F32) for i, n in enumerate(splits)]
 
     def body(*refs):
-        total = refs[0][...].astype(F32)
-        for r in refs[1 : len(terms)]:
-            total += r[...].astype(F32)
+        total = sum(r[...].astype(F32) for r in refs[: len(terms)])
         at = 0
-        for ref, n in zip(refs[len(terms) + len(after) :], splits):
+        for ref, n in zip(refs[len(terms) :], splits):
             ref[...] = total[at : at + n].astype(ref.dtype)
             at += n
+
+    return pl.pallas_call(
+        body,
+        out_shape=outs,
+        in_specs=[vmem() for _ in terms],
+        out_specs=[vmem() for _ in outs],
+        compiler_params=params(),
+        cost_estimate=cost(0, 64 << 10),
+    )(*terms)
+
+
+def add_ungroup(terms, after):
+    _, rows, width = terms[0].shape
+    outs = [shape(1, 2 * ROWS, width, dtype=BF16 if i else F32) for i in range(GROUP)]
+
+    def body(*refs):
+        total = sum(r[...].astype(F32) for r in refs[: len(terms)])[0]
+        low = lax.broadcasted_iota(jnp.int32, (2 * ROWS, 1), 0) < ROWS
+        for i, ref in enumerate(refs[-GROUP:]):
+            at = i // 2 * 2 * ROWS
+            out, back = total[at : at + 2 * ROWS], total[rows // 2 + at : rows // 2 + at + 2 * ROWS]
+            if i % 2:
+                block = jnp.where(low, pltpu.roll(out, ROWS, 0), back)
+            else:
+                block = jnp.where(low, out, pltpu.roll(back, ROWS, 0))
+            ref[0] = block.astype(ref.dtype)
 
     return pl.pallas_call(
         body,
@@ -261,26 +300,29 @@
     me = lax.axis_index("expert").astype(jnp.int32).reshape(1)
     wg, wu, wd = w_gate[0], w_up[0], w_down[0]
 
-    held = [pack(tokens, route_ids, route_weights, grad_out, experts)]
-    for masks in plan:
-        block = held[0] if len(held) == 1 else jnp.concatenate(held, axis=0)
+    block = pack(tokens, route_ids, route_weights, grad_out, experts)
+    block = regroup([block] + [exchange(block, mask, total, core) for mask in plan[0]])
+    for masks in plan[1:]:
         held = [block] + [exchange(block, mask, total, core) for mask in masks]
-    wg, wu, wd = fetch((wg, wu, wd), held[1])
-    pieces = held + [exchange(h, (core, core), total, core) for h in held]
+        block = jnp.concatenate(held, axis=0)
+    wg, wu, wd = fetch((wg, wu, wd), held[0])
+    own, wg, wu, wd = lax.optimization_barrier((held[0], wg, wu, wd))
+    pieces = held + [exchange(h, (core, core), total, core) for h in [own] + held[1:]]
 
     ways = len(held)
-    size = total // 2 // ways
-    if total <= CHUNK:
+    groups = total // GROUP
+    size = groups // 2 // ways
+    if groups <= CHUNK:
         parts, kept = expert_math(pieces, me, wg, wu, wd, experts, [size] * (2 * ways))
     else:
         whole = jnp.concatenate(pieces, axis=0)
         sums, saved = [], []
-        for at in range(0, total, CHUNK):
+        for at in range(0, groups, CHUNK):
             (got,), rest = expert_math([whole[at : at + CHUNK]], me, wg, wu, wd, experts, [CHUNK])
             sums.append(got)
             saved.append(rest)
         got = jnp.concatenate(sums, axis=0)
-        parts = [got[at : at + size] for at in range(0, total, size)]
+        parts = [got[at : at + size] for at in range(0, groups, size)]
         kept = [jnp.concatenate(p, axis=0) for p in zip(*saved)]
     token, dout, hidden, dgate, dupper = kept
 
@@ -292,11 +334,12 @@
     terms = [keep[0], arrived[0]]
     for at, mask in enumerate(plan[-1]):
         terms.append(exchange(add_pair(keep[at + 1], arrived[at + 1]), mask, total, core))
-    after = (gate_grad,)
-    for masks in reversed(plan[:-1]):
-        mine, *others = add(terms, [terms[0].shape[0] // (len(masks) + 1)] * (len(masks) + 1), after)
+    for masks in reversed(plan[1:-1]):
+        ways = len(masks) + 1
+        mine, *others = add(terms, [terms[0].shape[0] // ways] * ways)
         terms = [mine] + [exchange(o, mask, total, core) for o, mask in zip(others, masks)]
-        after = ()
+    mine, *others = add_ungroup(terms, (gate_grad,))
+    terms = [mine] + [exchange(o, mask, total, core) for o, mask in zip(others, plan[0])]
     mixed, back = finish(terms, (down_grad,))
     return mixed, back, gate_grad[None], up_grad[None], down_grad[None]
 

time: 46.7 us -> 49.4 us (1.058)
  local copies, waits for them, and re-layouts: 0 us -> 5.81 us
  waiting for transfers between devices: 14.3 us -> 10.6 us
  starting transfers between devices: 18.9 us -> 19.5 us
    unnamed x0 -> x8, local copies, waits for them, and re-layouts: none -> 5.81 us
    ppermute x20, waiting for transfers between devices: 14.3 us -> 10.6 us  [exchange(): lax.ppermute(x, AXES, [(i, i ^ masks[i // core % 2]) for i in range(total)])]
    ppermute x20, starting transfers between devices: 18.9 us -> 19.5 us  [exchange(): lax.ppermute(x, AXES, [(i, i ^ masks[i // core % 2]) for i in range(total)])]
  transfers between devices with their start and end apart: 20 -> 20, of which waited for: 9 -> 10; matrix products, arithmetic and copies ran while one was open for 0% -> 0% of each run, Pallas kernels for 16% -> 15%
where the time goes in v3:
time: 49.4 us; the launch traced here: 49 us
  starting transfers between devices  19.5 us (39%)
  Pallas kernels  12.3 us (25%)
  waiting for transfers between devices  10.6 us (21%)
  local copies, waits for them, and re-layouts  5.81 us (12%)
  between operations  0.71 us (1%)
    ppermute x20, starting transfers between devices, exchange(): lax.ppermute(x, AXES, [(i, i ^ masks[i // core % 2]) for i in range(total)])  19.5 us
    ppermute x20, waiting for transfers between devices, exchange(): lax.ppermute(x, AXES, [(i, i ^ masks[i // core % 2]) for i in range(total)])  10.6 us
    unnamed x8, local copies, waits for them, and re-layouts  5.81 us
    pallas_call x2, Pallas kernels, weight_grads(): pl.pallas_call(body, grid=(steps,), out_shape=[shape(rows, cols) for _ in...  4.51 us
    pallas_call x1, Pallas kernels, expert_math(): pl.pallas_call(body, out_shape=outs, in_specs=[vmem()] * count + [pl.Bloc...  3.16 us
    pallas_call x1, Pallas kernels, fetch(): pl.pallas_call(body, out_shape=[shape(*a.shape, dtype=a.dtype) for a in a...  2.88 us
  transfers between devices with their start and end apart: 20, of which 10 were waited for; matrix products, arithmetic and copies ran while one was open for 0% of the time, Pallas kernels for 15%

profile of v3, /device:TPU:0, one launch (start us, length us, event | category | flops | bytes accessed | tf_op | source)
XLA Modules:
  0.0 49.0 jit_solution(16242350491240522477)
XLA Ops:
  0.6 0.9 %shard_map.110.refs_0_ = bf16[1,8,2176]{2,1,0:T(8,128)(2,1)S(1)} custom-call(bf16[4,2048]{1,0:T(4,128)(2,1)} %t_in.1, s32[4,8]{1,0:T(4,128)} %i_in.1, s32[4,8]{1,0:T(4,128)} %w_in.1, bf16[4,2048]{1,0:T(4,128)(2,1)} %g_in.1), custom_call_target="tpu_custom_call" | custom-call | bytes 81920 | tf_op jit(solution)/shard_map/pallas_call | solution.py:87
  1.6 5.1 %collective-permute-start.2 = (bf16[1,8,2176]{2,1,0:T(8,128)(2,1)S(1)}, bf16[1,8,2176]{2,1,0:T(8,128)(2,1)S(1)}, u32[]{:S(2)}, u32[]{:S(2)}) collective-permute-start(bf16[1,8,2176]{2,1,0:T(8,128)(2,1)S(1)} %shard_map.110.refs_0_), channel_id=1, source_target_pairs={{0,24},{1,25},{2,26},{3,27},{4,28},{5,29},{6,30},{7,31},{8,16},{9,... | collective-permute-start | bytes 104456 | tf_op jit(solution)/shard_map/ppermute | solution.py:46
  6.7 0.0 collective-permute-start.1
  6.7 0.6 %collective-permute-start = (bf16[1,8,2176]{2,1,0:T(8,128)(2,1)S(1)}, bf16[1,8,2176]{2,1,0:T(8,128)(2,1)S(1)}, u32[]{:S(2)}, u32[]{:S(2)}) collective-permute-start(bf16[1,8,2176]{2,1,0:T(8,128)(2,1)S(1)} %shard_map.110.refs_0_), channel_id=1, source_target_pairs={{0,8},{1,9},{2,10},{3,11},{4,12},{5,13},{6,14},{7,15},{8,0},{9,1},... | collective-permute-start | bytes 104456 | tf_op jit(solution)/shard_map/ppermute | solution.py:46
  7.3 1.3 %collective-permute-done.2.refs_3_ = bf16[1,8,2176]{2,1,0:T(8,128)(2,1)S(1)} collective-permute-done((bf16[1,8,2176]{2,1,0:T(8,128)(2,1)S(1)}, bf16[1,8,2176]{2,1,0:T(8,128)(2,1)S(1)}, u32[]{:S(2)}, u32[]{:S(2)}) %collective-permute-start.2) | collective-permute-done | bytes 34848 | tf_op jit(solution)/shard_map/ppermute | solution.py:46
  8.6 2.9 %collective-permute-done.1.refs_2_ = bf16[1,8,2176]{2,1,0:T(8,128)(2,1)S(1)} collective-permute-done((bf16[1,8,2176]{2,1,0:T(8,128)(2,1)S(1)}, bf16[1,8,2176]{2,1,0:T(8,128)(2,1)S(1)}, u32[]{:S(2)}, u32[]{:S(2)}) %collective-permute-start.1) | collective-permute-done | bytes 34848 | tf_op jit(solution)/shard_map/ppermute | solution.py:46
  11.5 0.0 collective-permute-done.refs_1_
  11.6 2.5 %collective-permute-start.5 = (bf16[1,32,2176]{2,1,0:T(8,128)(2,1)S(1)}, bf16[1,32,2176]{2,1,0:T(8,128)(2,1)S(1)}, u32[]{:S(2)}, u32[]{:S(2)}) collective-permute-start(bf16[1,32,2176]{2,1,0:T(8,128)(2,1)S(1)} %shard_map.111.refs_3_.refs_0_), channel_id=1, source_target_pairs={{0,5},{1,4},{2,7},{3,6},{4,1},{5,0},{6,3},{7,2},{8,13},{9,12},{10,... | collective-permute-start | bytes 417800 | tf_op jit(solution)/shard_map/ppermute | solution.py:46
  14.1 0.5 %collective-permute-start.4 = (bf16[1,32,2176]{2,1,0:T(8,128)(2,1)S(1)}, bf16[1,32,2176]{2,1,0:T(8,128)(2,1)S(1)}, u32[]{:S(2)}, u32[]{:S(2)}) collective-permute-start(bf16[1,32,2176]{2,1,0:T(8,128)(2,1)S(1)} %shard_map.111.refs_3_.refs_0_), channel_id=1, source_target_pairs={{0,4},{1,5},{2,3},{3,2},{4,0},{5,1},{6,7},{7,6},{8,12},{9,13},{10,... | collective-permute-start | bytes 417800 | tf_op jit(solution)/shard_map/ppermute | solution.py:46
  14.6 0.5 %collective-permute-start.3 = (bf16[1,32,2176]{2,1,0:T(8,128)(2,1)S(1)}, bf16[1,32,2176]{2,1,0:T(8,128)(2,1)S(1)}, u32[]{:S(2)}, u32[]{:S(2)}) collective-permute-start(bf16[1,32,2176]{2,1,0:T(8,128)(2,1)S(1)} %shard_map.111.refs_3_.refs_0_), channel_id=1, source_target_pairs={{0,1},{1,0},{2,6},{3,7},{4,5},{5,4},{6,2},{7,3},{8,9},{9,8},{10,14... | collective-permute-start | bytes 417800 | tf_op jit(solution)/shard_map/ppermute | solution.py:46
  15.1 2.9 %shard_map.112 = (bf16[2048,512]{1,0:T(8,128)(2,1)S(1)}, bf16[2048,512]{1,0:T(8,128)(2,1)S(1)}, bf16[512,2048]{1,0:T(8,128)(2,1)S(1)}) custom-call(bf16[2048,512]{1,0:T(8,128)(2,1)} %bitcast.8, bf16[2048,512]{1,0:T(8,128)(2,1)} %bitcast.9, bf16[512,2048]{1,0:T(8,128)(2,1)} %bitcast.10, bf16[1,32,2176]{2,1,0:T(8,128)(2,1)S(1)} %shard_map.111.refs_3_.refs_0_), custom_call_target="tpu_custom_call" | custom-call | bytes 12582912 | tf_op jit(solution)/shard_map/pallas_call | solution.py:107
  18.0 0.0 copy-start
  18.0 1.3 %copy-done = bf16[2048,512]{1,0:T(8,128)(2,1)} copy-done((bf16[2048,512]{1,0:T(8,128)(2,1)}, bf16[2048,512]{1,0:T(8,128)(2,1)S(1)}, u32[]{:S(2)}) %copy-start) | copy-done | bytes 2097176
  19.3 0.0 copy-start.2
  19.3 1.3 %copy-done.2 = bf16[512,2048]{1,0:T(8,128)(2,1)} copy-done((bf16[512,2048]{1,0:T(8,128)(2,1)}, bf16[512,2048]{1,0:T(8,128)(2,1)S(1)}, u32[]{:S(2)}) %copy-start.2) | copy-done | bytes 2097176
  20.6 0.0 collective-permute-start.6
  20.7 0.0 collective-permute-done.5.refs_3_
  20.7 0.5 %collective-permute-start.9 = (bf16[1,32,2176]{2,1,0:T(8,128)(2,1)S(1)}, bf16[1,32,2176]{2,1,0:T(8,128)(2,1)S(1)}, u32[]{:S(2)}, u32[]{:S(2)}) collective-permute-start(bf16[1,32,2176]{2,1,0:T(8,128)(2,1)S(1)} %collective-permute-done.5.refs_3_), channel_id=1, source_target_pairs={{0,2},{1,3},{2,0},{3,1},{4,6},{5,7},{6,4},{7,5},{8,10},{9,11},{10,... | collective-permute-start | bytes 417800 | tf_op jit(solution)/shard_map/ppermute | solution.py:46
  21.2 0.0 collective-permute-done.4.refs_2_
  21.2 0.1 collective-permute-start.8
  21.2 0.0 collective-permute-done.3.refs_1_
  21.2 0.4 collective-permute-start.7
  21.7 0.3 collective-permute-done.6.refs_4_
  22.0 0.2 collective-permute-done.9.refs_7_
  22.2 0.3 collective-permute-done.8.refs_6_
  22.5 0.2 collective-permute-done.7.refs_5_
  22.7 0.0 copy-start.1
  22.7 1.6 %copy-done.1 = bf16[2048,512]{1,0:T(8,128)(2,1)S(1)} copy-done((bf16[2048,512]{1,0:T(8,128)(2,1)S(1)}, bf16[2048,512]{1,0:T(8,128)(2,1)}, u32[]{:S(2)}) %copy-start.1) | copy-done | bytes 2097176
  24.3 0.0 copy-start.3
  24.3 1.6 %copy-done.3 = bf16[512,2048]{1,0:T(8,128)(2,1)S(1)} copy-done((bf16[512,2048]{1,0:T(8,128)(2,1)S(1)}, bf16[512,2048]{1,0:T(8,128)(2,1)}, u32[]{:S(2)}) %copy-start.3) | copy-done | bytes 2097176
  25.9 3.2 %shard_map.113 = (bf16[1,32,2048]{2,1,0:T(8,128)(2,1)S(1)}, bf16[1,32,2048]{2,1,0:T(8,128)(2,1)S(1)}, bf16[1,32,2048]{2,1,0:T(8,128)(2,1)S(1)}, bf16[1,32,2048]{...) custom-call(bf16[1,32,2176]{2,1,0:T(8,128)(2,1)S(1)} %shard_map.111., ...), custom_call_target="tpu_custom_call" | custom-call | flops 1610612736 | bytes 10485760 | tf_op jit(solution)/shard_map/pallas_call | solution.py:182
  29.1 0.4 collective-permute-start.11
  29.5 0.2 collective-permute-start.13
  29.6 0.3 collective-permute-start.15
  30.0 0.2 collective-permute-start.10
  30.2 0.3 collective-permute-done.11.b_ref
  30.5 1.6 %collective-permute-start.12 = (bf16[1,32,2048]{2,1,0:T(8,128)(2,1)S(1)}, bf16[1,32,2048]{2,1,0:T(8,128)(2,1)S(1)}, u32[]{:S(2)}, u32[]{:S(2)}) collective-permute-start(bf16[1,32,2048]{2,1,0:T(8,128)(2,1)S(1)} %shard_map.114), channel_id=1, source_target_pairs={{0,1},{1,0},{2,6},{3,7},{4,5},{5,4},{6,2},{7,3},{8,9},{9,8},{10,14... | collective-permute-start | bytes 393224 | tf_op jit(solution)/shard_map/ppermute | solution.py:46
  32.1 0.0 collective-permute-done.13.b_ref
  32.1 1.6 %collective-permute-start.14 = (bf16[1,32,2048]{2,1,0:T(8,128)(2,1)S(1)}, bf16[1,32,2048]{2,1,0:T(8,128)(2,1)S(1)}, u32[]{:S(2)}, u32[]{:S(2)}) collective-permute-start(bf16[1,32,2048]{2,1,0:T(8,128)(2,1)S(1)} %shard_map.115), channel_id=1, source_target_pairs={{0,4},{1,5},{2,3},{3,2},{4,0},{5,1},{6,7},{7,6},{8,12},{9,13},{10,... | collective-permute-start | bytes 393224 | tf_op jit(solution)/shard_map/ppermute | solution.py:46
  33.7 0.0 collective-permute-done.15.b_ref
  33.8 0.5 %collective-permute-start.16 = (bf16[1,32,2048]{2,1,0:T(8,128)(2,1)S(1)}, bf16[1,32,2048]{2,1,0:T(8,128)(2,1)S(1)}, u32[]{:S(2)}, u32[]{:S(2)}) collective-permute-start(bf16[1,32,2048]{2,1,0:T(8,128)(2,1)S(1)} %shard_map.116), channel_id=1, source_target_pairs={{0,5},{1,4},{2,7},{3,6},{4,1},{5,0},{6,3},{7,2},{8,13},{9,12},{10,... | collective-permute-start | bytes 393224 | tf_op jit(solution)/shard_map/ppermute | solution.py:46
  34.3 2.6 %shard_map.117 = (bf16[2048,512]{1,0:T(8,128)(2,1)}, bf16[2048,512]{1,0:T(8,128)(2,1)}) custom-call(bf16[128,2048]{1,0:T(8,128)(2,1)S(1)} %get-tuple-element.48.l_ref, bf16[128,512]{1,0:T(8,128)(2,1)S(1)} %get-tuple-element.49.refs_0_, bf16[128,512]{1,0:T(8,128)(2,1)S(1)} %get-tuple-element.50.refs_1_), custom_call_target="tpu_custom_call" | custom-call | flops 536870912 | bytes 4194304 | tf_op jit(solution)/shard_map/pallas_call | solution.py:203
  36.9 0.0 collective-permute-done.10.refs_1_
  36.9 0.0 collective-permute-done.12.refs_2_
  36.9 0.3 collective-permute-done.14.refs_3_
  37.2 3.3 %collective-permute-done.16.refs_4_ = bf16[1,32,2048]{2,1,0:T(8,128)(2,1)S(1)} collective-permute-done((bf16[1,32,2048]{2,1,0:T(8,128)(2,1)S(1)}, bf16[1,32,2048]{2,1,0:T(8,128)(2,1)S(1)}, u32[]{:S(2)}, u32[]{:S(2)}) %collective-permute-start.16) | collective-permute-done | bytes 131104 | tf_op jit(solution)/shard_map/ppermute | solution.py:46
  40.4 0.1 shard_map.118
  40.5 0.1 collective-permute-start.17
  40.6 2.1 %collective-permute-start.18 = (bf16[1,8,2048]{2,1,0:T(8,128)(2,1)S(1)}, bf16[1,8,2048]{2,1,0:T(8,128)(2,1)S(1)}, u32[]{:S(2)}, u32[]{:S(2)}) collective-permute-start(bf16[1,8,2048]{2,1,0:T(8,128)(2,1)S(1)} %get-tuple-element.54), channel_id=1, source_target_pairs={{0,16},{1,17},{2,18},{3,19},{4,20},{5,21},{6,22},{7,23},{8,24},{9,... | collective-permute-start | bytes 98312 | tf_op jit(solution)/shard_map/ppermute | solution.py:46
  42.7 2.3 %collective-permute-start.19 = (bf16[1,8,2048]{2,1,0:T(8,128)(2,1)S(1)}, bf16[1,8,2048]{2,1,0:T(8,128)(2,1)S(1)}, u32[]{:S(2)}, u32[]{:S(2)}) collective-permute-start(bf16[1,8,2048]{2,1,0:T(8,128)(2,1)S(1)} %get-tuple-element.55), channel_id=1, source_target_pairs={{0,24},{1,25},{2,26},{3,27},{4,28},{5,29},{6,30},{7,31},{8,16},{9,... | collective-permute-start | bytes 98312 | tf_op jit(solution)/shard_map/ppermute | solution.py:46
  45.0 1.9 %shard_map.119.refs_4_ = bf16[512,2048]{1,0:T(8,128)(2,1)} custom-call(bf16[128,512]{1,0:T(8,128)(2,1)S(1)} %get-tuple-element.56.l_ref, bf16[128,2048]{1,0:T(8,128)(2,1)S(1)} %get-tuple-element.57.refs_0_), custom_call_target="tpu_custom_call" | custom-call | flops 268435456 | bytes 2097152 | tf_op jit(solution)/shard_map/pallas_call | solution.py:203
  46.9 0.0 collective-permute-done.17.refs_1_
  46.9 0.0 collective-permute-done.18.refs_2_
  46.9 1.5 %collective-permute-done.19.refs_3_ = bf16[1,8,2048]{2,1,0:T(8,128)(2,1)S(1)} collective-permute-done((bf16[1,8,2048]{2,1,0:T(8,128)(2,1)S(1)}, bf16[1,8,2048]{2,1,0:T(8,128)(2,1)S(1)}, u32[]{:S(2)}, u32[]{:S(2)}) %collective-permute-start.19) | collective-permute-done | bytes 32800 | tf_op jit(solution)/shard_map/ppermute | solution.py:46
  48.4 0.6 %shard_map.120 = (bf16[4,2048]{1,0:T(4,128)(2,1)}, bf16[4,2048]{1,0:T(4,128)(2,1)}) custom-call(f32[1,8,2048]{2,1,0:T(8,128)S(1)} %get-tuple-element.52.refs_0_, bf16[1,8,2048]{2,1,0:T(8,128)(2,1)S(1)} %collective-permute-done.17.refs_1_, bf16[1,8,2048]{2,1,0:T(8,128)(2,1)S(1)} %collective-permute-done.18.refs_2_, ...), custom_call_target="tpu_custom_call" | custom-call | bytes 65536 | tf_op jit(solution)/shard_map/pallas_call | solution.py:285
  (4 shorter events, 0.1 us)
Async XLA Ops:
  1.6 7.0 %collective-permute-start.2 = (bf16[1,8,2176]{2,1,0:T(8,128)(2,1)S(1)}, bf16[1,8,2176]{2,1,0:T(8,128)(2,1)S(1)}, u32[]{:S(2)}, u32[]{:S(2)}) collective-permute-start(bf16[1,8,2176]{2,1,0:T(8,128)(2,1)S(1)} %shard_map.110.refs_0_), channel_id=1, source_target_pairs={{0,24},{1,25},{2,26},{3,27},{4,28},{5,29},{6,30},{7,31},{8,16},{9,... | collective-permute-start | bytes 104456 | tf_op jit(solution)/shard_map/ppermute | solution.py:46
  6.7 4.8 %collective-permute-start.1 = (bf16[1,8,2176]{2,1,0:T(8,128)(2,1)S(1)}, bf16[1,8,2176]{2,1,0:T(8,128)(2,1)S(1)}, u32[]{:S(2)}, u32[]{:S(2)}) collective-permute-start(bf16[1,8,2176]{2,1,0:T(8,128)(2,1)S(1)} %shard_map.110.refs_0_), channel_id=1, source_target_pairs={{0,16},{1,17},{2,18},{3,19},{4,20},{5,21},{6,22},{7,23},{8,24},{9,... | collective-permute-start | bytes 104456 | tf_op jit(solution)/shard_map/ppermute | solution.py:46
  6.7 4.8 %collective-permute-start = (bf16[1,8,2176]{2,1,0:T(8,128)(2,1)S(1)}, bf16[1,8,2176]{2,1,0:T(8,128)(2,1)S(1)}, u32[]{:S(2)}, u32[]{:S(2)}) collective-permute-start(bf16[1,8,2176]{2,1,0:T(8,128)(2,1)S(1)} %shard_map.110.refs_0_), channel_id=1, source_target_pairs={{0,8},{1,9},{2,10},{3,11},{4,12},{5,13},{6,14},{7,15},{8,0},{9,1},... | collective-permute-start | bytes 104456 | tf_op jit(solution)/shard_map/ppermute | solution.py:46
  11.6 9.1 %collective-permute-start.5 = (bf16[1,32,2176]{2,1,0:T(8,128)(2,1)S(1)}, bf16[1,32,2176]{2,1,0:T(8,128)(2,1)S(1)}, u32[]{:S(2)}, u32[]{:S(2)}) collective-permute-start(bf16[1,32,2176]{2,1,0:T(8,128)(2,1)S(1)} %shard_map.111.refs_3_.refs_0_), channel_id=1, source_target_pairs={{0,5},{1,4},{2,7},{3,6},{4,1},{5,0},{6,3},{7,2},{8,13},{9,12},{10,... | collective-permute-start | bytes 417800 | tf_op jit(solution)/shard_map/ppermute | solution.py:46
  14.1 7.1 %collective-permute-start.4 = (bf16[1,32,2176]{2,1,0:T(8,128)(2,1)S(1)}, bf16[1,32,2176]{2,1,0:T(8,128)(2,1)S(1)}, u32[]{:S(2)}, u32[]{:S(2)}) collective-permute-start(bf16[1,32,2176]{2,1,0:T(8,128)(2,1)S(1)} %shard_map.111.refs_3_.refs_0_), channel_id=1, source_target_pairs={{0,4},{1,5},{2,3},{3,2},{4,0},{5,1},{6,7},{7,6},{8,12},{9,13},{10,... | collective-permute-start | bytes 417800 | tf_op jit(solution)/shard_map/ppermute | solution.py:46
  14.6 6.7 %collective-permute-start.3 = (bf16[1,32,2176]{2,1,0:T(8,128)(2,1)S(1)}, bf16[1,32,2176]{2,1,0:T(8,128)(2,1)S(1)}, u32[]{:S(2)}, u32[]{:S(2)}) collective-permute-start(bf16[1,32,2176]{2,1,0:T(8,128)(2,1)S(1)} %shard_map.111.refs_3_.refs_0_), channel_id=1, source_target_pairs={{0,1},{1,0},{2,6},{3,7},{4,5},{5,4},{6,2},{7,3},{8,9},{9,8},{10,14... | collective-permute-start | bytes 417800 | tf_op jit(solution)/shard_map/ppermute | solution.py:46
  18.0 1.3 %copy-start = (bf16[2048,512]{1,0:T(8,128)(2,1)}, bf16[2048,512]{1,0:T(8,128)(2,1)S(1)}, u32[]{:S(2)}) copy-start(bf16[2048,512]{1,0:T(8,128)(2,1)S(1)} %get-tuple-element.38.refs_10_) | copy-start | bytes 6291460
  19.3 1.3 %copy-start.2 = (bf16[512,2048]{1,0:T(8,128)(2,1)}, bf16[512,2048]{1,0:T(8,128)(2,1)S(1)}, u32[]{:S(2)}) copy-start(bf16[512,2048]{1,0:T(8,128)(2,1)S(1)} %get-tuple-element.39.refs_11_) | copy-start | bytes 6291460
  20.6 1.4 %collective-permute-start.6 = (bf16[1,32,2176]{2,1,0:T(8,128)(2,1)S(1)}, bf16[1,32,2176]{2,1,0:T(8,128)(2,1)S(1)}, u32[]{:S(2)}, u32[]{:S(2)}) collective-permute-start(bf16[1,32,2176]{2,1,0:T(8,128)(2,1)S(1)} %shard_map.111.refs_3_.refs_0_), channel_id=1, source_target_pairs={{0,2},{1,3},{2,0},{3,1},{4,6},{5,7},{6,4},{7,5},{8,10},{9,11},{10,... | collective-permute-start | bytes 417800 | tf_op jit(solution)/shard_map/ppermute | solution.py:46
  20.7 1.6 %collective-permute-start.9 = (bf16[1,32,2176]{2,1,0:T(8,128)(2,1)S(1)}, bf16[1,32,2176]{2,1,0:T(8,128)(2,1)S(1)}, u32[]{:S(2)}, u32[]{:S(2)}) collective-permute-start(bf16[1,32,2176]{2,1,0:T(8,128)(2,1)S(1)} %collective-permute-done.5.refs_3_), channel_id=1, source_target_pairs={{0,2},{1,3},{2,0},{3,1},{4,6},{5,7},{6,4},{7,5},{8,10},{9,11},{10,... | collective-permute-start | bytes 417800 | tf_op jit(solution)/shard_map/ppermute | solution.py:46
  21.2 1.4 %collective-permute-start.8 = (bf16[1,32,2176]{2,1,0:T(8,128)(2,1)S(1)}, bf16[1,32,2176]{2,1,0:T(8,128)(2,1)S(1)}, u32[]{:S(2)}, u32[]{:S(2)}) collective-permute-start(bf16[1,32,2176]{2,1,0:T(8,128)(2,1)S(1)} %collective-permute-done.4.refs_2_), channel_id=1, source_target_pairs={{0,2},{1,3},{2,0},{3,1},{4,6},{5,7},{6,4},{7,5},{8,10},{9,11},{10,... | collective-permute-start | bytes 417800 | tf_op jit(solution)/shard_map/ppermute | solution.py:46
  21.2 1.5 %collective-permute-start.7 = (bf16[1,32,2176]{2,1,0:T(8,128)(2,1)S(1)}, bf16[1,32,2176]{2,1,0:T(8,128)(2,1)S(1)}, u32[]{:S(2)}, u32[]{:S(2)}) collective-permute-start(bf16[1,32,2176]{2,1,0:T(8,128)(2,1)S(1)} %collective-permute-done.3.refs_1_), channel_id=1, source_target_pairs={{0,2},{1,3},{2,0},{3,1},{4,6},{5,7},{6,4},{7,5},{8,10},{9,11},{10,... | collective-permute-start | bytes 417800 | tf_op jit(solution)/shard_map/ppermute | solution.py:46
  22.7 1.6 %copy-start.1 = (bf16[2048,512]{1,0:T(8,128)(2,1)S(1)}, bf16[2048,512]{1,0:T(8,128)(2,1)}, u32[]{:S(2)}) copy-start(bf16[2048,512]{1,0:T(8,128)(2,1)} %copy-done) | copy-start | bytes 6291460
  24.3 1.6 %copy-start.3 = (bf16[512,2048]{1,0:T(8,128)(2,1)S(1)}, bf16[512,2048]{1,0:T(8,128)(2,1)}, u32[]{:S(2)}) copy-start(bf16[512,2048]{1,0:T(8,128)(2,1)} %copy-done.2) | copy-start | bytes 6291460
  29.1 1.4 %collective-permute-start.11 = (bf16[1,32,2048]{2,1,0:T(8,128)(2,1)S(1)}, bf16[1,32,2048]{2,1,0:T(8,128)(2,1)S(1)}, u32[]{:S(2)}, u32[]{:S(2)}) collective-permute-start(bf16[1,32,2048]{2,1,0:T(8,128)(2,1)S(1)} %get-tuple-element.43), channel_id=1, source_target_pairs={{0,2},{1,3},{2,0},{3,1},{4,6},{5,7},{6,4},{7,5},{8,10},{9,11},{10,... | collective-permute-start | bytes 393224 | tf_op jit(solution)/shard_map/ppermute | solution.py:46
  29.5 2.6 %collective-permute-start.13 = (bf16[1,32,2048]{2,1,0:T(8,128)(2,1)S(1)}, bf16[1,32,2048]{2,1,0:T(8,128)(2,1)S(1)}, u32[]{:S(2)}, u32[]{:S(2)}) collective-permute-start(bf16[1,32,2048]{2,1,0:T(8,128)(2,1)S(1)} %get-tuple-element.45), channel_id=1, source_target_pairs={{0,2},{1,3},{2,0},{3,1},{4,6},{5,7},{6,4},{7,5},{8,10},{9,11},{10,... | collective-permute-start | bytes 393224 | tf_op jit(solution)/shard_map/ppermute | solution.py:46
  29.6 4.1 %collective-permute-start.15 = (bf16[1,32,2048]{2,1,0:T(8,128)(2,1)S(1)}, bf16[1,32,2048]{2,1,0:T(8,128)(2,1)S(1)}, u32[]{:S(2)}, u32[]{:S(2)}) collective-permute-start(bf16[1,32,2048]{2,1,0:T(8,128)(2,1)S(1)} %get-tuple-element.47), channel_id=1, source_target_pairs={{0,2},{1,3},{2,0},{3,1},{4,6},{5,7},{6,4},{7,5},{8,10},{9,11},{10,... | collective-permute-start | bytes 393224 | tf_op jit(solution)/shard_map/ppermute | solution.py:46
  30.0 6.9 %collective-permute-start.10 = (bf16[1,32,2048]{2,1,0:T(8,128)(2,1)S(1)}, bf16[1,32,2048]{2,1,0:T(8,128)(2,1)S(1)}, u32[]{:S(2)}, u32[]{:S(2)}) collective-permute-start(bf16[1,32,2048]{2,1,0:T(8,128)(2,1)S(1)} %get-tuple-element.41), channel_id=1, source_target_pairs={{0,2},{1,3},{2,0},{3,1},{4,6},{5,7},{6,4},{7,5},{8,10},{9,11},{10,... | collective-permute-start | bytes 393224 | tf_op jit(solution)/shard_map/ppermute | solution.py:46
  30.5 6.4 %collective-permute-start.12 = (bf16[1,32,2048]{2,1,0:T(8,128)(2,1)S(1)}, bf16[1,32,2048]{2,1,0:T(8,128)(2,1)S(1)}, u32[]{:S(2)}, u32[]{:S(2)}) collective-permute-start(bf16[1,32,2048]{2,1,0:T(8,128)(2,1)S(1)} %shard_map.114), channel_id=1, source_target_pairs={{0,1},{1,0},{2,6},{3,7},{4,5},{5,4},{6,2},{7,3},{8,9},{9,8},{10,14... | collective-permute-start | bytes 393224 | tf_op jit(solution)/shard_map/ppermute | solution.py:46
  32.1 5.0 %collective-permute-start.14 = (bf16[1,32,2048]{2,1,0:T(8,128)(2,1)S(1)}, bf16[1,32,2048]{2,1,0:T(8,128)(2,1)S(1)}, u32[]{:S(2)}, u32[]{:S(2)}) collective-permute-start(bf16[1,32,2048]{2,1,0:T(8,128)(2,1)S(1)} %shard_map.115), channel_id=1, source_target_pairs={{0,4},{1,5},{2,3},{3,2},{4,0},{5,1},{6,7},{7,6},{8,12},{9,13},{10,... | collective-permute-start | bytes 393224 | tf_op jit(solution)/shard_map/ppermute | solution.py:46
  33.8 6.7 %collective-permute-start.16 = (bf16[1,32,2048]{2,1,0:T(8,128)(2,1)S(1)}, bf16[1,32,2048]{2,1,0:T(8,128)(2,1)S(1)}, u32[]{:S(2)}, u32[]{:S(2)}) collective-permute-start(bf16[1,32,2048]{2,1,0:T(8,128)(2,1)S(1)} %shard_map.116), channel_id=1, source_target_pairs={{0,5},{1,4},{2,7},{3,6},{4,1},{5,0},{6,3},{7,2},{8,13},{9,12},{10,... | collective-permute-start | bytes 393224 | tf_op jit(solution)/shard_map/ppermute | solution.py:46
  40.5 6.4 %collective-permute-start.17 = (bf16[1,8,2048]{2,1,0:T(8,128)(2,1)S(1)}, bf16[1,8,2048]{2,1,0:T(8,128)(2,1)S(1)}, u32[]{:S(2)}, u32[]{:S(2)}) collective-permute-start(bf16[1,8,2048]{2,1,0:T(8,128)(2,1)S(1)} %get-tuple-element.53), channel_id=1, source_target_pairs={{0,8},{1,9},{2,10},{3,11},{4,12},{5,13},{6,14},{7,15},{8,0},{9,1},... | collective-permute-start | bytes 98312 | tf_op jit(solution)/shard_map/ppermute | solution.py:46
  40.6 6.3 %collective-permute-start.18 = (bf16[1,8,2048]{2,1,0:T(8,128)(2,1)S(1)}, bf16[1,8,2048]{2,1,0:T(8,128)(2,1)S(1)}, u32[]{:S(2)}, u32[]{:S(2)}) collective-permute-start(bf16[1,8,2048]{2,1,0:T(8,128)(2,1)S(1)} %get-tuple-element.54), channel_id=1, source_target_pairs={{0,16},{1,17},{2,18},{3,19},{4,20},{5,21},{6,22},{7,23},{8,24},{9,... | collective-permute-start | bytes 98312 | tf_op jit(solution)/shard_map/ppermute | solution.py:46
  42.7 5.7 %collective-permute-start.19 = (bf16[1,8,2048]{2,1,0:T(8,128)(2,1)S(1)}, bf16[1,8,2048]{2,1,0:T(8,128)(2,1)S(1)}, u32[]{:S(2)}, u32[]{:S(2)}) collective-permute-start(bf16[1,8,2048]{2,1,0:T(8,128)(2,1)S(1)} %get-tuple-element.55), channel_id=1, source_target_pairs={{0,24},{1,25},{2,26},{3,27},{4,28},{5,29},{6,30},{7,31},{8,16},{9,... | collective-permute-start | bytes 98312 | tf_op jit(solution)/shard_map/ppermute | solution.py:46

commit v4 on v3

--- a/solution.py
+++ b/solution.py
@@ -9,7 +9,8 @@
 ROWS = 4
 GROUP = 4
 CHUNK = 8
-VMEM_LIMIT = 16 * 1024 * 1024
+LARGE = 16 * 1024 * 1024
+SMALL = 4 * 1024 * 1024
 F32 = jnp.float32
 BF16 = jnp.bfloat16
 
@@ -30,8 +31,8 @@
     return jax.ShapeDtypeStruct(dims, dtype)
 
 
-def params():
-    return pltpu.CompilerParams(vmem_limit_bytes=VMEM_LIMIT)
+def params(limit=SMALL):
+    return pltpu.CompilerParams(vmem_limit_bytes=limit)
 
 
 def cost(flops, moved):
@@ -95,10 +96,32 @@
     )(*outside(args))
 
 
-def fetch(arrays, after):
-    def body(*refs):
-        n = len(arrays)
-        copies = [pltpu.make_async_copy(refs[k], refs[n + 1 + k], refs[-1].at[k]) for k in range(n)]
+def fetch(w, block):
+    def body(w_ref, b_ref, o_ref, c_ref, sem):
+        copy = pltpu.make_async_copy(w_ref, o_ref, sem)
+        copy.start()
+        c_ref[...] = b_ref[...]
+        copy.wait()
+
+    return pl.pallas_call(
+        body,
+        out_shape=[shape(*w.shape), shape(*block.shape)],
+        in_specs=[hbm(), vmem()],
+        out_specs=[vmem(), vmem()],
+        scratch_shapes=[pltpu.SemaphoreType.DMA],
+        compiler_params=params(),
+        cost_estimate=cost(0, 4 << 20),
+    )(*outside((w,)), block)
+
+
+def fetch_behind(w_down, w_up, after):
+    rows = w_up.shape[0] // 2
+
+    def body(d_ref, u_ref, _, od_ref, ou_ref, sems):
+        copies = [
+            pltpu.make_async_copy(d_ref, od_ref, sems.at[0]),
+            pltpu.make_async_copy(u_ref.at[:rows], ou_ref, sems.at[1]),
+        ]
         for c in copies:
             c.start()
         for c in copies:
@@ -106,13 +129,13 @@
 
     return pl.pallas_call(
         body,
-        out_shape=[shape(*a.shape, dtype=a.dtype) for a in arrays],
-        in_specs=[hbm() for _ in arrays] + [pl.BlockSpec(memory_space=pl.ANY)],
-        out_specs=[vmem() for _ in arrays],
-        scratch_shapes=[pltpu.SemaphoreType.DMA((len(arrays),))],
-        compiler_params=params(),
-        cost_estimate=cost(0, 12 << 20),
-    )(*outside(arrays), after)
+        out_shape=[shape(*w_down.shape), shape(rows, w_up.shape[1])],
+        in_specs=[hbm(), hbm(), pl.BlockSpec(memory_space=pl.ANY)],
+        out_specs=[vmem(), vmem()],
+        scratch_shapes=[pltpu.SemaphoreType.DMA((2,))],
+        compiler_params=params(),
+        cost_estimate=cost(0, 6 << 20),
+    )(*outside((w_down, w_up)), after)
 
 
 def regroup(blocks):
@@ -136,9 +159,9 @@
     )(*blocks)
 
 
-def expert_math(pieces, me, w_gate, w_up, w_down, experts, splits):
+def expert_math(pieces, me, w_gate, w_down, w_first, w_up, experts, splits):
     blocks = sum(p.shape[0] for p in pieces)
-    width, hid = w_gate.shape
+    hid, width = w_down.shape
     _, rows, full = pieces[0].shape
     lanes = full - width
     half = rows // 2
@@ -146,22 +169,26 @@
     count = len(pieces)
 
     def body(*refs):
-        me_ref, wg_ref, wu_ref, wd_ref = refs[count : count + 4]
-        outs = refs[count + 4 :]
+        me_ref, wg_ref, wd_ref, wu_ref, up_in = refs[count : count + 5]
+        outs = refs[count + 5 : -5]
+        late_ref, gate_ref, upper_ref, dact_ref, sem = refs[-5:]
         parts, (t_ref, do_ref, h_ref, dg_ref, du_ref) = outs[: len(splits)], outs[len(splits) :]
+        copy = pltpu.make_async_copy(up_in.at[width // 2 :], late_ref, sem)
+        copy.start()
         x = jnp.concatenate([r[...] for r in refs[:count]], axis=0)
-        token = x[:, :half, :width].reshape(m, width)
-        t_ref[...] = token
+        t_ref[...] = x[:, :half, :width].reshape(m, width)
+        gate_ref[...] = dot(t_ref[...], wg_ref[...])
         side = x[:, :half, width:].reshape(m, lanes).astype(F32)
         lane = lax.broadcasted_iota(jnp.int32, (1, lanes), 1)
         mine = me_ref[0]
         scale = jnp.where(lane == mine, 1.0 / 256.0, 0.0) + jnp.where(lane == mine + experts, 1.0 / 65536.0, 0.0)
         coef = jnp.sum(side * scale, axis=1, keepdims=True)
-        dout = (coef * x[:, half:, :width].reshape(m, width).astype(F32)).astype(BF16)
-        do_ref[...] = dout
-        gate = dot(token, wg_ref[...])
-        upper = dot(token, wu_ref[...])
-        dact = dot(dout, wd_ref[...], 1, 1)
+        do_ref[...] = (coef * x[:, half:, :width].reshape(m, width).astype(F32)).astype(BF16)
+        dact_ref[...] = dot(do_ref[...], wd_ref[...], 1, 1)
+        upper_ref[...] = dot(t_ref[:, : width // 2], wu_ref[...])
+        copy.wait()
+        gate, dact = gate_ref[...], dact_ref[...]
+        upper = upper_ref[...] + dot(t_ref[:, width // 2 :], late_ref[...])
         sig = jax.nn.sigmoid(gate)
         swish = gate * sig
         hidden = (swish * upper).astype(BF16)
@@ -169,7 +196,8 @@
         dupper = (dact * swish).astype(BF16)
         h_ref[...], dg_ref[...], du_ref[...] = hidden, dgate, dupper
         part = (coef * dot(hidden, wd_ref[...])).astype(BF16).reshape(blocks, half, width)
-        back = dot(dgate, wg_ref[...], 1, 1) + dot(dupper, wu_ref[...], 1, 1)
+        back = jnp.concatenate([dot(dupper, w[...], 1, 1) for w in (wu_ref, late_ref)], axis=1)
+        back = dot(dgate, wg_ref[...], 1, 1) + back
         back = back.astype(BF16).reshape(blocks, half, width)
         at = 0
         for ref, n in zip(parts, splits):
@@ -182,11 +210,18 @@
     got = pl.pallas_call(
         body,
         out_shape=outs,
-        in_specs=[vmem()] * count + [pl.BlockSpec(memory_space=pltpu.SMEM)] + [vmem()] * 3,
+        in_specs=[vmem()] * count + [pl.BlockSpec(memory_space=pltpu.SMEM)] + [vmem()] * 3 + [hbm()],
         out_specs=[vmem() for _ in outs],
-        compiler_params=params(),
+        scratch_shapes=[
+            pltpu.VMEM((width // 2, hid), BF16),
+            pltpu.VMEM((m, hid), F32),
+            pltpu.VMEM((m, hid), F32),
+            pltpu.VMEM((m, hid), F32),
+            pltpu.SemaphoreType.DMA,
+        ],
+        compiler_params=params(LARGE),
         cost_estimate=cost(12 * m * width * hid, 10 << 20),
-    )(*pieces, me, w_gate, w_up, w_down)
+    )(*pieces, me, w_gate, w_down, w_first, *outside((w_up,)))
     return list(got[: len(splits)]), got[len(splits) :]
 
 
@@ -206,7 +241,7 @@
         out_shape=[shape(rows, cols) for _ in rights],
         in_specs=[pl.BlockSpec((m, tile), lambda i: (0, i))] + [pl.BlockSpec((m, cols), lambda i: (0, 0)) for _ in rights],
         out_specs=[pl.BlockSpec((tile, cols), lambda i: (i, 0)) for _ in rights],
-        compiler_params=params(),
+        compiler_params=params(LARGE),
         cost_estimate=cost(2 * m * rows * cols * len(rights), 2 * rows * cols * len(rights)),
     )(left, *rights)
 
@@ -305,20 +340,20 @@
     for masks in plan[1:]:
         held = [block] + [exchange(block, mask, total, core) for mask in masks]
         block = jnp.concatenate(held, axis=0)
-    wg, wu, wd = fetch((wg, wu, wd), held[0])
-    own, wg, wu, wd = lax.optimization_barrier((held[0], wg, wu, wd))
+    wg, own = fetch(wg, held[0])
+    wd, wu_first = fetch_behind(wd, wu, held[1])
     pieces = held + [exchange(h, (core, core), total, core) for h in [own] + held[1:]]
 
     ways = len(held)
     groups = total // GROUP
     size = groups // 2 // ways
     if groups <= CHUNK:
-        parts, kept = expert_math(pieces, me, wg, wu, wd, experts, [size] * (2 * ways))
+        parts, kept = expert_math(pieces, me, wg, wd, wu_first, wu, experts, [size] * (2 * ways))
     else:
         whole = jnp.concatenate(pieces, axis=0)
         sums, saved = [], []
         for at in range(0, groups, CHUNK):
-            (got,), rest = expert_math([whole[at : at + CHUNK]], me, wg, wu, wd, experts, [CHUNK])
+            (got,), rest = expert_math([whole[at : at + CHUNK]], me, wg, wd, wu_first, wu, experts, [CHUNK])
             sums.append(got)
             saved.append(rest)
         got = jnp.concatenate(sums, axis=0)
@@ -330,16 +365,17 @@
     (down_grad,) = weight_grads(hidden, [dout], 2)
 
     keep, send = parts[:ways], parts[ways:]
-    arrived = [exchange(p, (core, core), total, core) for p in send]
-    terms = [keep[0], arrived[0]]
-    for at, mask in enumerate(plan[-1]):
+    arrived = [exchange(p, (core, core), total, core) for p in send[::-1]][::-1]
+    terms = []
+    for at, mask in reversed(list(enumerate(plan[-1]))):
         terms.append(exchange(add_pair(keep[at + 1], arrived[at + 1]), mask, total, core))
+    terms += [keep[0], arrived[0]]
     for masks in reversed(plan[1:-1]):
         ways = len(masks) + 1
         mine, *others = add(terms, [terms[0].shape[0] // ways] * ways)
-        terms = [mine] + [exchange(o, mask, total, core) for o, mask in zip(others, masks)]
+        terms = [mine] + [exchange(o, mask, total, core) for o, mask in zip(others[::-1], masks[::-1])]
     mine, *others = add_ungroup(terms, (gate_grad,))
-    terms = [mine] + [exchange(o, mask, total, core) for o, mask in zip(others, plan[0])]
+    terms = [mine] + [exchange(o, mask, total, core) for o, mask in zip(others[::-1], plan[0][::-1])]
     mixed, back = finish(terms, (down_grad,))
     return mixed, back, gate_grad[None], up_grad[None], down_grad[None]
 

time: 49.4 us -> 44.7 us (0.905)
  local copies, waits for them, and re-layouts: 5.81 us -> 0 us
  Pallas kernels: 12.3 us -> 13.5 us
  starting transfers between devices: 19.5 us -> 19 us
  waiting for transfers between devices: 10.6 us -> 11.1 us
    unnamed x8 -> x0, local copies, waits for them, and re-layouts: 5.81 us -> none
    pallas_call x1, Pallas kernels: 3.16 us -> 3.78 us  [expert_math(): pl.pallas_call(body, out_shape=outs, in_specs=[vmem()] * count + [pl.Bloc...]
    pallas_call x1 -> x2, Pallas kernels: 2.88 us -> 3.47 us  [the longest x1 1.87 us: fetch_behind(): pl.pallas_call(body, out_shape=[shape(*w_down.shape), shape(rows, w_up.sh...]
    ppermute x20, starting transfers between devices: 19.5 us -> 19 us  [exchange(): lax.ppermute(x, AXES, [(i, i ^ masks[i // core % 2]) for i in range(total)])]
  transfers between devices with their start and end apart: 20 -> 20, of which waited for: 10 -> 9; matrix products, arithmetic and copies ran while one was open for 0% -> 0% of each run, Pallas kernels for 15% -> 18%
where the time goes in v4:
time: 44.7 us; the launch traced here: 44.4 us
  starting transfers between devices  19 us (43%)
  Pallas kernels  13.5 us (30%)
  waiting for transfers between devices  11.1 us (25%)
  between operations  0.74 us (2%)
    ppermute x20, starting transfers between devices, exchange(): lax.ppermute(x, AXES, [(i, i ^ masks[i // core % 2]) for i in range(total)])  19 us
    ppermute x20, waiting for transfers between devices, exchange(): lax.ppermute(x, AXES, [(i, i ^ masks[i // core % 2]) for i in range(total)])  11.1 us
    pallas_call x2, Pallas kernels, weight_grads(): pl.pallas_call(body, grid=(steps,), out_shape=[shape(rows, cols) for _ in...  4.5 us
    pallas_call x1, Pallas kernels, expert_math(): pl.pallas_call(body, out_shape=outs, in_specs=[vmem()] * count + [pl.Bloc...  3.78 us
    pallas_call x1, Pallas kernels, fetch_behind(): pl.pallas_call(body, out_shape=[shape(*w_down.shape), shape(rows, w_up.sh...  1.87 us
    pallas_call x1, Pallas kernels, fetch(): pl.pallas_call(body, out_shape=[shape(*w.shape), shape(*block.shape)], in...  1.6 us
    pallas_call x1, Pallas kernels, pack(): pl.pallas_call(body, out_shape=shape(1, 2 * rows, width + lanes), in_spec...  0.92 us
  transfers between devices with their start and end apart: 20, of which 9 were waited for; matrix products, arithmetic and copies ran while one was open for 0% of the time, Pallas kernels for 18%

profile of v4, /device:TPU:0, one launch (start us, length us, event | category | flops | bytes accessed | tf_op | source)
XLA Modules:
  0.0 44.4 jit_solution(9735339874501206689)
XLA Ops:
  0.6 0.9 %shard_map.110.refs_0_ = bf16[1,8,2176]{2,1,0:T(8,128)(2,1)S(1)} custom-call(bf16[4,2048]{1,0:T(4,128)(2,1)} %t_in.1, s32[4,8]{1,0:T(4,128)} %i_in.1, s32[4,8]{1,0:T(4,128)} %w_in.1, bf16[4,2048]{1,0:T(4,128)(2,1)} %g_in.1), custom_call_target="tpu_custom_call" | custom-call | bytes 81920 | tf_op jit(solution)/shard_map/pallas_call | solution.py:88
  1.6 5.1 %collective-permute-start.2 = (bf16[1,8,2176]{2,1,0:T(8,128)(2,1)S(1)}, bf16[1,8,2176]{2,1,0:T(8,128)(2,1)S(1)}, u32[]{:S(2)}, u32[]{:S(2)}) collective-permute-start(bf16[1,8,2176]{2,1,0:T(8,128)(2,1)S(1)} %shard_map.110.refs_0_), channel_id=1, source_target_pairs={{0,24},{1,25},{2,26},{3,27},{4,28},{5,29},{6,30},{7,31},{8,16},{9,... | collective-permute-start | bytes 104456 | tf_op jit(solution)/shard_map/ppermute | solution.py:47
  6.7 0.0 collective-permute-start.1
  6.7 0.6 %collective-permute-start = (bf16[1,8,2176]{2,1,0:T(8,128)(2,1)S(1)}, bf16[1,8,2176]{2,1,0:T(8,128)(2,1)S(1)}, u32[]{:S(2)}, u32[]{:S(2)}) collective-permute-start(bf16[1,8,2176]{2,1,0:T(8,128)(2,1)S(1)} %shard_map.110.refs_0_), channel_id=1, source_target_pairs={{0,8},{1,9},{2,10},{3,11},{4,12},{5,13},{6,14},{7,15},{8,0},{9,1},... | collective-permute-start | bytes 104456 | tf_op jit(solution)/shard_map/ppermute | solution.py:47
  7.3 1.3 %collective-permute-done.2.refs_3_ = bf16[1,8,2176]{2,1,0:T(8,128)(2,1)S(1)} collective-permute-done((bf16[1,8,2176]{2,1,0:T(8,128)(2,1)S(1)}, bf16[1,8,2176]{2,1,0:T(8,128)(2,1)S(1)}, u32[]{:S(2)}, u32[]{:S(2)}) %collective-permute-start.2) | collective-permute-done | bytes 34848 | tf_op jit(solution)/shard_map/ppermute | solution.py:47
  8.6 2.9 %collective-permute-done.1.refs_2_ = bf16[1,8,2176]{2,1,0:T(8,128)(2,1)S(1)} collective-permute-done((bf16[1,8,2176]{2,1,0:T(8,128)(2,1)S(1)}, bf16[1,8,2176]{2,1,0:T(8,128)(2,1)S(1)}, u32[]{:S(2)}, u32[]{:S(2)}) %collective-permute-start.1) | collective-permute-done | bytes 34848 | tf_op jit(solution)/shard_map/ppermute | solution.py:47
  11.5 0.0 collective-permute-done.refs_1_
  11.6 2.5 %collective-permute-start.5 = (bf16[1,32,2176]{2,1,0:T(8,128)(2,1)S(1)}, bf16[1,32,2176]{2,1,0:T(8,128)(2,1)S(1)}, u32[]{:S(2)}, u32[]{:S(2)}) collective-permute-start(bf16[1,32,2176]{2,1,0:T(8,128)(2,1)S(1)} %shard_map.111.b_ref.refs_0_), channel_id=1, source_target_pairs={{0,5},{1,4},{2,7},{3,6},{4,1},{5,0},{6,3},{7,2},{8,13},{9,12},{10,... | collective-permute-start | bytes 417800 | tf_op jit(solution)/shard_map/ppermute | solution.py:47
  14.1 0.5 %collective-permute-start.4 = (bf16[1,32,2176]{2,1,0:T(8,128)(2,1)S(1)}, bf16[1,32,2176]{2,1,0:T(8,128)(2,1)S(1)}, u32[]{:S(2)}, u32[]{:S(2)}) collective-permute-start(bf16[1,32,2176]{2,1,0:T(8,128)(2,1)S(1)} %shard_map.111.b_ref.refs_0_), channel_id=1, source_target_pairs={{0,4},{1,5},{2,3},{3,2},{4,0},{5,1},{6,7},{7,6},{8,12},{9,13},{10,... | collective-permute-start | bytes 417800 | tf_op jit(solution)/shard_map/ppermute | solution.py:47
  14.6 0.5 %collective-permute-start.3 = (bf16[1,32,2176]{2,1,0:T(8,128)(2,1)S(1)}, bf16[1,32,2176]{2,1,0:T(8,128)(2,1)S(1)}, u32[]{:S(2)}, u32[]{:S(2)}) collective-permute-start(bf16[1,32,2176]{2,1,0:T(8,128)(2,1)S(1)} %shard_map.111.b_ref.refs_0_), channel_id=1, source_target_pairs={{0,1},{1,0},{2,6},{3,7},{4,5},{5,4},{6,2},{7,3},{8,9},{9,8},{10,14... | collective-permute-start | bytes 417800 | tf_op jit(solution)/shard_map/ppermute | solution.py:47
  15.1 1.6 %shard_map.112 = (bf16[2048,512]{1,0:T(8,128)(2,1)S(1)}, bf16[1,32,2176]{2,1,0:T(8,128)(2,1)S(1)}) custom-call(bf16[2048,512]{1,0:T(8,128)(2,1)} %bitcast.10, bf16[1,32,2176]{2,1,0:T(8,128)(2,1)S(1)} %shard_map.111.b_ref.refs_0_), custom_call_target="tpu_custom_call" | custom-call | bytes 4194304 | tf_op jit(solution)/shard_map/pallas_call | solution.py:106
  16.7 0.1 collective-permute-start.6
  16.8 1.3 %collective-permute-done.5.refs_3_ = bf16[1,32,2176]{2,1,0:T(8,128)(2,1)S(1)} collective-permute-done((bf16[1,32,2176]{2,1,0:T(8,128)(2,1)S(1)}, bf16[1,32,2176]{2,1,0:T(8,128)(2,1)S(1)}, u32[]{:S(2)}, u32[]{:S(2)}) %collective-permute-start.5) | collective-permute-done | bytes 139296 | tf_op jit(solution)/shard_map/ppermute | solution.py:47
  18.1 0.0 collective-permute-start.9
  18.1 1.4 %collective-permute-done.4.refs_2_ = bf16[1,32,2176]{2,1,0:T(8,128)(2,1)S(1)} collective-permute-done((bf16[1,32,2176]{2,1,0:T(8,128)(2,1)S(1)}, bf16[1,32,2176]{2,1,0:T(8,128)(2,1)S(1)}, u32[]{:S(2)}, u32[]{:S(2)}) %collective-permute-start.4) | collective-permute-done | bytes 139296 | tf_op jit(solution)/shard_map/ppermute | solution.py:47
  19.5 0.0 collective-permute-start.8
  19.5 0.1 collective-permute-done.3._.refs_1_
  19.6 0.4 collective-permute-start.7
  20.0 1.9 %shard_map.113 = (bf16[512,2048]{1,0:T(8,128)(2,1)S(1)}, bf16[1024,512]{1,0:T(8,128)(2,1)S(1)}) custom-call(bf16[512,2048]{1,0:T(8,128)(2,1)} %bitcast.11, bf16[2048,512]{1,0:T(8,128)(2,1)} %bitcast.8, bf16[1,32,2176]{2,1,0:T(8,128)(2,1)S(1)} %collective-permute-done.3._.refs_1_), custom_call_target="tpu_custom_call" | custom-call | bytes 6291456 | tf_op jit(solution)/shard_map/pallas_call | solution.py:130
  21.9 0.0 collective-permute-done.6.refs_4_
  21.9 0.0 collective-permute-done.9.refs_7_
  21.9 0.0 collective-permute-done.8.refs_6_
  21.9 0.0 collective-permute-done.7.refs_5_
  22.0 3.8 %shard_map.114 = (bf16[1,32,2048]{2,1,0:T(8,128)(2,1)S(1)}, bf16[1,32,2048]{2,1,0:T(8,128)(2,1)S(1)}, bf16[1,32,2048]{2,1,0:T(8,128)(2,1)S(1)}, bf16[1,32,2048]{...) custom-call(bf16[1,32,2176]{2,1,0:T(8,128)(2,1)S(1)} %shard_map.111., ...), custom_call_target="tpu_custom_call" | custom-call | flops 1610612736 | bytes 10485760 | tf_op jit(solution)/shard_map/pallas_call | solution.py:210
  25.8 0.2 collective-permute-start.10
  25.9 0.4 collective-permute-start.12
  26.3 0.1 collective-permute-start.14
  26.4 0.4 collective-permute-start.16
  26.8 0.3 collective-permute-done.10.b_ref
  27.2 2.5 %collective-permute-start.11 = (bf16[1,32,2048]{2,1,0:T(8,128)(2,1)S(1)}, bf16[1,32,2048]{2,1,0:T(8,128)(2,1)S(1)}, u32[]{:S(2)}, u32[]{:S(2)}) collective-permute-start(bf16[1,32,2048]{2,1,0:T(8,128)(2,1)S(1)} %shard_map.115), channel_id=1, source_target_pairs={{0,5},{1,4},{2,7},{3,6},{4,1},{5,0},{6,3},{7,2},{8,13},{9,12},{10,... | collective-permute-start | bytes 393224 | tf_op jit(solution)/shard_map/ppermute | solution.py:47
  29.7 0.0 collective-permute-done.12.b_ref
  29.7 0.6 %collective-permute-start.13 = (bf16[1,32,2048]{2,1,0:T(8,128)(2,1)S(1)}, bf16[1,32,2048]{2,1,0:T(8,128)(2,1)S(1)}, u32[]{:S(2)}, u32[]{:S(2)}) collective-permute-start(bf16[1,32,2048]{2,1,0:T(8,128)(2,1)S(1)} %shard_map.116), channel_id=1, source_target_pairs={{0,4},{1,5},{2,3},{3,2},{4,0},{5,1},{6,7},{7,6},{8,12},{9,13},{10,... | collective-permute-start | bytes 393224 | tf_op jit(solution)/shard_map/ppermute | solution.py:47
  30.3 0.0 collective-permute-done.14.b_ref
  30.4 0.6 %collective-permute-start.15 = (bf16[1,32,2048]{2,1,0:T(8,128)(2,1)S(1)}, bf16[1,32,2048]{2,1,0:T(8,128)(2,1)S(1)}, u32[]{:S(2)}, u32[]{:S(2)}) collective-permute-start(bf16[1,32,2048]{2,1,0:T(8,128)(2,1)S(1)} %shard_map.117), channel_id=1, source_target_pairs={{0,1},{1,0},{2,6},{3,7},{4,5},{5,4},{6,2},{7,3},{8,9},{9,8},{10,14... | collective-permute-start | bytes 393224 | tf_op jit(solution)/shard_map/ppermute | solution.py:47
  31.0 2.6 %shard_map.118 = (bf16[2048,512]{1,0:T(8,128)(2,1)}, bf16[2048,512]{1,0:T(8,128)(2,1)}) custom-call(bf16[128,2048]{1,0:T(8,128)(2,1)S(1)} %get-tuple-element.42.l_ref, bf16[128,512]{1,0:T(8,128)(2,1)S(1)} %get-tuple-element.43.refs_0_, bf16[128,512]{1,0:T(8,128)(2,1)S(1)} %get-tuple-element.44.refs_1_), custom_call_target="tpu_custom_call" | custom-call | flops 536870912 | bytes 4194304 | tf_op jit(solution)/shard_map/pallas_call | solution.py:238
  33.6 0.0 collective-permute-done.16.refs_4_
  33.6 0.9 %collective-permute-done.11.refs_0_ = bf16[1,32,2048]{2,1,0:T(8,128)(2,1)S(1)} collective-permute-done((bf16[1,32,2048]{2,1,0:T(8,128)(2,1)S(1)}, bf16[1,32,2048]{2,1,0:T(8,128)(2,1)S(1)}, u32[]{:S(2)}, u32[]{:S(2)}) %collective-permute-start.11) | collective-permute-done | bytes 131104 | tf_op jit(solution)/shard_map/ppermute | solution.py:47
  34.5 2.0 %collective-permute-done.13.refs_1_ = bf16[1,32,2048]{2,1,0:T(8,128)(2,1)S(1)} collective-permute-done((bf16[1,32,2048]{2,1,0:T(8,128)(2,1)S(1)}, bf16[1,32,2048]{2,1,0:T(8,128)(2,1)S(1)}, u32[]{:S(2)}, u32[]{:S(2)}) %collective-permute-start.13) | collective-permute-done | bytes 131104 | tf_op jit(solution)/shard_map/ppermute | solution.py:47
  36.5 0.0 collective-permute-done.15.refs_2_
  36.5 0.1 shard_map.119
  36.7 1.9 %collective-permute-start.17 = (bf16[1,8,2048]{2,1,0:T(8,128)(2,1)S(1)}, bf16[1,8,2048]{2,1,0:T(8,128)(2,1)S(1)}, u32[]{:S(2)}, u32[]{:S(2)}) collective-permute-start(bf16[1,8,2048]{2,1,0:T(8,128)(2,1)S(1)} %get-tuple-element.47), channel_id=1, source_target_pairs={{0,24},{1,25},{2,26},{3,27},{4,28},{5,29},{6,30},{7,31},{8,16},{9,... | collective-permute-start | bytes 98312 | tf_op jit(solution)/shard_map/ppermute | solution.py:47
  38.6 0.2 collective-permute-start.18
  38.8 2.3 %collective-permute-start.19 = (bf16[1,8,2048]{2,1,0:T(8,128)(2,1)S(1)}, bf16[1,8,2048]{2,1,0:T(8,128)(2,1)S(1)}, u32[]{:S(2)}, u32[]{:S(2)}) collective-permute-start(bf16[1,8,2048]{2,1,0:T(8,128)(2,1)S(1)} %get-tuple-element.49), channel_id=1, source_target_pairs={{0,8},{1,9},{2,10},{3,11},{4,12},{5,13},{6,14},{7,15},{8,0},{9,1},... | collective-permute-start | bytes 98312 | tf_op jit(solution)/shard_map/ppermute | solution.py:47
  41.1 1.9 %shard_map.120.refs_4_ = bf16[512,2048]{1,0:T(8,128)(2,1)} custom-call(bf16[128,512]{1,0:T(8,128)(2,1)S(1)} %get-tuple-element.50.l_ref, bf16[128,2048]{1,0:T(8,128)(2,1)S(1)} %get-tuple-element.51.refs_0_), custom_call_target="tpu_custom_call" | custom-call | flops 268435456 | bytes 2097152 | tf_op jit(solution)/shard_map/pallas_call | solution.py:238
  43.0 0.0 collective-permute-done.17.refs_1_
  43.0 0.7 %collective-permute-done.18.refs_2_ = bf16[1,8,2048]{2,1,0:T(8,128)(2,1)S(1)} collective-permute-done((bf16[1,8,2048]{2,1,0:T(8,128)(2,1)S(1)}, bf16[1,8,2048]{2,1,0:T(8,128)(2,1)S(1)}, u32[]{:S(2)}, u32[]{:S(2)}) %collective-permute-start.18) | collective-permute-done | bytes 32800 | tf_op jit(solution)/shard_map/ppermute | solution.py:47
  43.8 0.0 collective-permute-done.19.refs_3_
  43.8 0.6 %shard_map.121 = (bf16[4,2048]{1,0:T(4,128)(2,1)}, bf16[4,2048]{1,0:T(4,128)(2,1)}) custom-call(f32[1,8,2048]{2,1,0:T(8,128)S(1)} %get-tuple-element.46.refs_0_, bf16[1,8,2048]{2,1,0:T(8,128)(2,1)S(1)} %collective-permute-done.17.refs_1_, bf16[1,8,2048]{2,1,0:T(8,128)(2,1)S(1)} %collective-permute-done.18.refs_2_, ...), custom_call_target="tpu_custom_call" | custom-call | bytes 65536 | tf_op jit(solution)/shard_map/pallas_call | solution.py:320
  (4 shorter events, 0.1 us)
Async XLA Ops:
  1.6 7.0 %collective-permute-start.2 = (bf16[1,8,2176]{2,1,0:T(8,128)(2,1)S(1)}, bf16[1,8,2176]{2,1,0:T(8,128)(2,1)S(1)}, u32[]{:S(2)}, u32[]{:S(2)}) collective-permute-start(bf16[1,8,2176]{2,1,0:T(8,128)(2,1)S(1)} %shard_map.110.refs_0_), channel_id=1, source_target_pairs={{0,24},{1,25},{2,26},{3,27},{4,28},{5,29},{6,30},{7,31},{8,16},{9,... | collective-permute-start | bytes 104456 | tf_op jit(solution)/shard_map/ppermute | solution.py:47
  6.7 4.8 %collective-permute-start.1 = (bf16[1,8,2176]{2,1,0:T(8,128)(2,1)S(1)}, bf16[1,8,2176]{2,1,0:T(8,128)(2,1)S(1)}, u32[]{:S(2)}, u32[]{:S(2)}) collective-permute-start(bf16[1,8,2176]{2,1,0:T(8,128)(2,1)S(1)} %shard_map.110.refs_0_), channel_id=1, source_target_pairs={{0,16},{1,17},{2,18},{3,19},{4,20},{5,21},{6,22},{7,23},{8,24},{9,... | collective-permute-start | bytes 104456 | tf_op jit(solution)/shard_map/ppermute | solution.py:47
  6.7 4.8 %collective-permute-start = (bf16[1,8,2176]{2,1,0:T(8,128)(2,1)S(1)}, bf16[1,8,2176]{2,1,0:T(8,128)(2,1)S(1)}, u32[]{:S(2)}, u32[]{:S(2)}) collective-permute-start(bf16[1,8,2176]{2,1,0:T(8,128)(2,1)S(1)} %shard_map.110.refs_0_), channel_id=1, source_target_pairs={{0,8},{1,9},{2,10},{3,11},{4,12},{5,13},{6,14},{7,15},{8,0},{9,1},... | collective-permute-start | bytes 104456 | tf_op jit(solution)/shard_map/ppermute | solution.py:47
  11.6 6.5 %collective-permute-start.5 = (bf16[1,32,2176]{2,1,0:T(8,128)(2,1)S(1)}, bf16[1,32,2176]{2,1,0:T(8,128)(2,1)S(1)}, u32[]{:S(2)}, u32[]{:S(2)}) collective-permute-start(bf16[1,32,2176]{2,1,0:T(8,128)(2,1)S(1)} %shard_map.111.b_ref.refs_0_), channel_id=1, source_target_pairs={{0,5},{1,4},{2,7},{3,6},{4,1},{5,0},{6,3},{7,2},{8,13},{9,12},{10,... | collective-permute-start | bytes 417800 | tf_op jit(solution)/shard_map/ppermute | solution.py:47
  14.1 5.5 %collective-permute-start.4 = (bf16[1,32,2176]{2,1,0:T(8,128)(2,1)S(1)}, bf16[1,32,2176]{2,1,0:T(8,128)(2,1)S(1)}, u32[]{:S(2)}, u32[]{:S(2)}) collective-permute-start(bf16[1,32,2176]{2,1,0:T(8,128)(2,1)S(1)} %shard_map.111.b_ref.refs_0_), channel_id=1, source_target_pairs={{0,4},{1,5},{2,3},{3,2},{4,0},{5,1},{6,7},{7,6},{8,12},{9,13},{10,... | collective-permute-start | bytes 417800 | tf_op jit(solution)/shard_map/ppermute | solution.py:47
  14.6 5.1 %collective-permute-start.3 = (bf16[1,32,2176]{2,1,0:T(8,128)(2,1)S(1)}, bf16[1,32,2176]{2,1,0:T(8,128)(2,1)S(1)}, u32[]{:S(2)}, u32[]{:S(2)}) collective-permute-start(bf16[1,32,2176]{2,1,0:T(8,128)(2,1)S(1)} %shard_map.111.b_ref.refs_0_), channel_id=1, source_target_pairs={{0,1},{1,0},{2,6},{3,7},{4,5},{5,4},{6,2},{7,3},{8,9},{9,8},{10,14... | collective-permute-start | bytes 417800 | tf_op jit(solution)/shard_map/ppermute | solution.py:47
  16.7 5.2 %collective-permute-start.6 = (bf16[1,32,2176]{2,1,0:T(8,128)(2,1)S(1)}, bf16[1,32,2176]{2,1,0:T(8,128)(2,1)S(1)}, u32[]{:S(2)}, u32[]{:S(2)}) collective-permute-start(bf16[1,32,2176]{2,1,0:T(8,128)(2,1)S(1)} %get-tuple-element.30), channel_id=1, source_target_pairs={{0,2},{1,3},{2,0},{3,1},{4,6},{5,7},{6,4},{7,5},{8,10},{9,11},{10,... | collective-permute-start | bytes 417800 | tf_op jit(solution)/shard_map/ppermute | solution.py:47
  18.1 3.9 %collective-permute-start.9 = (bf16[1,32,2176]{2,1,0:T(8,128)(2,1)S(1)}, bf16[1,32,2176]{2,1,0:T(8,128)(2,1)S(1)}, u32[]{:S(2)}, u32[]{:S(2)}) collective-permute-start(bf16[1,32,2176]{2,1,0:T(8,128)(2,1)S(1)} %collective-permute-done.5.refs_3_), channel_id=1, source_target_pairs={{0,2},{1,3},{2,0},{3,1},{4,6},{5,7},{6,4},{7,5},{8,10},{9,11},{10,... | collective-permute-start | bytes 417800 | tf_op jit(solution)/shard_map/ppermute | solution.py:47
  19.5 2.4 %collective-permute-start.8 = (bf16[1,32,2176]{2,1,0:T(8,128)(2,1)S(1)}, bf16[1,32,2176]{2,1,0:T(8,128)(2,1)S(1)}, u32[]{:S(2)}, u32[]{:S(2)}) collective-permute-start(bf16[1,32,2176]{2,1,0:T(8,128)(2,1)S(1)} %collective-permute-done.4.refs_2_), channel_id=1, source_target_pairs={{0,2},{1,3},{2,0},{3,1},{4,6},{5,7},{6,4},{7,5},{8,10},{9,11},{10,... | collective-permute-start | bytes 417800 | tf_op jit(solution)/shard_map/ppermute | solution.py:47
  19.6 2.3 %collective-permute-start.7 = (bf16[1,32,2176]{2,1,0:T(8,128)(2,1)S(1)}, bf16[1,32,2176]{2,1,0:T(8,128)(2,1)S(1)}, u32[]{:S(2)}, u32[]{:S(2)}) collective-permute-start(bf16[1,32,2176]{2,1,0:T(8,128)(2,1)S(1)} %collective-permute-done.3._.refs_1_), channel_id=1, source_target_pairs={{0,2},{1,3},{2,0},{3,1},{4,6},{5,7},{6,4},{7,5},{8,10},{9,11},{10,... | collective-permute-start | bytes 417800 | tf_op jit(solution)/shard_map/ppermute | solution.py:47
  25.8 1.4 %collective-permute-start.10 = (bf16[1,32,2048]{2,1,0:T(8,128)(2,1)S(1)}, bf16[1,32,2048]{2,1,0:T(8,128)(2,1)S(1)}, u32[]{:S(2)}, u32[]{:S(2)}) collective-permute-start(bf16[1,32,2048]{2,1,0:T(8,128)(2,1)S(1)} %get-tuple-element.35), channel_id=1, source_target_pairs={{0,2},{1,3},{2,0},{3,1},{4,6},{5,7},{6,4},{7,5},{8,10},{9,11},{10,... | collective-permute-start | bytes 393224 | tf_op jit(solution)/shard_map/ppermute | solution.py:47
  25.9 3.8 %collective-permute-start.12 = (bf16[1,32,2048]{2,1,0:T(8,128)(2,1)S(1)}, bf16[1,32,2048]{2,1,0:T(8,128)(2,1)S(1)}, u32[]{:S(2)}, u32[]{:S(2)}) collective-permute-start(bf16[1,32,2048]{2,1,0:T(8,128)(2,1)S(1)} %get-tuple-element.37), channel_id=1, source_target_pairs={{0,2},{1,3},{2,0},{3,1},{4,6},{5,7},{6,4},{7,5},{8,10},{9,11},{10,... | collective-permute-start | bytes 393224 | tf_op jit(solution)/shard_map/ppermute | solution.py:47
  26.3 4.0 %collective-permute-start.14 = (bf16[1,32,2048]{2,1,0:T(8,128)(2,1)S(1)}, bf16[1,32,2048]{2,1,0:T(8,128)(2,1)S(1)}, u32[]{:S(2)}, u32[]{:S(2)}) collective-permute-start(bf16[1,32,2048]{2,1,0:T(8,128)(2,1)S(1)} %get-tuple-element.39), channel_id=1, source_target_pairs={{0,2},{1,3},{2,0},{3,1},{4,6},{5,7},{6,4},{7,5},{8,10},{9,11},{10,... | collective-permute-start | bytes 393224 | tf_op jit(solution)/shard_map/ppermute | solution.py:47
  26.4 7.1 %collective-permute-start.16 = (bf16[1,32,2048]{2,1,0:T(8,128)(2,1)S(1)}, bf16[1,32,2048]{2,1,0:T(8,128)(2,1)S(1)}, u32[]{:S(2)}, u32[]{:S(2)}) collective-permute-start(bf16[1,32,2048]{2,1,0:T(8,128)(2,1)S(1)} %get-tuple-element.41), channel_id=1, source_target_pairs={{0,2},{1,3},{2,0},{3,1},{4,6},{5,7},{6,4},{7,5},{8,10},{9,11},{10,... | collective-permute-start | bytes 393224 | tf_op jit(solution)/shard_map/ppermute | solution.py:47
  27.2 7.3 %collective-permute-start.11 = (bf16[1,32,2048]{2,1,0:T(8,128)(2,1)S(1)}, bf16[1,32,2048]{2,1,0:T(8,128)(2,1)S(1)}, u32[]{:S(2)}, u32[]{:S(2)}) collective-permute-start(bf16[1,32,2048]{2,1,0:T(8,128)(2,1)S(1)} %shard_map.115), channel_id=1, source_target_pairs={{0,5},{1,4},{2,7},{3,6},{4,1},{5,0},{6,3},{7,2},{8,13},{9,12},{10,... | collective-permute-start | bytes 393224 | tf_op jit(solution)/shard_map/ppermute | solution.py:47
  29.7 6.8 %collective-permute-start.13 = (bf16[1,32,2048]{2,1,0:T(8,128)(2,1)S(1)}, bf16[1,32,2048]{2,1,0:T(8,128)(2,1)S(1)}, u32[]{:S(2)}, u32[]{:S(2)}) collective-permute-start(bf16[1,32,2048]{2,1,0:T(8,128)(2,1)S(1)} %shard_map.116), channel_id=1, source_target_pairs={{0,4},{1,5},{2,3},{3,2},{4,0},{5,1},{6,7},{7,6},{8,12},{9,13},{10,... | collective-permute-start | bytes 393224 | tf_op jit(solution)/shard_map/ppermute | solution.py:47
  30.4 6.2 %collective-permute-start.15 = (bf16[1,32,2048]{2,1,0:T(8,128)(2,1)S(1)}, bf16[1,32,2048]{2,1,0:T(8,128)(2,1)S(1)}, u32[]{:S(2)}, u32[]{:S(2)}) collective-permute-start(bf16[1,32,2048]{2,1,0:T(8,128)(2,1)S(1)} %shard_map.117), channel_id=1, source_target_pairs={{0,1},{1,0},{2,6},{3,7},{4,5},{5,4},{6,2},{7,3},{8,9},{9,8},{10,14... | collective-permute-start | bytes 393224 | tf_op jit(solution)/shard_map/ppermute | solution.py:47
  36.7 6.4 %collective-permute-start.17 = (bf16[1,8,2048]{2,1,0:T(8,128)(2,1)S(1)}, bf16[1,8,2048]{2,1,0:T(8,128)(2,1)S(1)}, u32[]{:S(2)}, u32[]{:S(2)}) collective-permute-start(bf16[1,8,2048]{2,1,0:T(8,128)(2,1)S(1)} %get-tuple-element.47), channel_id=1, source_target_pairs={{0,24},{1,25},{2,26},{3,27},{4,28},{5,29},{6,30},{7,31},{8,16},{9,... | collective-permute-start | bytes 98312 | tf_op jit(solution)/shard_map/ppermute | solution.py:47
  38.6 5.2 %collective-permute-start.18 = (bf16[1,8,2048]{2,1,0:T(8,128)(2,1)S(1)}, bf16[1,8,2048]{2,1,0:T(8,128)(2,1)S(1)}, u32[]{:S(2)}, u32[]{:S(2)}) collective-permute-start(bf16[1,8,2048]{2,1,0:T(8,128)(2,1)S(1)} %get-tuple-element.48), channel_id=1, source_target_pairs={{0,16},{1,17},{2,18},{3,19},{4,20},{5,21},{6,22},{7,23},{8,24},{9,... | collective-permute-start | bytes 98312 | tf_op jit(solution)/shard_map/ppermute | solution.py:47
  38.8 4.9 %collective-permute-start.19 = (bf16[1,8,2048]{2,1,0:T(8,128)(2,1)S(1)}, bf16[1,8,2048]{2,1,0:T(8,128)(2,1)S(1)}, u32[]{:S(2)}, u32[]{:S(2)}) collective-permute-start(bf16[1,8,2048]{2,1,0:T(8,128)(2,1)S(1)} %get-tuple-element.49), channel_id=1, source_target_pairs={{0,8},{1,9},{2,10},{3,11},{4,12},{5,13},{6,14},{7,15},{8,0},{9,1},... | collective-permute-start | bytes 98312 | tf_op jit(solution)/shard_map/ppermute | solution.py:47

commit v5 on v3

--- a/solution.py
+++ b/solution.py
@@ -9,7 +9,13 @@
 ROWS = 4
 GROUP = 4
 CHUNK = 8
-VMEM_LIMIT = 16 * 1024 * 1024
+LARGE = 16 * 1024 * 1024
+SMALL = 4 * 1024 * 1024
+GATHER_FIRST = (0, 1, 2)
+GATHER_LAST = (0, 1, 2)
+CORE_ORDER = (3, 2, 1, 0)
+SCATTER_FIRST = (2, 1, 0)
+SCATTER_LAST = (2, 1, 0)
 F32 = jnp.float32
 BF16 = jnp.bfloat16
 
@@ -30,8 +36,8 @@
     return jax.ShapeDtypeStruct(dims, dtype)
 
 
-def params():
-    return pltpu.CompilerParams(vmem_limit_bytes=VMEM_LIMIT)
+def params(limit=SMALL):
+    return pltpu.CompilerParams(vmem_limit_bytes=limit)
 
 
 def cost(flops, moved):
@@ -44,6 +50,15 @@
 
 def exchange(x, masks, total, core):
     return lax.ppermute(x, AXES, [(i, i ^ masks[i // core % 2]) for i in range(total)])
+
+
+def exchange_all(blocks, masks, order, total, core):
+    got = {}
+    for at in order:
+        if at < len(masks):
+            block = blocks[at] if isinstance(blocks, list) else blocks
+            got[at] = exchange(block, masks[at], total, core)
+    return got
 
 
 def stages(total, core):
@@ -95,9 +110,28 @@
     )(*outside(args))
 
 
-def fetch(arrays, after):
-    def body(*refs):
-        n = len(arrays)
+def fetch(w, block):
+    def body(w_ref, b_ref, o_ref, c_ref, sem):
+        copy = pltpu.make_async_copy(w_ref, o_ref, sem)
+        copy.start()
+        c_ref[...] = b_ref[...]
+        copy.wait()
+
+    return pl.pallas_call(
+        body,
+        out_shape=[shape(*w.shape), shape(*block.shape)],
+        in_specs=[hbm(), vmem()],
+        out_specs=[vmem(), vmem()],
+        scratch_shapes=[pltpu.SemaphoreType.DMA],
+        compiler_params=params(),
+        cost_estimate=cost(0, 4 << 20),
+    )(*outside((w,)), block)
+
+
+def fetch_behind(weights, after):
+    n = len(weights)
+
+    def body(*refs):
         copies = [pltpu.make_async_copy(refs[k], refs[n + 1 + k], refs[-1].at[k]) for k in range(n)]
         for c in copies:
             c.start()
@@ -106,20 +140,20 @@
 
     return pl.pallas_call(
         body,
-        out_shape=[shape(*a.shape, dtype=a.dtype) for a in arrays],
-        in_specs=[hbm() for _ in arrays] + [pl.BlockSpec(memory_space=pl.ANY)],
-        out_specs=[vmem() for _ in arrays],
-        scratch_shapes=[pltpu.SemaphoreType.DMA((len(arrays),))],
-        compiler_params=params(),
-        cost_estimate=cost(0, 12 << 20),
-    )(*outside(arrays), after)
-
-
-def regroup(blocks):
+        out_shape=[shape(*w.shape) for w in weights],
+        in_specs=[hbm() for _ in weights] + [pl.BlockSpec(memory_space=pl.ANY)],
+        out_specs=[vmem() for _ in weights],
+        scratch_shapes=[pltpu.SemaphoreType.DMA((n,))],
+        compiler_params=params(),
+        cost_estimate=cost(0, 8 << 20),
+    )(*outside(weights), after)
+
+
+def regroup(blocks, places):
     _, rows, width = blocks[0].shape
 
     def body(*refs):
-        x = [r[0].astype(F32) for r in refs[:-1]]
+        x = [refs[places.index(at)][0].astype(F32) for at in range(len(blocks))]
         low = lax.broadcasted_iota(jnp.int32, (rows, 1), 0) < ROWS
         pairs = list(zip(x[::2], x[1::2]))
         token = [jnp.where(low, a, pltpu.roll(b, ROWS, 0)) for a, b in pairs]
@@ -169,8 +203,8 @@
         dupper = (dact * swish).astype(BF16)
         h_ref[...], dg_ref[...], du_ref[...] = hidden, dgate, dupper
         part = (coef * dot(hidden, wd_ref[...])).astype(BF16).reshape(blocks, half, width)
-        back = dot(dgate, wg_ref[...], 1, 1) + dot(dupper, wu_ref[...], 1, 1)
-        back = back.astype(BF16).reshape(blocks, half, width)
+        back = dot(wg_ref[...], dgate, 1, 1) + dot(wu_ref[...], dupper, 1, 1)
+        back = back.astype(BF16).T.reshape(blocks, half, width)
         at = 0
         for ref, n in zip(parts, splits):
             ref[:, :half] = part[at : at + n]
@@ -184,7 +218,7 @@
         out_shape=outs,
         in_specs=[vmem()] * count + [pl.BlockSpec(memory_space=pltpu.SMEM)] + [vmem()] * 3,
         out_specs=[vmem() for _ in outs],
-        compiler_params=params(),
+        compiler_params=params(LARGE),
         cost_estimate=cost(12 * m * width * hid, 10 << 20),
     )(*pieces, me, w_gate, w_up, w_down)
     return list(got[: len(splits)]), got[len(splits) :]
@@ -206,7 +240,7 @@
         out_shape=[shape(rows, cols) for _ in rights],
         in_specs=[pl.BlockSpec((m, tile), lambda i: (0, i))] + [pl.BlockSpec((m, cols), lambda i: (0, 0)) for _ in rights],
         out_specs=[pl.BlockSpec((tile, cols), lambda i: (i, 0)) for _ in rights],
-        compiler_params=params(),
+        compiler_params=params(LARGE),
         cost_estimate=cost(2 * m * rows * cols * len(rights), 2 * rows * cols * len(rights)),
     )(left, *rights)
 
@@ -301,12 +335,14 @@
     wg, wu, wd = w_gate[0], w_up[0], w_down[0]
 
     block = pack(tokens, route_ids, route_weights, grad_out, experts)
-    block = regroup([block] + [exchange(block, mask, total, core) for mask in plan[0]])
+    got = exchange_all(block, plan[0], GATHER_FIRST, total, core)
+    block = regroup([block, *got.values()], [0] + [at + 1 for at in got])
     for masks in plan[1:]:
-        held = [block] + [exchange(block, mask, total, core) for mask in masks]
+        got = exchange_all(block, masks, GATHER_LAST, total, core)
+        held = [block] + [got[at] for at in range(len(masks))]
         block = jnp.concatenate(held, axis=0)
-    wg, wu, wd = fetch((wg, wu, wd), held[0])
-    own, wg, wu, wd = lax.optimization_barrier((held[0], wg, wu, wd))
+    wg, own = fetch(wg, held[0])
+    wu, wd = fetch_behind((wu, wd), held[1])
     pieces = held + [exchange(h, (core, core), total, core) for h in [own] + held[1:]]
 
     ways = len(held)
@@ -330,16 +366,16 @@
     (down_grad,) = weight_grads(hidden, [dout], 2)
 
     keep, send = parts[:ways], parts[ways:]
-    arrived = [exchange(p, (core, core), total, core) for p in send]
-    terms = [keep[0], arrived[0]]
-    for at, mask in enumerate(plan[-1]):
-        terms.append(exchange(add_pair(keep[at + 1], arrived[at + 1]), mask, total, core))
+    arrived = [exchange(send[at], (core, core), total, core) for at in CORE_ORDER if at < ways]
+    arrived = dict(zip([at for at in CORE_ORDER if at < ways], arrived))
+    sums = [add_pair(keep[at], arrived[at]) for at in range(1, ways)]
+    terms = [*exchange_all(sums, plan[-1], SCATTER_FIRST, total, core).values(), keep[0], arrived[0]]
     for masks in reversed(plan[1:-1]):
         ways = len(masks) + 1
         mine, *others = add(terms, [terms[0].shape[0] // ways] * ways)
-        terms = [mine] + [exchange(o, mask, total, core) for o, mask in zip(others, masks)]
+        terms = [mine, *exchange_all(others, masks, SCATTER_FIRST, total, core).values()]
     mine, *others = add_ungroup(terms, (gate_grad,))
-    terms = [mine] + [exchange(o, mask, total, core) for o, mask in zip(others, plan[0])]
+    terms = [mine, *exchange_all(others, plan[0], SCATTER_LAST, total, core).values()]
     mixed, back = finish(terms, (down_grad,))
     return mixed, back, gate_grad[None], up_grad[None], down_grad[None]
 

time: 49.4 us -> 44.3 us (0.90)
  local copies, waits for them, and re-layouts: 5.81 us -> 0 us
  Pallas kernels: 12.3 us -> 13.1 us
  starting transfers between devices: 19.5 us -> 19 us
  waiting for transfers between devices: 10.6 us -> 11.1 us
    unnamed x8 -> x0, local copies, waits for them, and re-layouts: 5.81 us -> none
    pallas_call x1 -> x2, Pallas kernels: 2.88 us -> 3.84 us  [the longest x1 2.24 us: fetch_behind(): pl.pallas_call(body, out_shape=[shape(*w.shape) for w in weights], in_spe...]
    ppermute x20, starting transfers between devices: 19.5 us -> 19 us  [exchange(): lax.ppermute(x, AXES, [(i, i ^ masks[i // core % 2]) for i in range(total)])]
  transfers between devices with their start and end apart: 20 -> 20, of which waited for: 10 -> 9; matrix products, arithmetic and copies ran while one was open for 0% -> 0% of each run, Pallas kernels for 15% -> 19%
where the time goes in v5:
time: 44.3 us; the launch traced here: 43.9 us
  starting transfers between devices  19 us (43%)
  Pallas kernels  13.1 us (30%)
  waiting for transfers between devices  11.1 us (25%)
  between operations  0.74 us (2%)
    ppermute x20, starting transfers between devices, exchange(): lax.ppermute(x, AXES, [(i, i ^ masks[i // core % 2]) for i in range(total)])  19 us
    ppermute x20, waiting for transfers between devices, exchange(): lax.ppermute(x, AXES, [(i, i ^ masks[i // core % 2]) for i in range(total)])  11.1 us
    pallas_call x2, Pallas kernels, weight_grads(): pl.pallas_call(body, grid=(steps,), out_shape=[shape(rows, cols) for _ in...  4.49 us
    pallas_call x1, Pallas kernels, expert_math(): pl.pallas_call(body, out_shape=outs, in_specs=[vmem()] * count + [pl.Bloc...  2.97 us
    pallas_call x1, Pallas kernels, fetch_behind(): pl.pallas_call(body, out_shape=[shape(*w.shape) for w in weights], in_spe...  2.24 us
    pallas_call x1, Pallas kernels, fetch(): pl.pallas_call(body, out_shape=[shape(*w.shape), shape(*block.shape)], in...  1.6 us
    pallas_call x1, Pallas kernels, pack(): pl.pallas_call(body, out_shape=shape(1, 2 * rows, width + lanes), in_spec...  0.92 us
  transfers between devices with their start and end apart: 20, of which 9 were waited for; matrix products, arithmetic and copies ran while one was open for 0% of the time, Pallas kernels for 19%

profile of v5, /device:TPU:0, one launch (start us, length us, event | category | flops | bytes accessed | tf_op | source)
XLA Modules:
  0.0 43.9 jit_solution(2390695682662241160)
XLA Ops:
  0.6 0.9 %shard_map.110.refs_0_ = bf16[1,8,2176]{2,1,0:T(8,128)(2,1)S(1)} custom-call(bf16[4,2048]{1,0:T(4,128)(2,1)} %t_in.1, s32[4,8]{1,0:T(4,128)} %i_in.1, s32[4,8]{1,0:T(4,128)} %w_in.1, bf16[4,2048]{1,0:T(4,128)(2,1)} %g_in.1), custom_call_target="tpu_custom_call" | custom-call | bytes 81920 | tf_op jit(solution)/shard_map/pallas_call | solution.py:102
  1.6 5.1 %collective-permute-start.2 = (bf16[1,8,2176]{2,1,0:T(8,128)(2,1)S(1)}, bf16[1,8,2176]{2,1,0:T(8,128)(2,1)S(1)}, u32[]{:S(2)}, u32[]{:S(2)}) collective-permute-start(bf16[1,8,2176]{2,1,0:T(8,128)(2,1)S(1)} %shard_map.110.refs_0_), channel_id=1, source_target_pairs={{0,24},{1,25},{2,26},{3,27},{4,28},{5,29},{6,30},{7,31},{8,16},{9,... | collective-permute-start | bytes 104456 | tf_op jit(solution)/shard_map/ppermute | solution.py:52
  6.7 0.0 collective-permute-start.1
  6.7 0.6 %collective-permute-start = (bf16[1,8,2176]{2,1,0:T(8,128)(2,1)S(1)}, bf16[1,8,2176]{2,1,0:T(8,128)(2,1)S(1)}, u32[]{:S(2)}, u32[]{:S(2)}) collective-permute-start(bf16[1,8,2176]{2,1,0:T(8,128)(2,1)S(1)} %shard_map.110.refs_0_), channel_id=1, source_target_pairs={{0,8},{1,9},{2,10},{3,11},{4,12},{5,13},{6,14},{7,15},{8,0},{9,1},... | collective-permute-start | bytes 104456 | tf_op jit(solution)/shard_map/ppermute | solution.py:52
  7.3 1.3 %collective-permute-done.2.refs_3_ = bf16[1,8,2176]{2,1,0:T(8,128)(2,1)S(1)} collective-permute-done((bf16[1,8,2176]{2,1,0:T(8,128)(2,1)S(1)}, bf16[1,8,2176]{2,1,0:T(8,128)(2,1)S(1)}, u32[]{:S(2)}, u32[]{:S(2)}) %collective-permute-start.2) | collective-permute-done | bytes 34848 | tf_op jit(solution)/shard_map/ppermute | solution.py:52
  8.6 2.9 %collective-permute-done.1.refs_2_ = bf16[1,8,2176]{2,1,0:T(8,128)(2,1)S(1)} collective-permute-done((bf16[1,8,2176]{2,1,0:T(8,128)(2,1)S(1)}, bf16[1,8,2176]{2,1,0:T(8,128)(2,1)S(1)}, u32[]{:S(2)}, u32[]{:S(2)}) %collective-permute-start.1) | collective-permute-done | bytes 34848 | tf_op jit(solution)/shard_map/ppermute | solution.py:52
  11.5 0.0 collective-permute-done.refs_1_
  11.6 2.5 %collective-permute-start.5 = (bf16[1,32,2176]{2,1,0:T(8,128)(2,1)S(1)}, bf16[1,32,2176]{2,1,0:T(8,128)(2,1)S(1)}, u32[]{:S(2)}, u32[]{:S(2)}) collective-permute-start(bf16[1,32,2176]{2,1,0:T(8,128)(2,1)S(1)} %shard_map.111.b_ref.refs_0_), channel_id=1, source_target_pairs={{0,5},{1,4},{2,7},{3,6},{4,1},{5,0},{6,3},{7,2},{8,13},{9,12},{10,... | collective-permute-start | bytes 417800 | tf_op jit(solution)/shard_map/ppermute | solution.py:52
  14.1 0.5 %collective-permute-start.4 = (bf16[1,32,2176]{2,1,0:T(8,128)(2,1)S(1)}, bf16[1,32,2176]{2,1,0:T(8,128)(2,1)S(1)}, u32[]{:S(2)}, u32[]{:S(2)}) collective-permute-start(bf16[1,32,2176]{2,1,0:T(8,128)(2,1)S(1)} %shard_map.111.b_ref.refs_0_), channel_id=1, source_target_pairs={{0,4},{1,5},{2,3},{3,2},{4,0},{5,1},{6,7},{7,6},{8,12},{9,13},{10,... | collective-permute-start | bytes 417800 | tf_op jit(solution)/shard_map/ppermute | solution.py:52
  14.6 0.5 %collective-permute-start.3 = (bf16[1,32,2176]{2,1,0:T(8,128)(2,1)S(1)}, bf16[1,32,2176]{2,1,0:T(8,128)(2,1)S(1)}, u32[]{:S(2)}, u32[]{:S(2)}) collective-permute-start(bf16[1,32,2176]{2,1,0:T(8,128)(2,1)S(1)} %shard_map.111.b_ref.refs_0_), channel_id=1, source_target_pairs={{0,1},{1,0},{2,6},{3,7},{4,5},{5,4},{6,2},{7,3},{8,9},{9,8},{10,14... | collective-permute-start | bytes 417800 | tf_op jit(solution)/shard_map/ppermute | solution.py:52
  15.1 1.6 %shard_map.112 = (bf16[2048,512]{1,0:T(8,128)(2,1)S(1)}, bf16[1,32,2176]{2,1,0:T(8,128)(2,1)S(1)}) custom-call(bf16[2048,512]{1,0:T(8,128)(2,1)} %bitcast.8, bf16[1,32,2176]{2,1,0:T(8,128)(2,1)S(1)} %shard_map.111.b_ref.refs_0_), custom_call_target="tpu_custom_call" | custom-call | bytes 4194304 | tf_op jit(solution)/shard_map/pallas_call | solution.py:120
  16.7 0.1 collective-permute-start.6
  16.8 1.3 %collective-permute-done.5.refs_3_ = bf16[1,32,2176]{2,1,0:T(8,128)(2,1)S(1)} collective-permute-done((bf16[1,32,2176]{2,1,0:T(8,128)(2,1)S(1)}, bf16[1,32,2176]{2,1,0:T(8,128)(2,1)S(1)}, u32[]{:S(2)}, u32[]{:S(2)}) %collective-permute-start.5) | collective-permute-done | bytes 139296 | tf_op jit(solution)/shard_map/ppermute | solution.py:52
  18.1 0.0 collective-permute-start.9
  18.1 1.4 %collective-permute-done.4.refs_2_ = bf16[1,32,2176]{2,1,0:T(8,128)(2,1)S(1)} collective-permute-done((bf16[1,32,2176]{2,1,0:T(8,128)(2,1)S(1)}, bf16[1,32,2176]{2,1,0:T(8,128)(2,1)S(1)}, u32[]{:S(2)}, u32[]{:S(2)}) %collective-permute-start.4) | collective-permute-done | bytes 139296 | tf_op jit(solution)/shard_map/ppermute | solution.py:52
  19.5 0.0 collective-permute-start.8
  19.5 0.1 collective-permute-done.3.refs_2_.refs_1_
  19.6 0.4 collective-permute-start.7
  20.0 2.2 %shard_map.113 = (bf16[2048,512]{1,0:T(8,128)(2,1)S(1)}, bf16[512,2048]{1,0:T(8,128)(2,1)S(1)}) custom-call(bf16[2048,512]{1,0:T(8,128)(2,1)} %bitcast.9, bf16[512,2048]{1,0:T(8,128)(2,1)} %bitcast.10, bf16[1,32,2176]{2,1,0:T(8,128)(2,1)S(1)} %collective-permute-done.3.refs_2_.refs_1_), custom_call_target="tpu_custom_call" | custom-call | bytes 8388608 | tf_op jit(solution)/shard_map/pallas_call | solution.py:141
  22.3 0.0 collective-permute-done.6.refs_4_
  22.3 0.0 collective-permute-done.9.refs_7_
  22.3 0.0 collective-permute-done.8.refs_6_
  22.3 0.0 collective-permute-done.7.refs_5_
  22.3 3.0 %shard_map.114 = (bf16[1,32,2048]{2,1,0:T(8,128)(2,1)S(1)}, bf16[1,32,2048]{2,1,0:T(8,128)(2,1)S(1)}, bf16[1,32,2048]{2,1,0:T(8,128)(2,1)S(1)}, bf16[1,32,2048]{...) custom-call(bf16[1,32,2176]{2,1,0:T(8,128)(2,1)S(1)} %shard_map.111., ...), custom_call_target="tpu_custom_call" | custom-call | flops 1610612736 | bytes 10485760 | tf_op jit(solution)/shard_map/pallas_call | solution.py:216
  25.3 0.2 collective-permute-start.10
  25.5 0.4 collective-permute-start.12
  25.9 0.1 collective-permute-start.14
  26.0 0.4 collective-permute-start.16
  26.4 0.3 collective-permute-done.10.b_ref
  26.8 2.5 %collective-permute-start.11 = (bf16[1,32,2048]{2,1,0:T(8,128)(2,1)S(1)}, bf16[1,32,2048]{2,1,0:T(8,128)(2,1)S(1)}, u32[]{:S(2)}, u32[]{:S(2)}) collective-permute-start(bf16[1,32,2048]{2,1,0:T(8,128)(2,1)S(1)} %shard_map.115), channel_id=1, source_target_pairs={{0,5},{1,4},{2,7},{3,6},{4,1},{5,0},{6,3},{7,2},{8,13},{9,12},{10,... | collective-permute-start | bytes 393224 | tf_op jit(solution)/shard_map/ppermute | solution.py:52
  29.2 0.0 collective-permute-done.12.b_ref
  29.3 0.6 %collective-permute-start.13 = (bf16[1,32,2048]{2,1,0:T(8,128)(2,1)S(1)}, bf16[1,32,2048]{2,1,0:T(8,128)(2,1)S(1)}, u32[]{:S(2)}, u32[]{:S(2)}) collective-permute-start(bf16[1,32,2048]{2,1,0:T(8,128)(2,1)S(1)} %shard_map.116), channel_id=1, source_target_pairs={{0,4},{1,5},{2,3},{3,2},{4,0},{5,1},{6,7},{7,6},{8,12},{9,13},{10,... | collective-permute-start | bytes 393224 | tf_op jit(solution)/shard_map/ppermute | solution.py:52
  29.9 0.0 collective-permute-done.14.b_ref
  29.9 0.6 %collective-permute-start.15 = (bf16[1,32,2048]{2,1,0:T(8,128)(2,1)S(1)}, bf16[1,32,2048]{2,1,0:T(8,128)(2,1)S(1)}, u32[]{:S(2)}, u32[]{:S(2)}) collective-permute-start(bf16[1,32,2048]{2,1,0:T(8,128)(2,1)S(1)} %shard_map.117), channel_id=1, source_target_pairs={{0,1},{1,0},{2,6},{3,7},{4,5},{5,4},{6,2},{7,3},{8,9},{9,8},{10,14... | collective-permute-start | bytes 393224 | tf_op jit(solution)/shard_map/ppermute | solution.py:52
  30.5 2.6 %shard_map.118 = (bf16[2048,512]{1,0:T(8,128)(2,1)}, bf16[2048,512]{1,0:T(8,128)(2,1)}) custom-call(bf16[128,2048]{1,0:T(8,128)(2,1)S(1)} %get-tuple-element.42.l_ref, bf16[128,512]{1,0:T(8,128)(2,1)S(1)} %get-tuple-element.43.refs_0_, bf16[128,512]{1,0:T(8,128)(2,1)S(1)} %get-tuple-element.44.refs_1_), custom_call_target="tpu_custom_call" | custom-call | flops 536870912 | bytes 4194304 | tf_op jit(solution)/shard_map/pallas_call | solution.py:237
  33.1 0.0 collective-permute-done.16.refs_4_
  33.1 1.0 %collective-permute-done.11.refs_0_ = bf16[1,32,2048]{2,1,0:T(8,128)(2,1)S(1)} collective-permute-done((bf16[1,32,2048]{2,1,0:T(8,128)(2,1)S(1)}, bf16[1,32,2048]{2,1,0:T(8,128)(2,1)S(1)}, u32[]{:S(2)}, u32[]{:S(2)}) %collective-permute-start.11) | collective-permute-done | bytes 131104 | tf_op jit(solution)/shard_map/ppermute | solution.py:52
  34.1 2.0 %collective-permute-done.13.refs_1_ = bf16[1,32,2048]{2,1,0:T(8,128)(2,1)S(1)} collective-permute-done((bf16[1,32,2048]{2,1,0:T(8,128)(2,1)S(1)}, bf16[1,32,2048]{2,1,0:T(8,128)(2,1)S(1)}, u32[]{:S(2)}, u32[]{:S(2)}) %collective-permute-start.13) | collective-permute-done | bytes 131104 | tf_op jit(solution)/shard_map/ppermute | solution.py:52
  36.1 0.0 collective-permute-done.15.refs_2_
  36.1 0.1 shard_map.119
  36.2 1.9 %collective-permute-start.17 = (bf16[1,8,2048]{2,1,0:T(8,128)(2,1)S(1)}, bf16[1,8,2048]{2,1,0:T(8,128)(2,1)S(1)}, u32[]{:S(2)}, u32[]{:S(2)}) collective-permute-start(bf16[1,8,2048]{2,1,0:T(8,128)(2,1)S(1)} %get-tuple-element.47), channel_id=1, source_target_pairs={{0,24},{1,25},{2,26},{3,27},{4,28},{5,29},{6,30},{7,31},{8,16},{9,... | collective-permute-start | bytes 98312 | tf_op jit(solution)/shard_map/ppermute | solution.py:52
  38.1 0.3 collective-permute-start.18
  38.4 2.3 %collective-permute-start.19 = (bf16[1,8,2048]{2,1,0:T(8,128)(2,1)S(1)}, bf16[1,8,2048]{2,1,0:T(8,128)(2,1)S(1)}, u32[]{:S(2)}, u32[]{:S(2)}) collective-permute-start(bf16[1,8,2048]{2,1,0:T(8,128)(2,1)S(1)} %get-tuple-element.49), channel_id=1, source_target_pairs={{0,8},{1,9},{2,10},{3,11},{4,12},{5,13},{6,14},{7,15},{8,0},{9,1},... | collective-permute-start | bytes 98312 | tf_op jit(solution)/shard_map/ppermute | solution.py:52
  40.7 1.9 %shard_map.120.refs_4_ = bf16[512,2048]{1,0:T(8,128)(2,1)} custom-call(bf16[128,512]{1,0:T(8,128)(2,1)S(1)} %get-tuple-element.50.l_ref, bf16[128,2048]{1,0:T(8,128)(2,1)S(1)} %get-tuple-element.51.refs_0_), custom_call_target="tpu_custom_call" | custom-call | flops 268435456 | bytes 2097152 | tf_op jit(solution)/shard_map/pallas_call | solution.py:237
  42.6 0.0 collective-permute-done.17.refs_1_
  42.6 0.7 %collective-permute-done.18.refs_2_ = bf16[1,8,2048]{2,1,0:T(8,128)(2,1)S(1)} collective-permute-done((bf16[1,8,2048]{2,1,0:T(8,128)(2,1)S(1)}, bf16[1,8,2048]{2,1,0:T(8,128)(2,1)S(1)}, u32[]{:S(2)}, u32[]{:S(2)}) %collective-permute-start.18) | collective-permute-done | bytes 32800 | tf_op jit(solution)/shard_map/ppermute | solution.py:52
  43.3 0.0 collective-permute-done.19.refs_3_
  43.3 0.6 %shard_map.121 = (bf16[4,2048]{1,0:T(4,128)(2,1)}, bf16[4,2048]{1,0:T(4,128)(2,1)}) custom-call(f32[1,8,2048]{2,1,0:T(8,128)S(1)} %get-tuple-element.46.refs_0_, bf16[1,8,2048]{2,1,0:T(8,128)(2,1)S(1)} %collective-permute-done.17.refs_1_, bf16[1,8,2048]{2,1,0:T(8,128)(2,1)S(1)} %collective-permute-done.18.refs_2_, ...), custom_call_target="tpu_custom_call" | custom-call | bytes 65536 | tf_op jit(solution)/shard_map/pallas_call | solution.py:319
  (4 shorter events, 0.1 us)
Async XLA Ops:
  1.6 7.0 %collective-permute-start.2 = (bf16[1,8,2176]{2,1,0:T(8,128)(2,1)S(1)}, bf16[1,8,2176]{2,1,0:T(8,128)(2,1)S(1)}, u32[]{:S(2)}, u32[]{:S(2)}) collective-permute-start(bf16[1,8,2176]{2,1,0:T(8,128)(2,1)S(1)} %shard_map.110.refs_0_), channel_id=1, source_target_pairs={{0,24},{1,25},{2,26},{3,27},{4,28},{5,29},{6,30},{7,31},{8,16},{9,... | collective-permute-start | bytes 104456 | tf_op jit(solution)/shard_map/ppermute | solution.py:52
  6.7 4.8 %collective-permute-start.1 = (bf16[1,8,2176]{2,1,0:T(8,128)(2,1)S(1)}, bf16[1,8,2176]{2,1,0:T(8,128)(2,1)S(1)}, u32[]{:S(2)}, u32[]{:S(2)}) collective-permute-start(bf16[1,8,2176]{2,1,0:T(8,128)(2,1)S(1)} %shard_map.110.refs_0_), channel_id=1, source_target_pairs={{0,16},{1,17},{2,18},{3,19},{4,20},{5,21},{6,22},{7,23},{8,24},{9,... | collective-permute-start | bytes 104456 | tf_op jit(solution)/shard_map/ppermute | solution.py:52
  6.7 4.8 %collective-permute-start = (bf16[1,8,2176]{2,1,0:T(8,128)(2,1)S(1)}, bf16[1,8,2176]{2,1,0:T(8,128)(2,1)S(1)}, u32[]{:S(2)}, u32[]{:S(2)}) collective-permute-start(bf16[1,8,2176]{2,1,0:T(8,128)(2,1)S(1)} %shard_map.110.refs_0_), channel_id=1, source_target_pairs={{0,8},{1,9},{2,10},{3,11},{4,12},{5,13},{6,14},{7,15},{8,0},{9,1},... | collective-permute-start | bytes 104456 | tf_op jit(solution)/shard_map/ppermute | solution.py:52
  11.6 6.5 %collective-permute-start.5 = (bf16[1,32,2176]{2,1,0:T(8,128)(2,1)S(1)}, bf16[1,32,2176]{2,1,0:T(8,128)(2,1)S(1)}, u32[]{:S(2)}, u32[]{:S(2)}) collective-permute-start(bf16[1,32,2176]{2,1,0:T(8,128)(2,1)S(1)} %shard_map.111.b_ref.refs_0_), channel_id=1, source_target_pairs={{0,5},{1,4},{2,7},{3,6},{4,1},{5,0},{6,3},{7,2},{8,13},{9,12},{10,... | collective-permute-start | bytes 417800 | tf_op jit(solution)/shard_map/ppermute | solution.py:52
  14.1 5.5 %collective-permute-start.4 = (bf16[1,32,2176]{2,1,0:T(8,128)(2,1)S(1)}, bf16[1,32,2176]{2,1,0:T(8,128)(2,1)S(1)}, u32[]{:S(2)}, u32[]{:S(2)}) collective-permute-start(bf16[1,32,2176]{2,1,0:T(8,128)(2,1)S(1)} %shard_map.111.b_ref.refs_0_), channel_id=1, source_target_pairs={{0,4},{1,5},{2,3},{3,2},{4,0},{5,1},{6,7},{7,6},{8,12},{9,13},{10,... | collective-permute-start | bytes 417800 | tf_op jit(solution)/shard_map/ppermute | solution.py:52
  14.6 5.1 %collective-permute-start.3 = (bf16[1,32,2176]{2,1,0:T(8,128)(2,1)S(1)}, bf16[1,32,2176]{2,1,0:T(8,128)(2,1)S(1)}, u32[]{:S(2)}, u32[]{:S(2)}) collective-permute-start(bf16[1,32,2176]{2,1,0:T(8,128)(2,1)S(1)} %shard_map.111.b_ref.refs_0_), channel_id=1, source_target_pairs={{0,1},{1,0},{2,6},{3,7},{4,5},{5,4},{6,2},{7,3},{8,9},{9,8},{10,14... | collective-permute-start | bytes 417800 | tf_op jit(solution)/shard_map/ppermute | solution.py:52
  16.7 5.6 %collective-permute-start.6 = (bf16[1,32,2176]{2,1,0:T(8,128)(2,1)S(1)}, bf16[1,32,2176]{2,1,0:T(8,128)(2,1)S(1)}, u32[]{:S(2)}, u32[]{:S(2)}) collective-permute-start(bf16[1,32,2176]{2,1,0:T(8,128)(2,1)S(1)} %get-tuple-element.30), channel_id=1, source_target_pairs={{0,2},{1,3},{2,0},{3,1},{4,6},{5,7},{6,4},{7,5},{8,10},{9,11},{10,... | collective-permute-start | bytes 417800 | tf_op jit(solution)/shard_map/ppermute | solution.py:52
  18.1 4.2 %collective-permute-start.9 = (bf16[1,32,2176]{2,1,0:T(8,128)(2,1)S(1)}, bf16[1,32,2176]{2,1,0:T(8,128)(2,1)S(1)}, u32[]{:S(2)}, u32[]{:S(2)}) collective-permute-start(bf16[1,32,2176]{2,1,0:T(8,128)(2,1)S(1)} %collective-permute-done.5.refs_3_), channel_id=1, source_target_pairs={{0,2},{1,3},{2,0},{3,1},{4,6},{5,7},{6,4},{7,5},{8,10},{9,11},{10,... | collective-permute-start | bytes 417800 | tf_op jit(solution)/shard_map/ppermute | solution.py:52
  19.5 2.8 %collective-permute-start.8 = (bf16[1,32,2176]{2,1,0:T(8,128)(2,1)S(1)}, bf16[1,32,2176]{2,1,0:T(8,128)(2,1)S(1)}, u32[]{:S(2)}, u32[]{:S(2)}) collective-permute-start(bf16[1,32,2176]{2,1,0:T(8,128)(2,1)S(1)} %collective-permute-done.4.refs_2_), channel_id=1, source_target_pairs={{0,2},{1,3},{2,0},{3,1},{4,6},{5,7},{6,4},{7,5},{8,10},{9,11},{10,... | collective-permute-start | bytes 417800 | tf_op jit(solution)/shard_map/ppermute | solution.py:52
  19.6 2.7 %collective-permute-start.7 = (bf16[1,32,2176]{2,1,0:T(8,128)(2,1)S(1)}, bf16[1,32,2176]{2,1,0:T(8,128)(2,1)S(1)}, u32[]{:S(2)}, u32[]{:S(2)}) collective-permute-start(bf16[1,32,2176]{2,1,0:T(8,128)(2,1)S(1)} %collective-permute-done.3.refs_2_.refs_1_), channel_id=1, source_target_pairs={{0,2},{1,3},{2,0},{3,1},{4,6},{5,7},{6,4},{7,5},{8,10},{9,11},{10,... | collective-permute-start | bytes 417800 | tf_op jit(solution)/shard_map/ppermute | solution.py:52
  25.3 1.4 %collective-permute-start.10 = (bf16[1,32,2048]{2,1,0:T(8,128)(2,1)S(1)}, bf16[1,32,2048]{2,1,0:T(8,128)(2,1)S(1)}, u32[]{:S(2)}, u32[]{:S(2)}) collective-permute-start(bf16[1,32,2048]{2,1,0:T(8,128)(2,1)S(1)} %get-tuple-element.35), channel_id=1, source_target_pairs={{0,2},{1,3},{2,0},{3,1},{4,6},{5,7},{6,4},{7,5},{8,10},{9,11},{10,... | collective-permute-start | bytes 393224 | tf_op jit(solution)/shard_map/ppermute | solution.py:52
  25.5 3.7 %collective-permute-start.12 = (bf16[1,32,2048]{2,1,0:T(8,128)(2,1)S(1)}, bf16[1,32,2048]{2,1,0:T(8,128)(2,1)S(1)}, u32[]{:S(2)}, u32[]{:S(2)}) collective-permute-start(bf16[1,32,2048]{2,1,0:T(8,128)(2,1)S(1)} %get-tuple-element.37), channel_id=1, source_target_pairs={{0,2},{1,3},{2,0},{3,1},{4,6},{5,7},{6,4},{7,5},{8,10},{9,11},{10,... | collective-permute-start | bytes 393224 | tf_op jit(solution)/shard_map/ppermute | solution.py:52
  25.9 4.0 %collective-permute-start.14 = (bf16[1,32,2048]{2,1,0:T(8,128)(2,1)S(1)}, bf16[1,32,2048]{2,1,0:T(8,128)(2,1)S(1)}, u32[]{:S(2)}, u32[]{:S(2)}) collective-permute-start(bf16[1,32,2048]{2,1,0:T(8,128)(2,1)S(1)} %get-tuple-element.39), channel_id=1, source_target_pairs={{0,2},{1,3},{2,0},{3,1},{4,6},{5,7},{6,4},{7,5},{8,10},{9,11},{10,... | collective-permute-start | bytes 393224 | tf_op jit(solution)/shard_map/ppermute | solution.py:52
  26.0 7.1 %collective-permute-start.16 = (bf16[1,32,2048]{2,1,0:T(8,128)(2,1)S(1)}, bf16[1,32,2048]{2,1,0:T(8,128)(2,1)S(1)}, u32[]{:S(2)}, u32[]{:S(2)}) collective-permute-start(bf16[1,32,2048]{2,1,0:T(8,128)(2,1)S(1)} %get-tuple-element.41), channel_id=1, source_target_pairs={{0,2},{1,3},{2,0},{3,1},{4,6},{5,7},{6,4},{7,5},{8,10},{9,11},{10,... | collective-permute-start | bytes 393224 | tf_op jit(solution)/shard_map/ppermute | solution.py:52
  26.8 7.3 %collective-permute-start.11 = (bf16[1,32,2048]{2,1,0:T(8,128)(2,1)S(1)}, bf16[1,32,2048]{2,1,0:T(8,128)(2,1)S(1)}, u32[]{:S(2)}, u32[]{:S(2)}) collective-permute-start(bf16[1,32,2048]{2,1,0:T(8,128)(2,1)S(1)} %shard_map.115), channel_id=1, source_target_pairs={{0,5},{1,4},{2,7},{3,6},{4,1},{5,0},{6,3},{7,2},{8,13},{9,12},{10,... | collective-permute-start | bytes 393224 | tf_op jit(solution)/shard_map/ppermute | solution.py:52
  29.3 6.8 %collective-permute-start.13 = (bf16[1,32,2048]{2,1,0:T(8,128)(2,1)S(1)}, bf16[1,32,2048]{2,1,0:T(8,128)(2,1)S(1)}, u32[]{:S(2)}, u32[]{:S(2)}) collective-permute-start(bf16[1,32,2048]{2,1,0:T(8,128)(2,1)S(1)} %shard_map.116), channel_id=1, source_target_pairs={{0,4},{1,5},{2,3},{3,2},{4,0},{5,1},{6,7},{7,6},{8,12},{9,13},{10,... | collective-permute-start | bytes 393224 | tf_op jit(solution)/shard_map/ppermute | solution.py:52
  29.9 6.2 %collective-permute-start.15 = (bf16[1,32,2048]{2,1,0:T(8,128)(2,1)S(1)}, bf16[1,32,2048]{2,1,0:T(8,128)(2,1)S(1)}, u32[]{:S(2)}, u32[]{:S(2)}) collective-permute-start(bf16[1,32,2048]{2,1,0:T(8,128)(2,1)S(1)} %shard_map.117), channel_id=1, source_target_pairs={{0,1},{1,0},{2,6},{3,7},{4,5},{5,4},{6,2},{7,3},{8,9},{9,8},{10,14... | collective-permute-start | bytes 393224 | tf_op jit(solution)/shard_map/ppermute | solution.py:52
  36.2 6.4 %collective-permute-start.17 = (bf16[1,8,2048]{2,1,0:T(8,128)(2,1)S(1)}, bf16[1,8,2048]{2,1,0:T(8,128)(2,1)S(1)}, u32[]{:S(2)}, u32[]{:S(2)}) collective-permute-start(bf16[1,8,2048]{2,1,0:T(8,128)(2,1)S(1)} %get-tuple-element.47), channel_id=1, source_target_pairs={{0,24},{1,25},{2,26},{3,27},{4,28},{5,29},{6,30},{7,31},{8,16},{9,... | collective-permute-start | bytes 98312 | tf_op jit(solution)/shard_map/ppermute | solution.py:52
  38.1 5.2 %collective-permute-start.18 = (bf16[1,8,2048]{2,1,0:T(8,128)(2,1)S(1)}, bf16[1,8,2048]{2,1,0:T(8,128)(2,1)S(1)}, u32[]{:S(2)}, u32[]{:S(2)}) collective-permute-start(bf16[1,8,2048]{2,1,0:T(8,128)(2,1)S(1)} %get-tuple-element.48), channel_id=1, source_target_pairs={{0,16},{1,17},{2,18},{3,19},{4,20},{5,21},{6,22},{7,23},{8,24},{9,... | collective-permute-start | bytes 98312 | tf_op jit(solution)/shard_map/ppermute | solution.py:52
  38.4 4.9 %collective-permute-start.19 = (bf16[1,8,2048]{2,1,0:T(8,128)(2,1)S(1)}, bf16[1,8,2048]{2,1,0:T(8,128)(2,1)S(1)}, u32[]{:S(2)}, u32[]{:S(2)}) collective-permute-start(bf16[1,8,2048]{2,1,0:T(8,128)(2,1)S(1)} %get-tuple-element.49), channel_id=1, source_target_pairs={{0,8},{1,9},{2,10},{3,11},{4,12},{5,13},{6,14},{7,15},{8,0},{9,1},... | collective-permute-start | bytes 98312 | tf_op jit(solution)/shard_map/ppermute | solution.py:52

commit v6 on v5

--- a/solution.py
+++ b/solution.py
@@ -11,11 +11,6 @@
 CHUNK = 8
 LARGE = 16 * 1024 * 1024
 SMALL = 4 * 1024 * 1024
-GATHER_FIRST = (0, 1, 2)
-GATHER_LAST = (0, 1, 2)
-CORE_ORDER = (3, 2, 1, 0)
-SCATTER_FIRST = (2, 1, 0)
-SCATTER_LAST = (2, 1, 0)
 F32 = jnp.float32
 BF16 = jnp.bfloat16
 
@@ -48,33 +43,20 @@
     return lax.dot_general(a, b, (((ca,), (cb,)), ((), ())), preferred_element_type=F32)
 
 
-def exchange(x, masks, total, core):
-    return lax.ppermute(x, AXES, [(i, i ^ masks[i // core % 2]) for i in range(total)])
-
-
-def exchange_all(blocks, masks, order, total, core):
-    got = {}
-    for at in order:
-        if at < len(masks):
-            block = blocks[at] if isinstance(blocks, list) else blocks
-            got[at] = exchange(block, masks[at], total, core)
-    return got
+def exchange(x, mask, total):
+    return lax.ppermute(x, AXES, [(i, i ^ mask) for i in range(total)])
+
+
+def exchange_all(blocks, masks, total):
+    if not isinstance(blocks, list):
+        blocks = [blocks] * len(masks)
+    return [exchange(block, mask, total) for block, mask in zip(blocks, masks)]
 
 
 def stages(total, core):
     bits = [1 << b for b in reversed(range(total.bit_length() - 1)) if 1 << b != core]
-    plan = []
-    while bits:
-        a, bits = bits[0], bits[1:]
-        if not bits:
-            plan.append([(a, a)])
-            continue
-        b, bits = bits[0], bits[1:]
-        if (a > core) == (b > core) and b > 2 * core:
-            plan.append([(b, b), (a, a), (a + b, a + b)])
-        else:
-            plan.append([(b, a), (a, b), (a + b, a + b)])
-    return plan
+    pairs = [bits[i : i + 2] for i in range(0, len(bits), 2)]
+    return [[p[1], p[0], p[0] + p[1]] if len(p) == 2 else p for p in pairs]
 
 
 def pack(tokens, route_ids, route_weights, grad_out, experts):
@@ -149,11 +131,11 @@
     )(*outside(weights), after)
 
 
-def regroup(blocks, places):
+def regroup(blocks):
     _, rows, width = blocks[0].shape
 
     def body(*refs):
-        x = [refs[places.index(at)][0].astype(F32) for at in range(len(blocks))]
+        x = [r[0].astype(F32) for r in refs[:-1]]
         low = lax.broadcasted_iota(jnp.int32, (rows, 1), 0) < ROWS
         pairs = list(zip(x[::2], x[1::2]))
         token = [jnp.where(low, a, pltpu.roll(b, ROWS, 0)) for a, b in pairs]
@@ -195,7 +177,9 @@
         do_ref[...] = dout
         gate = dot(token, wg_ref[...])
         upper = dot(token, wu_ref[...])
-        dact = dot(dout, wd_ref[...], 1, 1)
+        mid = hid // 2
+        dact = [dot(wd_ref[:mid], dout, 1, 1).T, dot(dout, wd_ref[mid:], 1, 1)]
+        dact = jnp.concatenate(dact, axis=1)
         sig = jax.nn.sigmoid(gate)
         swish = gate * sig
         hidden = (swish * upper).astype(BF16)
@@ -203,8 +187,10 @@
         dupper = (dact * swish).astype(BF16)
         h_ref[...], dg_ref[...], du_ref[...] = hidden, dgate, dupper
         part = (coef * dot(hidden, wd_ref[...])).astype(BF16).reshape(blocks, half, width)
-        back = dot(wg_ref[...], dgate, 1, 1) + dot(wu_ref[...], dupper, 1, 1)
-        back = back.astype(BF16).T.reshape(blocks, half, width)
+        mid = width // 2
+        back = (dot(wg_ref[:mid], dgate, 1, 1) + dot(wu_ref[:mid], dupper, 1, 1)).astype(BF16).T
+        rest = (dot(dgate, wg_ref[mid:], 1, 1) + dot(dupper, wu_ref[mid:], 1, 1)).astype(BF16)
+        back = jnp.concatenate([back, rest], axis=1).reshape(blocks, half, width)
         at = 0
         for ref, n in zip(parts, splits):
             ref[:, :half] = part[at : at + n]
@@ -335,15 +321,13 @@
     wg, wu, wd = w_gate[0], w_up[0], w_down[0]
 
     block = pack(tokens, route_ids, route_weights, grad_out, experts)
-    got = exchange_all(block, plan[0], GATHER_FIRST, total, core)
-    block = regroup([block, *got.values()], [0] + [at + 1 for at in got])
+    block = regroup([block] + exchange_all(block, plan[0], total))
     for masks in plan[1:]:
-        got = exchange_all(block, masks, GATHER_LAST, total, core)
-        held = [block] + [got[at] for at in range(len(masks))]
+        held = [block] + exchange_all(block, masks, total)
         block = jnp.concatenate(held, axis=0)
     wg, own = fetch(wg, held[0])
     wu, wd = fetch_behind((wu, wd), held[1])
-    pieces = held + [exchange(h, (core, core), total, core) for h in [own] + held[1:]]
+    pieces = held + [exchange(h, core, total) for h in [own] + held[1:]]
 
     ways = len(held)
     groups = total // GROUP
@@ -366,16 +350,15 @@
     (down_grad,) = weight_grads(hidden, [dout], 2)
 
     keep, send = parts[:ways], parts[ways:]
-    arrived = [exchange(send[at], (core, core), total, core) for at in CORE_ORDER if at < ways]
-    arrived = dict(zip([at for at in CORE_ORDER if at < ways], arrived))
+    arrived = [exchange(p, core, total) for p in send[::-1]][::-1]
     sums = [add_pair(keep[at], arrived[at]) for at in range(1, ways)]
-    terms = [*exchange_all(sums, plan[-1], SCATTER_FIRST, total, core).values(), keep[0], arrived[0]]
+    terms = [*exchange_all(sums[::-1], plan[-1][::-1], total), keep[0], arrived[0]]
     for masks in reversed(plan[1:-1]):
         ways = len(masks) + 1
         mine, *others = add(terms, [terms[0].shape[0] // ways] * ways)
-        terms = [mine, *exchange_all(others, masks, SCATTER_FIRST, total, core).values()]
+        terms = [mine, *exchange_all(others[::-1], masks[::-1], total)]
     mine, *others = add_ungroup(terms, (gate_grad,))
-    terms = [mine, *exchange_all(others, plan[0], SCATTER_LAST, total, core).values()]
+    terms = [mine, *exchange_all(others[::-1], plan[0][::-1], total)]
     mixed, back = finish(terms, (down_grad,))
     return mixed, back, gate_grad[None], up_grad[None], down_grad[None]
 

time: 44.3 us -> 44.1 us (level)
  no operation moved by 1% of the time
where the time goes in v6:
time: 44.1 us; the launch traced here: 43.7 us
  starting transfers between devices  19.1 us (43%)
  Pallas kernels  12.9 us (29%)
  waiting for transfers between devices  10.9 us (25%)
  between operations  0.75 us (2%)
    ppermute x20, starting transfers between devices, exchange(): return lax.ppermute(x, AXES, [(i, i ^ mask) for i in range(total)])  19.1 us
    ppermute x20, waiting for transfers between devices, exchange(): return lax.ppermute(x, AXES, [(i, i ^ mask) for i in range(total)])  10.9 us
    pallas_call x2, Pallas kernels, weight_grads(): pl.pallas_call(body, grid=(steps,), out_shape=[shape(rows, cols) for _ in...  4.49 us
    pallas_call x1, Pallas kernels, expert_math(): pl.pallas_call(body, out_shape=outs, in_specs=[vmem()] * count + [pl.Bloc...  2.83 us
    pallas_call x1, Pallas kernels, fetch_behind(): pl.pallas_call(body, out_shape=[shape(*w.shape) for w in weights], in_spe...  2.24 us
    pallas_call x1, Pallas kernels, fetch(): pl.pallas_call(body, out_shape=[shape(*w.shape), shape(*block.shape)], in...  1.6 us
    pallas_call x1, Pallas kernels, pack(): pl.pallas_call(body, out_shape=shape(1, 2 * rows, width + lanes), in_spec...  0.92 us
  transfers between devices with their start and end apart: 20, of which 9 were waited for; matrix products, arithmetic and copies ran while one was open for 0% of the time, Pallas kernels for 19%

profile of v6, /device:TPU:0, one launch (start us, length us, event | category | flops | bytes accessed | tf_op | source)
XLA Modules:
  0.0 43.7 jit_solution(14363338709022912150)
XLA Ops:
  0.6 0.9 %shard_map.110.refs_0_ = bf16[1,8,2176]{2,1,0:T(8,128)(2,1)S(1)} custom-call(bf16[4,2048]{1,0:T(4,128)(2,1)} %t_in.1, s32[4,8]{1,0:T(4,128)} %i_in.1, s32[4,8]{1,0:T(4,128)} %w_in.1, bf16[4,2048]{1,0:T(4,128)(2,1)} %g_in.1), custom_call_target="tpu_custom_call" | custom-call | bytes 81920 | tf_op jit(solution)/shard_map/pallas_call | solution.py:84
  1.6 5.1 %collective-permute-start.2 = (bf16[1,8,2176]{2,1,0:T(8,128)(2,1)S(1)}, bf16[1,8,2176]{2,1,0:T(8,128)(2,1)S(1)}, u32[]{:S(2)}, u32[]{:S(2)}) collective-permute-start(bf16[1,8,2176]{2,1,0:T(8,128)(2,1)S(1)} %shard_map.110.refs_0_), channel_id=1, source_target_pairs={{0,24},{1,25},{2,26},{3,27},{4,28},{5,29},{6,30},{7,31},{8,16},{9,... | collective-permute-start | bytes 104456 | tf_op jit(solution)/shard_map/ppermute | solution.py:47
  6.7 0.0 collective-permute-start.1
  6.7 0.6 %collective-permute-start = (bf16[1,8,2176]{2,1,0:T(8,128)(2,1)S(1)}, bf16[1,8,2176]{2,1,0:T(8,128)(2,1)S(1)}, u32[]{:S(2)}, u32[]{:S(2)}) collective-permute-start(bf16[1,8,2176]{2,1,0:T(8,128)(2,1)S(1)} %shard_map.110.refs_0_), channel_id=1, source_target_pairs={{0,8},{1,9},{2,10},{3,11},{4,12},{5,13},{6,14},{7,15},{8,0},{9,1},... | collective-permute-start | bytes 104456 | tf_op jit(solution)/shard_map/ppermute | solution.py:47
  7.3 1.3 %collective-permute-done.2.refs_3_ = bf16[1,8,2176]{2,1,0:T(8,128)(2,1)S(1)} collective-permute-done((bf16[1,8,2176]{2,1,0:T(8,128)(2,1)S(1)}, bf16[1,8,2176]{2,1,0:T(8,128)(2,1)S(1)}, u32[]{:S(2)}, u32[]{:S(2)}) %collective-permute-start.2) | collective-permute-done | bytes 34848 | tf_op jit(solution)/shard_map/ppermute | solution.py:47
  8.6 2.9 %collective-permute-done.1.refs_2_ = bf16[1,8,2176]{2,1,0:T(8,128)(2,1)S(1)} collective-permute-done((bf16[1,8,2176]{2,1,0:T(8,128)(2,1)S(1)}, bf16[1,8,2176]{2,1,0:T(8,128)(2,1)S(1)}, u32[]{:S(2)}, u32[]{:S(2)}) %collective-permute-start.1) | collective-permute-done | bytes 34848 | tf_op jit(solution)/shard_map/ppermute | solution.py:47
  11.5 0.0 collective-permute-done.refs_1_
  11.6 2.5 %collective-permute-start.5 = (bf16[1,32,2176]{2,1,0:T(8,128)(2,1)S(1)}, bf16[1,32,2176]{2,1,0:T(8,128)(2,1)S(1)}, u32[]{:S(2)}, u32[]{:S(2)}) collective-permute-start(bf16[1,32,2176]{2,1,0:T(8,128)(2,1)S(1)} %shard_map.111.b_ref.refs_0_), channel_id=1, source_target_pairs={{0,5},{1,4},{2,7},{3,6},{4,1},{5,0},{6,3},{7,2},{8,13},{9,12},{10,... | collective-permute-start | bytes 417800 | tf_op jit(solution)/shard_map/ppermute | solution.py:47
  14.1 0.5 %collective-permute-start.4 = (bf16[1,32,2176]{2,1,0:T(8,128)(2,1)S(1)}, bf16[1,32,2176]{2,1,0:T(8,128)(2,1)S(1)}, u32[]{:S(2)}, u32[]{:S(2)}) collective-permute-start(bf16[1,32,2176]{2,1,0:T(8,128)(2,1)S(1)} %shard_map.111.b_ref.refs_0_), channel_id=1, source_target_pairs={{0,4},{1,5},{2,6},{3,7},{4,0},{5,1},{6,2},{7,3},{8,12},{9,13},{10,... | collective-permute-start | bytes 417800 | tf_op jit(solution)/shard_map/ppermute | solution.py:47
  14.6 0.5 %collective-permute-start.3 = (bf16[1,32,2176]{2,1,0:T(8,128)(2,1)S(1)}, bf16[1,32,2176]{2,1,0:T(8,128)(2,1)S(1)}, u32[]{:S(2)}, u32[]{:S(2)}) collective-permute-start(bf16[1,32,2176]{2,1,0:T(8,128)(2,1)S(1)} %shard_map.111.b_ref.refs_0_), channel_id=1, source_target_pairs={{0,1},{1,0},{2,3},{3,2},{4,5},{5,4},{6,7},{7,6},{8,9},{9,8},{10,11... | collective-permute-start | bytes 417800 | tf_op jit(solution)/shard_map/ppermute | solution.py:47
  15.1 1.6 %shard_map.112 = (bf16[2048,512]{1,0:T(8,128)(2,1)S(1)}, bf16[1,32,2176]{2,1,0:T(8,128)(2,1)S(1)}) custom-call(bf16[2048,512]{1,0:T(8,128)(2,1)} %bitcast.8, bf16[1,32,2176]{2,1,0:T(8,128)(2,1)S(1)} %shard_map.111.b_ref.refs_0_), custom_call_target="tpu_custom_call" | custom-call | bytes 4194304 | tf_op jit(solution)/shard_map/pallas_call | solution.py:102
  16.7 0.1 collective-permute-start.6
  16.8 2.3 %collective-permute-done.5.refs_3_ = bf16[1,32,2176]{2,1,0:T(8,128)(2,1)S(1)} collective-permute-done((bf16[1,32,2176]{2,1,0:T(8,128)(2,1)S(1)}, bf16[1,32,2176]{2,1,0:T(8,128)(2,1)S(1)}, u32[]{:S(2)}, u32[]{:S(2)}) %collective-permute-start.5) | collective-permute-done | bytes 139296 | tf_op jit(solution)/shard_map/ppermute | solution.py:47
  19.1 0.0 collective-permute-start.9
  19.1 0.8 %collective-permute-done.4.refs_2_ = bf16[1,32,2176]{2,1,0:T(8,128)(2,1)S(1)} collective-permute-done((bf16[1,32,2176]{2,1,0:T(8,128)(2,1)S(1)}, bf16[1,32,2176]{2,1,0:T(8,128)(2,1)S(1)}, u32[]{:S(2)}, u32[]{:S(2)}) %collective-permute-start.4) | collective-permute-done | bytes 139296 | tf_op jit(solution)/shard_map/ppermute | solution.py:47
  19.8 0.0 collective-permute-start.8
  19.9 0.0 collective-permute-done.3.refs_2_.refs_1_
  19.9 0.5 %collective-permute-start.7 = (bf16[1,32,2176]{2,1,0:T(8,128)(2,1)S(1)}, bf16[1,32,2176]{2,1,0:T(8,128)(2,1)S(1)}, u32[]{:S(2)}, u32[]{:S(2)}) collective-permute-start(bf16[1,32,2176]{2,1,0:T(8,128)(2,1)S(1)} %collective-permute-done.3.refs_2_.refs_1_), channel_id=1, source_target_pairs={{0,2},{1,3},{2,0},{3,1},{4,6},{5,7},{6,4},{7,5},{8,10},{9,11},{10,... | collective-permute-start | bytes 417800 | tf_op jit(solution)/shard_map/ppermute | solution.py:47
  20.4 2.2 %shard_map.113 = (bf16[2048,512]{1,0:T(8,128)(2,1)S(1)}, bf16[512,2048]{1,0:T(8,128)(2,1)S(1)}) custom-call(bf16[2048,512]{1,0:T(8,128)(2,1)} %bitcast.9, bf16[512,2048]{1,0:T(8,128)(2,1)} %bitcast.10, bf16[1,32,2176]{2,1,0:T(8,128)(2,1)S(1)} %collective-permute-done.3.refs_2_.refs_1_), custom_call_target="tpu_custom_call" | custom-call | bytes 8388608 | tf_op jit(solution)/shard_map/pallas_call | solution.py:123
  22.6 0.0 collective-permute-done.6.refs_4_
  22.6 0.0 collective-permute-done.9.refs_7_
  22.6 0.0 collective-permute-done.8.refs_6_
  22.6 0.0 collective-permute-done.7.refs_5_
  22.6 2.8 %shard_map.114 = (bf16[1,32,2048]{2,1,0:T(8,128)(2,1)S(1)}, bf16[1,32,2048]{2,1,0:T(8,128)(2,1)S(1)}, bf16[1,32,2048]{2,1,0:T(8,128)(2,1)S(1)}, bf16[1,32,2048]{...) custom-call(bf16[1,32,2176]{2,1,0:T(8,128)(2,1)S(1)} %shard_map.111., ...), custom_call_target="tpu_custom_call" | custom-call | flops 1610612736 | bytes 10485760 | tf_op jit(solution)/shard_map/pallas_call | solution.py:202
  25.5 0.1 collective-permute-start.10
  25.6 0.5 %collective-permute-start.12 = (bf16[1,32,2048]{2,1,0:T(8,128)(2,1)S(1)}, bf16[1,32,2048]{2,1,0:T(8,128)(2,1)S(1)}, u32[]{:S(2)}, u32[]{:S(2)}) collective-permute-start(bf16[1,32,2048]{2,1,0:T(8,128)(2,1)S(1)} %get-tuple-element.37), channel_id=1, source_target_pairs={{0,2},{1,3},{2,0},{3,1},{4,6},{5,7},{6,4},{7,5},{8,10},{9,11},{10,... | collective-permute-start | bytes 393224 | tf_op jit(solution)/shard_map/ppermute | solution.py:47
  26.1 0.1 collective-permute-start.14
  26.1 0.4 collective-permute-start.16
  26.6 0.3 collective-permute-done.10.b_ref
  26.9 1.5 %collective-permute-start.11 = (bf16[1,32,2048]{2,1,0:T(8,128)(2,1)S(1)}, bf16[1,32,2048]{2,1,0:T(8,128)(2,1)S(1)}, u32[]{:S(2)}, u32[]{:S(2)}) collective-permute-start(bf16[1,32,2048]{2,1,0:T(8,128)(2,1)S(1)} %shard_map.115), channel_id=1, source_target_pairs={{0,5},{1,4},{2,7},{3,6},{4,1},{5,0},{6,3},{7,2},{8,13},{9,12},{10,... | collective-permute-start | bytes 393224 | tf_op jit(solution)/shard_map/ppermute | solution.py:47
  28.4 0.0 collective-permute-done.12.b_ref
  28.4 1.3 %collective-permute-start.13 = (bf16[1,32,2048]{2,1,0:T(8,128)(2,1)S(1)}, bf16[1,32,2048]{2,1,0:T(8,128)(2,1)S(1)}, u32[]{:S(2)}, u32[]{:S(2)}) collective-permute-start(bf16[1,32,2048]{2,1,0:T(8,128)(2,1)S(1)} %shard_map.116), channel_id=1, source_target_pairs={{0,4},{1,5},{2,6},{3,7},{4,0},{5,1},{6,2},{7,3},{8,12},{9,13},{10,... | collective-permute-start | bytes 393224 | tf_op jit(solution)/shard_map/ppermute | solution.py:47
  29.7 0.0 collective-permute-done.14.b_ref
  29.7 1.0 %collective-permute-start.15 = (bf16[1,32,2048]{2,1,0:T(8,128)(2,1)S(1)}, bf16[1,32,2048]{2,1,0:T(8,128)(2,1)S(1)}, u32[]{:S(2)}, u32[]{:S(2)}) collective-permute-start(bf16[1,32,2048]{2,1,0:T(8,128)(2,1)S(1)} %shard_map.117), channel_id=1, source_target_pairs={{0,1},{1,0},{2,3},{3,2},{4,5},{5,4},{6,7},{7,6},{8,9},{9,8},{10,11... | collective-permute-start | bytes 393224 | tf_op jit(solution)/shard_map/ppermute | solution.py:47
  30.7 2.6 %shard_map.118 = (bf16[2048,512]{1,0:T(8,128)(2,1)}, bf16[2048,512]{1,0:T(8,128)(2,1)}) custom-call(bf16[128,2048]{1,0:T(8,128)(2,1)S(1)} %get-tuple-element.42.l_ref, bf16[128,512]{1,0:T(8,128)(2,1)S(1)} %get-tuple-element.43.refs_0_, bf16[128,512]{1,0:T(8,128)(2,1)S(1)} %get-tuple-element.44.refs_1_), custom_call_target="tpu_custom_call" | custom-call | flops 536870912 | bytes 4194304 | tf_op jit(solution)/shard_map/pallas_call | solution.py:223
  33.3 0.0 collective-permute-done.16.refs_4_
  33.3 1.0 %collective-permute-done.11.refs_0_ = bf16[1,32,2048]{2,1,0:T(8,128)(2,1)S(1)} collective-permute-done((bf16[1,32,2048]{2,1,0:T(8,128)(2,1)S(1)}, bf16[1,32,2048]{2,1,0:T(8,128)(2,1)S(1)}, u32[]{:S(2)}, u32[]{:S(2)}) %collective-permute-start.11) | collective-permute-done | bytes 131104 | tf_op jit(solution)/shard_map/ppermute | solution.py:47
  34.3 2.0 %collective-permute-done.13.refs_1_ = bf16[1,32,2048]{2,1,0:T(8,128)(2,1)S(1)} collective-permute-done((bf16[1,32,2048]{2,1,0:T(8,128)(2,1)S(1)}, bf16[1,32,2048]{2,1,0:T(8,128)(2,1)S(1)}, u32[]{:S(2)}, u32[]{:S(2)}) %collective-permute-start.13) | collective-permute-done | bytes 131104 | tf_op jit(solution)/shard_map/ppermute | solution.py:47
  36.3 0.0 collective-permute-done.15.refs_2_
  36.3 0.1 shard_map.119
  36.4 1.6 %collective-permute-start.17 = (bf16[1,8,2048]{2,1,0:T(8,128)(2,1)S(1)}, bf16[1,8,2048]{2,1,0:T(8,128)(2,1)S(1)}, u32[]{:S(2)}, u32[]{:S(2)}) collective-permute-start(bf16[1,8,2048]{2,1,0:T(8,128)(2,1)S(1)} %get-tuple-element.47), channel_id=1, source_target_pairs={{0,24},{1,25},{2,26},{3,27},{4,28},{5,29},{6,30},{7,31},{8,16},{9,... | collective-permute-start | bytes 98312 | tf_op jit(solution)/shard_map/ppermute | solution.py:47
  38.0 0.5 %collective-permute-start.18 = (bf16[1,8,2048]{2,1,0:T(8,128)(2,1)S(1)}, bf16[1,8,2048]{2,1,0:T(8,128)(2,1)S(1)}, u32[]{:S(2)}, u32[]{:S(2)}) collective-permute-start(bf16[1,8,2048]{2,1,0:T(8,128)(2,1)S(1)} %get-tuple-element.48), channel_id=1, source_target_pairs={{0,16},{1,17},{2,18},{3,19},{4,20},{5,21},{6,22},{7,23},{8,24},{9,... | collective-permute-start | bytes 98312 | tf_op jit(solution)/shard_map/ppermute | solution.py:47
  38.5 2.3 %collective-permute-start.19 = (bf16[1,8,2048]{2,1,0:T(8,128)(2,1)S(1)}, bf16[1,8,2048]{2,1,0:T(8,128)(2,1)S(1)}, u32[]{:S(2)}, u32[]{:S(2)}) collective-permute-start(bf16[1,8,2048]{2,1,0:T(8,128)(2,1)S(1)} %get-tuple-element.49), channel_id=1, source_target_pairs={{0,8},{1,9},{2,10},{3,11},{4,12},{5,13},{6,14},{7,15},{8,0},{9,1},... | collective-permute-start | bytes 98312 | tf_op jit(solution)/shard_map/ppermute | solution.py:47
  40.8 1.9 %shard_map.120.refs_4_ = bf16[512,2048]{1,0:T(8,128)(2,1)} custom-call(bf16[128,512]{1,0:T(8,128)(2,1)S(1)} %get-tuple-element.50.l_ref, bf16[128,2048]{1,0:T(8,128)(2,1)S(1)} %get-tuple-element.51.refs_0_), custom_call_target="tpu_custom_call" | custom-call | flops 268435456 | bytes 2097152 | tf_op jit(solution)/shard_map/pallas_call | solution.py:223
  42.7 0.0 collective-permute-done.17.refs_1_
  42.7 0.1 collective-permute-done.18.refs_2_
  42.9 0.2 collective-permute-done.19.refs_3_
  43.1 0.6 %shard_map.121 = (bf16[4,2048]{1,0:T(4,128)(2,1)}, bf16[4,2048]{1,0:T(4,128)(2,1)}) custom-call(f32[1,8,2048]{2,1,0:T(8,128)S(1)} %get-tuple-element.46.refs_0_, bf16[1,8,2048]{2,1,0:T(8,128)(2,1)S(1)} %collective-permute-done.17.refs_1_, bf16[1,8,2048]{2,1,0:T(8,128)(2,1)S(1)} %collective-permute-done.18.refs_2_, ...), custom_call_target="tpu_custom_call" | custom-call | bytes 65536 | tf_op jit(solution)/shard_map/pallas_call | solution.py:305
  (4 shorter events, 0.1 us)
Async XLA Ops:
  1.6 7.0 %collective-permute-start.2 = (bf16[1,8,2176]{2,1,0:T(8,128)(2,1)S(1)}, bf16[1,8,2176]{2,1,0:T(8,128)(2,1)S(1)}, u32[]{:S(2)}, u32[]{:S(2)}) collective-permute-start(bf16[1,8,2176]{2,1,0:T(8,128)(2,1)S(1)} %shard_map.110.refs_0_), channel_id=1, source_target_pairs={{0,24},{1,25},{2,26},{3,27},{4,28},{5,29},{6,30},{7,31},{8,16},{9,... | collective-permute-start | bytes 104456 | tf_op jit(solution)/shard_map/ppermute | solution.py:47
  6.7 4.8 %collective-permute-start.1 = (bf16[1,8,2176]{2,1,0:T(8,128)(2,1)S(1)}, bf16[1,8,2176]{2,1,0:T(8,128)(2,1)S(1)}, u32[]{:S(2)}, u32[]{:S(2)}) collective-permute-start(bf16[1,8,2176]{2,1,0:T(8,128)(2,1)S(1)} %shard_map.110.refs_0_), channel_id=1, source_target_pairs={{0,16},{1,17},{2,18},{3,19},{4,20},{5,21},{6,22},{7,23},{8,24},{9,... | collective-permute-start | bytes 104456 | tf_op jit(solution)/shard_map/ppermute | solution.py:47
  6.7 4.8 %collective-permute-start = (bf16[1,8,2176]{2,1,0:T(8,128)(2,1)S(1)}, bf16[1,8,2176]{2,1,0:T(8,128)(2,1)S(1)}, u32[]{:S(2)}, u32[]{:S(2)}) collective-permute-start(bf16[1,8,2176]{2,1,0:T(8,128)(2,1)S(1)} %shard_map.110.refs_0_), channel_id=1, source_target_pairs={{0,8},{1,9},{2,10},{3,11},{4,12},{5,13},{6,14},{7,15},{8,0},{9,1},... | collective-permute-start | bytes 104456 | tf_op jit(solution)/shard_map/ppermute | solution.py:47
  11.6 7.5 %collective-permute-start.5 = (bf16[1,32,2176]{2,1,0:T(8,128)(2,1)S(1)}, bf16[1,32,2176]{2,1,0:T(8,128)(2,1)S(1)}, u32[]{:S(2)}, u32[]{:S(2)}) collective-permute-start(bf16[1,32,2176]{2,1,0:T(8,128)(2,1)S(1)} %shard_map.111.b_ref.refs_0_), channel_id=1, source_target_pairs={{0,5},{1,4},{2,7},{3,6},{4,1},{5,0},{6,3},{7,2},{8,13},{9,12},{10,... | collective-permute-start | bytes 417800 | tf_op jit(solution)/shard_map/ppermute | solution.py:47
  14.1 5.8 %collective-permute-start.4 = (bf16[1,32,2176]{2,1,0:T(8,128)(2,1)S(1)}, bf16[1,32,2176]{2,1,0:T(8,128)(2,1)S(1)}, u32[]{:S(2)}, u32[]{:S(2)}) collective-permute-start(bf16[1,32,2176]{2,1,0:T(8,128)(2,1)S(1)} %shard_map.111.b_ref.refs_0_), channel_id=1, source_target_pairs={{0,4},{1,5},{2,6},{3,7},{4,0},{5,1},{6,2},{7,3},{8,12},{9,13},{10,... | collective-permute-start | bytes 417800 | tf_op jit(solution)/shard_map/ppermute | solution.py:47
  14.6 5.3 %collective-permute-start.3 = (bf16[1,32,2176]{2,1,0:T(8,128)(2,1)S(1)}, bf16[1,32,2176]{2,1,0:T(8,128)(2,1)S(1)}, u32[]{:S(2)}, u32[]{:S(2)}) collective-permute-start(bf16[1,32,2176]{2,1,0:T(8,128)(2,1)S(1)} %shard_map.111.b_ref.refs_0_), channel_id=1, source_target_pairs={{0,1},{1,0},{2,3},{3,2},{4,5},{5,4},{6,7},{7,6},{8,9},{9,8},{10,11... | collective-permute-start | bytes 417800 | tf_op jit(solution)/shard_map/ppermute | solution.py:47
  16.7 5.9 %collective-permute-start.6 = (bf16[1,32,2176]{2,1,0:T(8,128)(2,1)S(1)}, bf16[1,32,2176]{2,1,0:T(8,128)(2,1)S(1)}, u32[]{:S(2)}, u32[]{:S(2)}) collective-permute-start(bf16[1,32,2176]{2,1,0:T(8,128)(2,1)S(1)} %get-tuple-element.30), channel_id=1, source_target_pairs={{0,2},{1,3},{2,0},{3,1},{4,6},{5,7},{6,4},{7,5},{8,10},{9,11},{10,... | collective-permute-start | bytes 417800 | tf_op jit(solution)/shard_map/ppermute | solution.py:47
  19.1 3.6 %collective-permute-start.9 = (bf16[1,32,2176]{2,1,0:T(8,128)(2,1)S(1)}, bf16[1,32,2176]{2,1,0:T(8,128)(2,1)S(1)}, u32[]{:S(2)}, u32[]{:S(2)}) collective-permute-start(bf16[1,32,2176]{2,1,0:T(8,128)(2,1)S(1)} %collective-permute-done.5.refs_3_), channel_id=1, source_target_pairs={{0,2},{1,3},{2,0},{3,1},{4,6},{5,7},{6,4},{7,5},{8,10},{9,11},{10,... | collective-permute-start | bytes 417800 | tf_op jit(solution)/shard_map/ppermute | solution.py:47
  19.8 2.8 %collective-permute-start.8 = (bf16[1,32,2176]{2,1,0:T(8,128)(2,1)S(1)}, bf16[1,32,2176]{2,1,0:T(8,128)(2,1)S(1)}, u32[]{:S(2)}, u32[]{:S(2)}) collective-permute-start(bf16[1,32,2176]{2,1,0:T(8,128)(2,1)S(1)} %collective-permute-done.4.refs_2_), channel_id=1, source_target_pairs={{0,2},{1,3},{2,0},{3,1},{4,6},{5,7},{6,4},{7,5},{8,10},{9,11},{10,... | collective-permute-start | bytes 417800 | tf_op jit(solution)/shard_map/ppermute | solution.py:47
  19.9 2.8 %collective-permute-start.7 = (bf16[1,32,2176]{2,1,0:T(8,128)(2,1)S(1)}, bf16[1,32,2176]{2,1,0:T(8,128)(2,1)S(1)}, u32[]{:S(2)}, u32[]{:S(2)}) collective-permute-start(bf16[1,32,2176]{2,1,0:T(8,128)(2,1)S(1)} %collective-permute-done.3.refs_2_.refs_1_), channel_id=1, source_target_pairs={{0,2},{1,3},{2,0},{3,1},{4,6},{5,7},{6,4},{7,5},{8,10},{9,11},{10,... | collective-permute-start | bytes 417800 | tf_op jit(solution)/shard_map/ppermute | solution.py:47
  25.5 1.4 %collective-permute-start.10 = (bf16[1,32,2048]{2,1,0:T(8,128)(2,1)S(1)}, bf16[1,32,2048]{2,1,0:T(8,128)(2,1)S(1)}, u32[]{:S(2)}, u32[]{:S(2)}) collective-permute-start(bf16[1,32,2048]{2,1,0:T(8,128)(2,1)S(1)} %get-tuple-element.35), channel_id=1, source_target_pairs={{0,2},{1,3},{2,0},{3,1},{4,6},{5,7},{6,4},{7,5},{8,10},{9,11},{10,... | collective-permute-start | bytes 393224 | tf_op jit(solution)/shard_map/ppermute | solution.py:47
  25.6 2.8 %collective-permute-start.12 = (bf16[1,32,2048]{2,1,0:T(8,128)(2,1)S(1)}, bf16[1,32,2048]{2,1,0:T(8,128)(2,1)S(1)}, u32[]{:S(2)}, u32[]{:S(2)}) collective-permute-start(bf16[1,32,2048]{2,1,0:T(8,128)(2,1)S(1)} %get-tuple-element.37), channel_id=1, source_target_pairs={{0,2},{1,3},{2,0},{3,1},{4,6},{5,7},{6,4},{7,5},{8,10},{9,11},{10,... | collective-permute-start | bytes 393224 | tf_op jit(solution)/shard_map/ppermute | solution.py:47
  26.1 3.6 %collective-permute-start.14 = (bf16[1,32,2048]{2,1,0:T(8,128)(2,1)S(1)}, bf16[1,32,2048]{2,1,0:T(8,128)(2,1)S(1)}, u32[]{:S(2)}, u32[]{:S(2)}) collective-permute-start(bf16[1,32,2048]{2,1,0:T(8,128)(2,1)S(1)} %get-tuple-element.39), channel_id=1, source_target_pairs={{0,2},{1,3},{2,0},{3,1},{4,6},{5,7},{6,4},{7,5},{8,10},{9,11},{10,... | collective-permute-start | bytes 393224 | tf_op jit(solution)/shard_map/ppermute | solution.py:47
  26.1 7.1 %collective-permute-start.16 = (bf16[1,32,2048]{2,1,0:T(8,128)(2,1)S(1)}, bf16[1,32,2048]{2,1,0:T(8,128)(2,1)S(1)}, u32[]{:S(2)}, u32[]{:S(2)}) collective-permute-start(bf16[1,32,2048]{2,1,0:T(8,128)(2,1)S(1)} %get-tuple-element.41), channel_id=1, source_target_pairs={{0,2},{1,3},{2,0},{3,1},{4,6},{5,7},{6,4},{7,5},{8,10},{9,11},{10,... | collective-permute-start | bytes 393224 | tf_op jit(solution)/shard_map/ppermute | solution.py:47
  26.9 7.3 %collective-permute-start.11 = (bf16[1,32,2048]{2,1,0:T(8,128)(2,1)S(1)}, bf16[1,32,2048]{2,1,0:T(8,128)(2,1)S(1)}, u32[]{:S(2)}, u32[]{:S(2)}) collective-permute-start(bf16[1,32,2048]{2,1,0:T(8,128)(2,1)S(1)} %shard_map.115), channel_id=1, source_target_pairs={{0,5},{1,4},{2,7},{3,6},{4,1},{5,0},{6,3},{7,2},{8,13},{9,12},{10,... | collective-permute-start | bytes 393224 | tf_op jit(solution)/shard_map/ppermute | solution.py:47
  28.4 7.8 %collective-permute-start.13 = (bf16[1,32,2048]{2,1,0:T(8,128)(2,1)S(1)}, bf16[1,32,2048]{2,1,0:T(8,128)(2,1)S(1)}, u32[]{:S(2)}, u32[]{:S(2)}) collective-permute-start(bf16[1,32,2048]{2,1,0:T(8,128)(2,1)S(1)} %shard_map.116), channel_id=1, source_target_pairs={{0,4},{1,5},{2,6},{3,7},{4,0},{5,1},{6,2},{7,3},{8,12},{9,13},{10,... | collective-permute-start | bytes 393224 | tf_op jit(solution)/shard_map/ppermute | solution.py:47
  29.7 6.5 %collective-permute-start.15 = (bf16[1,32,2048]{2,1,0:T(8,128)(2,1)S(1)}, bf16[1,32,2048]{2,1,0:T(8,128)(2,1)S(1)}, u32[]{:S(2)}, u32[]{:S(2)}) collective-permute-start(bf16[1,32,2048]{2,1,0:T(8,128)(2,1)S(1)} %shard_map.117), channel_id=1, source_target_pairs={{0,1},{1,0},{2,3},{3,2},{4,5},{5,4},{6,7},{7,6},{8,9},{9,8},{10,11... | collective-permute-start | bytes 393224 | tf_op jit(solution)/shard_map/ppermute | solution.py:47
  36.4 6.4 %collective-permute-start.17 = (bf16[1,8,2048]{2,1,0:T(8,128)(2,1)S(1)}, bf16[1,8,2048]{2,1,0:T(8,128)(2,1)S(1)}, u32[]{:S(2)}, u32[]{:S(2)}) collective-permute-start(bf16[1,8,2048]{2,1,0:T(8,128)(2,1)S(1)} %get-tuple-element.47), channel_id=1, source_target_pairs={{0,24},{1,25},{2,26},{3,27},{4,28},{5,29},{6,30},{7,31},{8,16},{9,... | collective-permute-start | bytes 98312 | tf_op jit(solution)/shard_map/ppermute | solution.py:47
  38.0 4.9 %collective-permute-start.18 = (bf16[1,8,2048]{2,1,0:T(8,128)(2,1)S(1)}, bf16[1,8,2048]{2,1,0:T(8,128)(2,1)S(1)}, u32[]{:S(2)}, u32[]{:S(2)}) collective-permute-start(bf16[1,8,2048]{2,1,0:T(8,128)(2,1)S(1)} %get-tuple-element.48), channel_id=1, source_target_pairs={{0,16},{1,17},{2,18},{3,19},{4,20},{5,21},{6,22},{7,23},{8,24},{9,... | collective-permute-start | bytes 98312 | tf_op jit(solution)/shard_map/ppermute | solution.py:47
  38.5 4.6 %collective-permute-start.19 = (bf16[1,8,2048]{2,1,0:T(8,128)(2,1)S(1)}, bf16[1,8,2048]{2,1,0:T(8,128)(2,1)S(1)}, u32[]{:S(2)}, u32[]{:S(2)}) collective-permute-start(bf16[1,8,2048]{2,1,0:T(8,128)(2,1)S(1)} %get-tuple-element.49), channel_id=1, source_target_pairs={{0,8},{1,9},{2,10},{3,11},{4,12},{5,13},{6,14},{7,15},{8,0},{9,1},... | collective-permute-start | bytes 98312 | tf_op jit(solution)/shard_map/ppermute | solution.py:47

commit v7 on v6

--- a/solution.py
+++ b/solution.py
@@ -110,25 +110,29 @@
     )(*outside((w,)), block)
 
 
-def fetch_behind(weights, after):
+def fetch_behind(weights, inside, after):
     n = len(weights)
 
     def body(*refs):
-        copies = [pltpu.make_async_copy(refs[k], refs[n + 1 + k], refs[-1].at[k]) for k in range(n)]
+        outs = refs[n + 2 : -1]
+        copies = [pltpu.make_async_copy(refs[k], outs[k], refs[-1].at[k]) for k in range(n)]
         for c in copies:
             c.start()
-        for c in copies:
+        outs[n][...] = refs[n][...].T
+        copies[0].wait()
+        outs[n + 1][...] = outs[0][...].T
+        for c in copies[1:]:
             c.wait()
 
     return pl.pallas_call(
         body,
-        out_shape=[shape(*w.shape) for w in weights],
-        in_specs=[hbm() for _ in weights] + [pl.BlockSpec(memory_space=pl.ANY)],
-        out_specs=[vmem() for _ in weights],
+        out_shape=[shape(*w.shape) for w in weights] + [shape(*inside.shape[::-1]), shape(*weights[0].shape[::-1])],
+        in_specs=[hbm() for _ in weights] + [vmem(), pl.BlockSpec(memory_space=pl.ANY)],
+        out_specs=[vmem() for _ in range(n + 2)],
         scratch_shapes=[pltpu.SemaphoreType.DMA((n,))],
         compiler_params=params(),
         cost_estimate=cost(0, 8 << 20),
-    )(*outside(weights), after)
+    )(*outside(weights), inside, after)
 
 
 def regroup(blocks):
@@ -152,7 +156,7 @@
     )(*blocks)
 
 
-def expert_math(pieces, me, w_gate, w_up, w_down, experts, splits):
+def expert_math(pieces, me, w_gate, turned, w_up, w_down, experts, splits):
     blocks = sum(p.shape[0] for p in pieces)
     width, hid = w_gate.shape
     _, rows, full = pieces[0].shape
@@ -162,8 +166,8 @@
     count = len(pieces)
 
     def body(*refs):
-        me_ref, wg_ref, wu_ref, wd_ref = refs[count : count + 4]
-        outs = refs[count + 4 :]
+        me_ref, wg_ref, gw_ref, dw_ref, wu_ref, wd_ref = refs[count : count + 6]
+        outs = refs[count + 6 :]
         parts, (t_ref, do_ref, h_ref, dg_ref, du_ref) = outs[: len(splits)], outs[len(splits) :]
         x = jnp.concatenate([r[...] for r in refs[:count]], axis=0)
         token = x[:, :half, :width].reshape(m, width)
@@ -177,9 +181,7 @@
         do_ref[...] = dout
         gate = dot(token, wg_ref[...])
         upper = dot(token, wu_ref[...])
-        mid = hid // 2
-        dact = [dot(wd_ref[:mid], dout, 1, 1).T, dot(dout, wd_ref[mid:], 1, 1)]
-        dact = jnp.concatenate(dact, axis=1)
+        dact = dot(dout, dw_ref[...])
         sig = jax.nn.sigmoid(gate)
         swish = gate * sig
         hidden = (swish * upper).astype(BF16)
@@ -188,9 +190,9 @@
         h_ref[...], dg_ref[...], du_ref[...] = hidden, dgate, dupper
         part = (coef * dot(hidden, wd_ref[...])).astype(BF16).reshape(blocks, half, width)
         mid = width // 2
-        back = (dot(wg_ref[:mid], dgate, 1, 1) + dot(wu_ref[:mid], dupper, 1, 1)).astype(BF16).T
-        rest = (dot(dgate, wg_ref[mid:], 1, 1) + dot(dupper, wu_ref[mid:], 1, 1)).astype(BF16)
-        back = jnp.concatenate([back, rest], axis=1).reshape(blocks, half, width)
+        back = [dot(wu_ref[:mid], dupper, 1, 1).T, dot(dupper, wu_ref[mid:], 1, 1)]
+        back = dot(dgate, gw_ref[...]) + jnp.concatenate(back, axis=1)
+        back = back.astype(BF16).reshape(blocks, half, width)
         at = 0
         for ref, n in zip(parts, splits):
             ref[:, :half] = part[at : at + n]
@@ -202,11 +204,11 @@
     got = pl.pallas_call(
         body,
         out_shape=outs,
-        in_specs=[vmem()] * count + [pl.BlockSpec(memory_space=pltpu.SMEM)] + [vmem()] * 3,
+        in_specs=[vmem()] * count + [pl.BlockSpec(memory_space=pltpu.SMEM)] + [vmem()] * 5,
         out_specs=[vmem() for _ in outs],
         compiler_params=params(LARGE),
         cost_estimate=cost(12 * m * width * hid, 10 << 20),
-    )(*pieces, me, w_gate, w_up, w_down)
+    )(*pieces, me, w_gate, *turned, w_up, w_down)
     return list(got[: len(splits)]), got[len(splits) :]
 
 
@@ -326,19 +328,19 @@
         held = [block] + exchange_all(block, masks, total)
         block = jnp.concatenate(held, axis=0)
     wg, own = fetch(wg, held[0])
-    wu, wd = fetch_behind((wu, wd), held[1])
+    wd, wu, *turned = fetch_behind((wd, wu), wg, held[1])
     pieces = held + [exchange(h, core, total) for h in [own] + held[1:]]
 
     ways = len(held)
     groups = total // GROUP
     size = groups // 2 // ways
     if groups <= CHUNK:
-        parts, kept = expert_math(pieces, me, wg, wu, wd, experts, [size] * (2 * ways))
+        parts, kept = expert_math(pieces, me, wg, turned, wu, wd, experts, [size] * (2 * ways))
     else:
         whole = jnp.concatenate(pieces, axis=0)
         sums, saved = [], []
         for at in range(0, groups, CHUNK):
-            (got,), rest = expert_math([whole[at : at + CHUNK]], me, wg, wu, wd, experts, [CHUNK])
+            (got,), rest = expert_math([whole[at : at + CHUNK]], me, wg, turned, wu, wd, experts, [CHUNK])
             sums.append(got)
             saved.append(rest)
         got = jnp.concatenate(sums, axis=0)

time: 44.1 us -> 43.5 us (0.986)
  Pallas kernels: 12.9 us -> 12.4 us
    pallas_call x1, Pallas kernels: 2.83 us -> 2.23 us  [expert_math(): pl.pallas_call(body, out_shape=outs, in_specs=[vmem()] * count + [pl.Bloc...]
  transfers between devices with their start and end apart: 20 -> 20, of which waited for: 9 -> 9; matrix products, arithmetic and copies ran while one was open for 0% -> 0% of each run, Pallas kernels for 19% -> 20%
where the time goes in v7:
time: 43.5 us; the launch traced here: 43.1 us
  starting transfers between devices  19.1 us (44%)
  Pallas kernels  12.4 us (29%)
  waiting for transfers between devices  10.9 us (25%)
  between operations  0.75 us (2%)
    ppermute x20, starting transfers between devices, exchange(): return lax.ppermute(x, AXES, [(i, i ^ mask) for i in range(total)])  19.1 us
    ppermute x20, waiting for transfers between devices, exchange(): return lax.ppermute(x, AXES, [(i, i ^ mask) for i in range(total)])  10.9 us
    pallas_call x2, Pallas kernels, weight_grads(): pl.pallas_call(body, grid=(steps,), out_shape=[shape(rows, cols) for _ in...  4.5 us
    pallas_call x1, Pallas kernels, fetch_behind(): pl.pallas_call(body, out_shape=[shape(*w.shape) for w in weights] + [shap...  2.25 us
    pallas_call x1, Pallas kernels, expert_math(): pl.pallas_call(body, out_shape=outs, in_specs=[vmem()] * count + [pl.Bloc...  2.23 us
    pallas_call x1, Pallas kernels, fetch(): pl.pallas_call(body, out_shape=[shape(*w.shape), shape(*block.shape)], in...  1.6 us
    pallas_call x1, Pallas kernels, pack(): pl.pallas_call(body, out_shape=shape(1, 2 * rows, width + lanes), in_spec...  0.92 us
  transfers between devices with their start and end apart: 20, of which 9 were waited for; matrix products, arithmetic and copies ran while one was open for 0% of the time, Pallas kernels for 20%

profile of v7, /device:TPU:0, one launch (start us, length us, event | category | flops | bytes accessed | tf_op | source)
XLA Modules:
  0.0 43.1 jit_solution(1043683658696467236)
XLA Ops:
  0.6 0.9 %shard_map.110.refs_0_ = bf16[1,8,2176]{2,1,0:T(8,128)(2,1)S(1)} custom-call(bf16[4,2048]{1,0:T(4,128)(2,1)} %t_in.1, s32[4,8]{1,0:T(4,128)} %i_in.1, s32[4,8]{1,0:T(4,128)} %w_in.1, bf16[4,2048]{1,0:T(4,128)(2,1)} %g_in.1), custom_call_target="tpu_custom_call" | custom-call | bytes 81920 | tf_op jit(solution)/shard_map/pallas_call | solution.py:84
  1.6 5.1 %collective-permute-start.2 = (bf16[1,8,2176]{2,1,0:T(8,128)(2,1)S(1)}, bf16[1,8,2176]{2,1,0:T(8,128)(2,1)S(1)}, u32[]{:S(2)}, u32[]{:S(2)}) collective-permute-start(bf16[1,8,2176]{2,1,0:T(8,128)(2,1)S(1)} %shard_map.110.refs_0_), channel_id=1, source_target_pairs={{0,24},{1,25},{2,26},{3,27},{4,28},{5,29},{6,30},{7,31},{8,16},{9,... | collective-permute-start | bytes 104456 | tf_op jit(solution)/shard_map/ppermute | solution.py:47
  6.7 0.0 collective-permute-start.1
  6.7 0.6 %collective-permute-start = (bf16[1,8,2176]{2,1,0:T(8,128)(2,1)S(1)}, bf16[1,8,2176]{2,1,0:T(8,128)(2,1)S(1)}, u32[]{:S(2)}, u32[]{:S(2)}) collective-permute-start(bf16[1,8,2176]{2,1,0:T(8,128)(2,1)S(1)} %shard_map.110.refs_0_), channel_id=1, source_target_pairs={{0,8},{1,9},{2,10},{3,11},{4,12},{5,13},{6,14},{7,15},{8,0},{9,1},... | collective-permute-start | bytes 104456 | tf_op jit(solution)/shard_map/ppermute | solution.py:47
  7.3 1.3 %collective-permute-done.2.refs_3_ = bf16[1,8,2176]{2,1,0:T(8,128)(2,1)S(1)} collective-permute-done((bf16[1,8,2176]{2,1,0:T(8,128)(2,1)S(1)}, bf16[1,8,2176]{2,1,0:T(8,128)(2,1)S(1)}, u32[]{:S(2)}, u32[]{:S(2)}) %collective-permute-start.2) | collective-permute-done | bytes 34848 | tf_op jit(solution)/shard_map/ppermute | solution.py:47
  8.6 2.9 %collective-permute-done.1.refs_2_ = bf16[1,8,2176]{2,1,0:T(8,128)(2,1)S(1)} collective-permute-done((bf16[1,8,2176]{2,1,0:T(8,128)(2,1)S(1)}, bf16[1,8,2176]{2,1,0:T(8,128)(2,1)S(1)}, u32[]{:S(2)}, u32[]{:S(2)}) %collective-permute-start.1) | collective-permute-done | bytes 34848 | tf_op jit(solution)/shard_map/ppermute | solution.py:47
  11.5 0.0 collective-permute-done.refs_1_
  11.6 2.5 %collective-permute-start.5 = (bf16[1,32,2176]{2,1,0:T(8,128)(2,1)S(1)}, bf16[1,32,2176]{2,1,0:T(8,128)(2,1)S(1)}, u32[]{:S(2)}, u32[]{:S(2)}) collective-permute-start(bf16[1,32,2176]{2,1,0:T(8,128)(2,1)S(1)} %shard_map.111.b_ref.refs_0_), channel_id=1, source_target_pairs={{0,5},{1,4},{2,7},{3,6},{4,1},{5,0},{6,3},{7,2},{8,13},{9,12},{10,... | collective-permute-start | bytes 417800 | tf_op jit(solution)/shard_map/ppermute | solution.py:47
  14.1 0.5 %collective-permute-start.4 = (bf16[1,32,2176]{2,1,0:T(8,128)(2,1)S(1)}, bf16[1,32,2176]{2,1,0:T(8,128)(2,1)S(1)}, u32[]{:S(2)}, u32[]{:S(2)}) collective-permute-start(bf16[1,32,2176]{2,1,0:T(8,128)(2,1)S(1)} %shard_map.111.b_ref.refs_0_), channel_id=1, source_target_pairs={{0,4},{1,5},{2,6},{3,7},{4,0},{5,1},{6,2},{7,3},{8,12},{9,13},{10,... | collective-permute-start | bytes 417800 | tf_op jit(solution)/shard_map/ppermute | solution.py:47
  14.6 0.5 %collective-permute-start.3 = (bf16[1,32,2176]{2,1,0:T(8,128)(2,1)S(1)}, bf16[1,32,2176]{2,1,0:T(8,128)(2,1)S(1)}, u32[]{:S(2)}, u32[]{:S(2)}) collective-permute-start(bf16[1,32,2176]{2,1,0:T(8,128)(2,1)S(1)} %shard_map.111.b_ref.refs_0_), channel_id=1, source_target_pairs={{0,1},{1,0},{2,3},{3,2},{4,5},{5,4},{6,7},{7,6},{8,9},{9,8},{10,11... | collective-permute-start | bytes 417800 | tf_op jit(solution)/shard_map/ppermute | solution.py:47
  15.1 1.6 %shard_map.112 = (bf16[2048,512]{1,0:T(8,128)(2,1)S(1)}, bf16[1,32,2176]{2,1,0:T(8,128)(2,1)S(1)}) custom-call(bf16[2048,512]{1,0:T(8,128)(2,1)} %bitcast.8, bf16[1,32,2176]{2,1,0:T(8,128)(2,1)S(1)} %shard_map.111.b_ref.refs_0_), custom_call_target="tpu_custom_call" | custom-call | bytes 4194304 | tf_op jit(solution)/shard_map/pallas_call | solution.py:102
  16.7 0.1 collective-permute-start.6
  16.8 2.3 %collective-permute-done.5.refs_3_ = bf16[1,32,2176]{2,1,0:T(8,128)(2,1)S(1)} collective-permute-done((bf16[1,32,2176]{2,1,0:T(8,128)(2,1)S(1)}, bf16[1,32,2176]{2,1,0:T(8,128)(2,1)S(1)}, u32[]{:S(2)}, u32[]{:S(2)}) %collective-permute-start.5) | collective-permute-done | bytes 139296 | tf_op jit(solution)/shard_map/ppermute | solution.py:47
  19.1 0.0 collective-permute-start.9
  19.1 0.8 %collective-permute-done.4.refs_2_ = bf16[1,32,2176]{2,1,0:T(8,128)(2,1)S(1)} collective-permute-done((bf16[1,32,2176]{2,1,0:T(8,128)(2,1)S(1)}, bf16[1,32,2176]{2,1,0:T(8,128)(2,1)S(1)}, u32[]{:S(2)}, u32[]{:S(2)}) %collective-permute-start.4) | collective-permute-done | bytes 139296 | tf_op jit(solution)/shard_map/ppermute | solution.py:47
  19.8 0.0 collective-permute-start.8
  19.9 0.0 collective-permute-done.3.refs_3_.refs_1_
  19.9 0.5 %collective-permute-start.7 = (bf16[1,32,2176]{2,1,0:T(8,128)(2,1)S(1)}, bf16[1,32,2176]{2,1,0:T(8,128)(2,1)S(1)}, u32[]{:S(2)}, u32[]{:S(2)}) collective-permute-start(bf16[1,32,2176]{2,1,0:T(8,128)(2,1)S(1)} %collective-permute-done.3.refs_3_.refs_1_), channel_id=1, source_target_pairs={{0,2},{1,3},{2,0},{3,1},{4,6},{5,7},{6,4},{7,5},{8,10},{9,11},{10,... | collective-permute-start | bytes 417800 | tf_op jit(solution)/shard_map/ppermute | solution.py:47
  20.4 2.2 %shard_map.113 = (bf16[512,2048]{1,0:T(8,128)(2,1)S(1)}, bf16[2048,512]{1,0:T(8,128)(2,1)S(1)}, bf16[512,2048]{1,0:T(8,128)(2,1)S(1)}, bf16[2048,512]{1,0:T(8,128)(2,1)S(1)}) custom-call(bf16[512,2048]{1,0:T(8,128)(2,1)} %bitcast.9, bf16[2048,512]{1,0:T(8,128)(2,1)} %bitcast.10, bf16[2048,512]{1,0:T(8,128)(2,1)S(1)} %get-tuple-element.33.refs_2_.refs_9_, ...), custom_call_target="tpu_custom_call" | custom-call | bytes 8388608 | tf_op jit(solution)/shard_map/pallas_call | solution.py:127
  22.6 0.0 collective-permute-done.6.refs_4_
  22.6 0.0 collective-permute-done.9.refs_7_
  22.6 0.0 collective-permute-done.8.refs_6_
  22.6 0.0 collective-permute-done.7.refs_5_
  22.7 2.2 %shard_map.114 = (bf16[1,32,2048]{2,1,0:T(8,128)(2,1)S(1)}, bf16[1,32,2048]{2,1,0:T(8,128)(2,1)S(1)}, bf16[1,32,2048]{2,1,0:T(8,128)(2,1)S(1)}, bf16[1,32,2048]{...) custom-call(bf16[1,32,2176]{2,1,0:T(8,128)(2,1)S(1)} %shard_map.111., ...), custom_call_target="tpu_custom_call" | custom-call | flops 1610612736 | bytes 10485760 | tf_op jit(solution)/shard_map/pallas_call | solution.py:204
  24.9 0.1 collective-permute-start.10
  25.0 0.5 %collective-permute-start.12 = (bf16[1,32,2048]{2,1,0:T(8,128)(2,1)S(1)}, bf16[1,32,2048]{2,1,0:T(8,128)(2,1)S(1)}, u32[]{:S(2)}, u32[]{:S(2)}) collective-permute-start(bf16[1,32,2048]{2,1,0:T(8,128)(2,1)S(1)} %get-tuple-element.41), channel_id=1, source_target_pairs={{0,2},{1,3},{2,0},{3,1},{4,6},{5,7},{6,4},{7,5},{8,10},{9,11},{10,... | collective-permute-start | bytes 393224 | tf_op jit(solution)/shard_map/ppermute | solution.py:47
  25.5 0.1 collective-permute-start.14
  25.6 0.4 %collective-permute-start.16 = (bf16[1,32,2048]{2,1,0:T(8,128)(2,1)S(1)}, bf16[1,32,2048]{2,1,0:T(8,128)(2,1)S(1)}, u32[]{:S(2)}, u32[]{:S(2)}) collective-permute-start(bf16[1,32,2048]{2,1,0:T(8,128)(2,1)S(1)} %get-tuple-element.45), channel_id=1, source_target_pairs={{0,2},{1,3},{2,0},{3,1},{4,6},{5,7},{6,4},{7,5},{8,10},{9,11},{10,... | collective-permute-start | bytes 393224 | tf_op jit(solution)/shard_map/ppermute | solution.py:47
  26.0 0.3 collective-permute-done.10.b_ref
  26.3 1.5 %collective-permute-start.11 = (bf16[1,32,2048]{2,1,0:T(8,128)(2,1)S(1)}, bf16[1,32,2048]{2,1,0:T(8,128)(2,1)S(1)}, u32[]{:S(2)}, u32[]{:S(2)}) collective-permute-start(bf16[1,32,2048]{2,1,0:T(8,128)(2,1)S(1)} %shard_map.115), channel_id=1, source_target_pairs={{0,5},{1,4},{2,7},{3,6},{4,1},{5,0},{6,3},{7,2},{8,13},{9,12},{10,... | collective-permute-start | bytes 393224 | tf_op jit(solution)/shard_map/ppermute | solution.py:47
  27.8 0.0 collective-permute-done.12.b_ref
  27.8 1.3 %collective-permute-start.13 = (bf16[1,32,2048]{2,1,0:T(8,128)(2,1)S(1)}, bf16[1,32,2048]{2,1,0:T(8,128)(2,1)S(1)}, u32[]{:S(2)}, u32[]{:S(2)}) collective-permute-start(bf16[1,32,2048]{2,1,0:T(8,128)(2,1)S(1)} %shard_map.116), channel_id=1, source_target_pairs={{0,4},{1,5},{2,6},{3,7},{4,0},{5,1},{6,2},{7,3},{8,12},{9,13},{10,... | collective-permute-start | bytes 393224 | tf_op jit(solution)/shard_map/ppermute | solution.py:47
  29.1 0.0 collective-permute-done.14.b_ref
  29.2 0.9 %collective-permute-start.15 = (bf16[1,32,2048]{2,1,0:T(8,128)(2,1)S(1)}, bf16[1,32,2048]{2,1,0:T(8,128)(2,1)S(1)}, u32[]{:S(2)}, u32[]{:S(2)}) collective-permute-start(bf16[1,32,2048]{2,1,0:T(8,128)(2,1)S(1)} %shard_map.117), channel_id=1, source_target_pairs={{0,1},{1,0},{2,3},{3,2},{4,5},{5,4},{6,7},{7,6},{8,9},{9,8},{10,11... | collective-permute-start | bytes 393224 | tf_op jit(solution)/shard_map/ppermute | solution.py:47
  30.1 2.6 %shard_map.118 = (bf16[2048,512]{1,0:T(8,128)(2,1)}, bf16[2048,512]{1,0:T(8,128)(2,1)}) custom-call(bf16[128,2048]{1,0:T(8,128)(2,1)S(1)} %get-tuple-element.46.l_ref, bf16[128,512]{1,0:T(8,128)(2,1)S(1)} %get-tuple-element.47.refs_0_, bf16[128,512]{1,0:T(8,128)(2,1)S(1)} %get-tuple-element.48.refs_1_), custom_call_target="tpu_custom_call" | custom-call | flops 536870912 | bytes 4194304 | tf_op jit(solution)/shard_map/pallas_call | solution.py:225
  32.7 0.0 collective-permute-done.16.refs_4_
  32.7 1.0 %collective-permute-done.11.refs_0_ = bf16[1,32,2048]{2,1,0:T(8,128)(2,1)S(1)} collective-permute-done((bf16[1,32,2048]{2,1,0:T(8,128)(2,1)S(1)}, bf16[1,32,2048]{2,1,0:T(8,128)(2,1)S(1)}, u32[]{:S(2)}, u32[]{:S(2)}) %collective-permute-start.11) | collective-permute-done | bytes 131104 | tf_op jit(solution)/shard_map/ppermute | solution.py:47
  33.7 2.0 %collective-permute-done.13.refs_1_ = bf16[1,32,2048]{2,1,0:T(8,128)(2,1)S(1)} collective-permute-done((bf16[1,32,2048]{2,1,0:T(8,128)(2,1)S(1)}, bf16[1,32,2048]{2,1,0:T(8,128)(2,1)S(1)}, u32[]{:S(2)}, u32[]{:S(2)}) %collective-permute-start.13) | collective-permute-done | bytes 131104 | tf_op jit(solution)/shard_map/ppermute | solution.py:47
  35.7 0.0 collective-permute-done.15.refs_2_
  35.7 0.1 shard_map.119
  35.8 1.6 %collective-permute-start.17 = (bf16[1,8,2048]{2,1,0:T(8,128)(2,1)S(1)}, bf16[1,8,2048]{2,1,0:T(8,128)(2,1)S(1)}, u32[]{:S(2)}, u32[]{:S(2)}) collective-permute-start(bf16[1,8,2048]{2,1,0:T(8,128)(2,1)S(1)} %get-tuple-element.51), channel_id=1, source_target_pairs={{0,24},{1,25},{2,26},{3,27},{4,28},{5,29},{6,30},{7,31},{8,16},{9,... | collective-permute-start | bytes 98312 | tf_op jit(solution)/shard_map/ppermute | solution.py:47
  37.4 0.5 %collective-permute-start.18 = (bf16[1,8,2048]{2,1,0:T(8,128)(2,1)S(1)}, bf16[1,8,2048]{2,1,0:T(8,128)(2,1)S(1)}, u32[]{:S(2)}, u32[]{:S(2)}) collective-permute-start(bf16[1,8,2048]{2,1,0:T(8,128)(2,1)S(1)} %get-tuple-element.52), channel_id=1, source_target_pairs={{0,16},{1,17},{2,18},{3,19},{4,20},{5,21},{6,22},{7,23},{8,24},{9,... | collective-permute-start | bytes 98312 | tf_op jit(solution)/shard_map/ppermute | solution.py:47
  38.0 2.3 %collective-permute-start.19 = (bf16[1,8,2048]{2,1,0:T(8,128)(2,1)S(1)}, bf16[1,8,2048]{2,1,0:T(8,128)(2,1)S(1)}, u32[]{:S(2)}, u32[]{:S(2)}) collective-permute-start(bf16[1,8,2048]{2,1,0:T(8,128)(2,1)S(1)} %get-tuple-element.53), channel_id=1, source_target_pairs={{0,8},{1,9},{2,10},{3,11},{4,12},{5,13},{6,14},{7,15},{8,0},{9,1},... | collective-permute-start | bytes 98312 | tf_op jit(solution)/shard_map/ppermute | solution.py:47
  40.2 1.9 %shard_map.120.refs_4_ = bf16[512,2048]{1,0:T(8,128)(2,1)} custom-call(bf16[128,512]{1,0:T(8,128)(2,1)S(1)} %get-tuple-element.54.l_ref, bf16[128,2048]{1,0:T(8,128)(2,1)S(1)} %get-tuple-element.55.refs_0_), custom_call_target="tpu_custom_call" | custom-call | flops 268435456 | bytes 2097152 | tf_op jit(solution)/shard_map/pallas_call | solution.py:225
  42.1 0.0 collective-permute-done.17.refs_1_
  42.2 0.1 collective-permute-done.18.refs_2_
  42.3 0.2 collective-permute-done.19.refs_3_
  42.5 0.6 %shard_map.121 = (bf16[4,2048]{1,0:T(4,128)(2,1)}, bf16[4,2048]{1,0:T(4,128)(2,1)}) custom-call(f32[1,8,2048]{2,1,0:T(8,128)S(1)} %get-tuple-element.50.refs_0_, bf16[1,8,2048]{2,1,0:T(8,128)(2,1)S(1)} %collective-permute-done.17.refs_1_, bf16[1,8,2048]{2,1,0:T(8,128)(2,1)S(1)} %collective-permute-done.18.refs_2_, ...), custom_call_target="tpu_custom_call" | custom-call | bytes 65536 | tf_op jit(solution)/shard_map/pallas_call | solution.py:307
  (4 shorter events, 0.1 us)
Async XLA Ops:
  1.6 7.0 %collective-permute-start.2 = (bf16[1,8,2176]{2,1,0:T(8,128)(2,1)S(1)}, bf16[1,8,2176]{2,1,0:T(8,128)(2,1)S(1)}, u32[]{:S(2)}, u32[]{:S(2)}) collective-permute-start(bf16[1,8,2176]{2,1,0:T(8,128)(2,1)S(1)} %shard_map.110.refs_0_), channel_id=1, source_target_pairs={{0,24},{1,25},{2,26},{3,27},{4,28},{5,29},{6,30},{7,31},{8,16},{9,... | collective-permute-start | bytes 104456 | tf_op jit(solution)/shard_map/ppermute | solution.py:47
  6.7 4.8 %collective-permute-start.1 = (bf16[1,8,2176]{2,1,0:T(8,128)(2,1)S(1)}, bf16[1,8,2176]{2,1,0:T(8,128)(2,1)S(1)}, u32[]{:S(2)}, u32[]{:S(2)}) collective-permute-start(bf16[1,8,2176]{2,1,0:T(8,128)(2,1)S(1)} %shard_map.110.refs_0_), channel_id=1, source_target_pairs={{0,16},{1,17},{2,18},{3,19},{4,20},{5,21},{6,22},{7,23},{8,24},{9,... | collective-permute-start | bytes 104456 | tf_op jit(solution)/shard_map/ppermute | solution.py:47
  6.7 4.8 %collective-permute-start = (bf16[1,8,2176]{2,1,0:T(8,128)(2,1)S(1)}, bf16[1,8,2176]{2,1,0:T(8,128)(2,1)S(1)}, u32[]{:S(2)}, u32[]{:S(2)}) collective-permute-start(bf16[1,8,2176]{2,1,0:T(8,128)(2,1)S(1)} %shard_map.110.refs_0_), channel_id=1, source_target_pairs={{0,8},{1,9},{2,10},{3,11},{4,12},{5,13},{6,14},{7,15},{8,0},{9,1},... | collective-permute-start | bytes 104456 | tf_op jit(solution)/shard_map/ppermute | solution.py:47
  11.6 7.5 %collective-permute-start.5 = (bf16[1,32,2176]{2,1,0:T(8,128)(2,1)S(1)}, bf16[1,32,2176]{2,1,0:T(8,128)(2,1)S(1)}, u32[]{:S(2)}, u32[]{:S(2)}) collective-permute-start(bf16[1,32,2176]{2,1,0:T(8,128)(2,1)S(1)} %shard_map.111.b_ref.refs_0_), channel_id=1, source_target_pairs={{0,5},{1,4},{2,7},{3,6},{4,1},{5,0},{6,3},{7,2},{8,13},{9,12},{10,... | collective-permute-start | bytes 417800 | tf_op jit(solution)/shard_map/ppermute | solution.py:47
  14.1 5.8 %collective-permute-start.4 = (bf16[1,32,2176]{2,1,0:T(8,128)(2,1)S(1)}, bf16[1,32,2176]{2,1,0:T(8,128)(2,1)S(1)}, u32[]{:S(2)}, u32[]{:S(2)}) collective-permute-start(bf16[1,32,2176]{2,1,0:T(8,128)(2,1)S(1)} %shard_map.111.b_ref.refs_0_), channel_id=1, source_target_pairs={{0,4},{1,5},{2,6},{3,7},{4,0},{5,1},{6,2},{7,3},{8,12},{9,13},{10,... | collective-permute-start | bytes 417800 | tf_op jit(solution)/shard_map/ppermute | solution.py:47
  14.6 5.3 %collective-permute-start.3 = (bf16[1,32,2176]{2,1,0:T(8,128)(2,1)S(1)}, bf16[1,32,2176]{2,1,0:T(8,128)(2,1)S(1)}, u32[]{:S(2)}, u32[]{:S(2)}) collective-permute-start(bf16[1,32,2176]{2,1,0:T(8,128)(2,1)S(1)} %shard_map.111.b_ref.refs_0_), channel_id=1, source_target_pairs={{0,1},{1,0},{2,3},{3,2},{4,5},{5,4},{6,7},{7,6},{8,9},{9,8},{10,11... | collective-permute-start | bytes 417800 | tf_op jit(solution)/shard_map/ppermute | solution.py:47
  16.7 5.9 %collective-permute-start.6 = (bf16[1,32,2176]{2,1,0:T(8,128)(2,1)S(1)}, bf16[1,32,2176]{2,1,0:T(8,128)(2,1)S(1)}, u32[]{:S(2)}, u32[]{:S(2)}) collective-permute-start(bf16[1,32,2176]{2,1,0:T(8,128)(2,1)S(1)} %get-tuple-element.32), channel_id=1, source_target_pairs={{0,2},{1,3},{2,0},{3,1},{4,6},{5,7},{6,4},{7,5},{8,10},{9,11},{10,... | collective-permute-start | bytes 417800 | tf_op jit(solution)/shard_map/ppermute | solution.py:47
  19.1 3.6 %collective-permute-start.9 = (bf16[1,32,2176]{2,1,0:T(8,128)(2,1)S(1)}, bf16[1,32,2176]{2,1,0:T(8,128)(2,1)S(1)}, u32[]{:S(2)}, u32[]{:S(2)}) collective-permute-start(bf16[1,32,2176]{2,1,0:T(8,128)(2,1)S(1)} %collective-permute-done.5.refs_3_), channel_id=1, source_target_pairs={{0,2},{1,3},{2,0},{3,1},{4,6},{5,7},{6,4},{7,5},{8,10},{9,11},{10,... | collective-permute-start | bytes 417800 | tf_op jit(solution)/shard_map/ppermute | solution.py:47
  19.8 2.8 %collective-permute-start.8 = (bf16[1,32,2176]{2,1,0:T(8,128)(2,1)S(1)}, bf16[1,32,2176]{2,1,0:T(8,128)(2,1)S(1)}, u32[]{:S(2)}, u32[]{:S(2)}) collective-permute-start(bf16[1,32,2176]{2,1,0:T(8,128)(2,1)S(1)} %collective-permute-done.4.refs_2_), channel_id=1, source_target_pairs={{0,2},{1,3},{2,0},{3,1},{4,6},{5,7},{6,4},{7,5},{8,10},{9,11},{10,... | collective-permute-start | bytes 417800 | tf_op jit(solution)/shard_map/ppermute | solution.py:47
  19.9 2.8 %collective-permute-start.7 = (bf16[1,32,2176]{2,1,0:T(8,128)(2,1)S(1)}, bf16[1,32,2176]{2,1,0:T(8,128)(2,1)S(1)}, u32[]{:S(2)}, u32[]{:S(2)}) collective-permute-start(bf16[1,32,2176]{2,1,0:T(8,128)(2,1)S(1)} %collective-permute-done.3.refs_3_.refs_1_), channel_id=1, source_target_pairs={{0,2},{1,3},{2,0},{3,1},{4,6},{5,7},{6,4},{7,5},{8,10},{9,11},{10,... | collective-permute-start | bytes 417800 | tf_op jit(solution)/shard_map/ppermute | solution.py:47
  24.9 1.4 %collective-permute-start.10 = (bf16[1,32,2048]{2,1,0:T(8,128)(2,1)S(1)}, bf16[1,32,2048]{2,1,0:T(8,128)(2,1)S(1)}, u32[]{:S(2)}, u32[]{:S(2)}) collective-permute-start(bf16[1,32,2048]{2,1,0:T(8,128)(2,1)S(1)} %get-tuple-element.39), channel_id=1, source_target_pairs={{0,2},{1,3},{2,0},{3,1},{4,6},{5,7},{6,4},{7,5},{8,10},{9,11},{10,... | collective-permute-start | bytes 393224 | tf_op jit(solution)/shard_map/ppermute | solution.py:47
  25.0 2.8 %collective-permute-start.12 = (bf16[1,32,2048]{2,1,0:T(8,128)(2,1)S(1)}, bf16[1,32,2048]{2,1,0:T(8,128)(2,1)S(1)}, u32[]{:S(2)}, u32[]{:S(2)}) collective-permute-start(bf16[1,32,2048]{2,1,0:T(8,128)(2,1)S(1)} %get-tuple-element.41), channel_id=1, source_target_pairs={{0,2},{1,3},{2,0},{3,1},{4,6},{5,7},{6,4},{7,5},{8,10},{9,11},{10,... | collective-permute-start | bytes 393224 | tf_op jit(solution)/shard_map/ppermute | solution.py:47
  25.5 3.7 %collective-permute-start.14 = (bf16[1,32,2048]{2,1,0:T(8,128)(2,1)S(1)}, bf16[1,32,2048]{2,1,0:T(8,128)(2,1)S(1)}, u32[]{:S(2)}, u32[]{:S(2)}) collective-permute-start(bf16[1,32,2048]{2,1,0:T(8,128)(2,1)S(1)} %get-tuple-element.43), channel_id=1, source_target_pairs={{0,2},{1,3},{2,0},{3,1},{4,6},{5,7},{6,4},{7,5},{8,10},{9,11},{10,... | collective-permute-start | bytes 393224 | tf_op jit(solution)/shard_map/ppermute | solution.py:47
  25.6 7.1 %collective-permute-start.16 = (bf16[1,32,2048]{2,1,0:T(8,128)(2,1)S(1)}, bf16[1,32,2048]{2,1,0:T(8,128)(2,1)S(1)}, u32[]{:S(2)}, u32[]{:S(2)}) collective-permute-start(bf16[1,32,2048]{2,1,0:T(8,128)(2,1)S(1)} %get-tuple-element.45), channel_id=1, source_target_pairs={{0,2},{1,3},{2,0},{3,1},{4,6},{5,7},{6,4},{7,5},{8,10},{9,11},{10,... | collective-permute-start | bytes 393224 | tf_op jit(solution)/shard_map/ppermute | solution.py:47
  26.3 7.3 %collective-permute-start.11 = (bf16[1,32,2048]{2,1,0:T(8,128)(2,1)S(1)}, bf16[1,32,2048]{2,1,0:T(8,128)(2,1)S(1)}, u32[]{:S(2)}, u32[]{:S(2)}) collective-permute-start(bf16[1,32,2048]{2,1,0:T(8,128)(2,1)S(1)} %shard_map.115), channel_id=1, source_target_pairs={{0,5},{1,4},{2,7},{3,6},{4,1},{5,0},{6,3},{7,2},{8,13},{9,12},{10,... | collective-permute-start | bytes 393224 | tf_op jit(solution)/shard_map/ppermute | solution.py:47
  27.8 7.8 %collective-permute-start.13 = (bf16[1,32,2048]{2,1,0:T(8,128)(2,1)S(1)}, bf16[1,32,2048]{2,1,0:T(8,128)(2,1)S(1)}, u32[]{:S(2)}, u32[]{:S(2)}) collective-permute-start(bf16[1,32,2048]{2,1,0:T(8,128)(2,1)S(1)} %shard_map.116), channel_id=1, source_target_pairs={{0,4},{1,5},{2,6},{3,7},{4,0},{5,1},{6,2},{7,3},{8,12},{9,13},{10,... | collective-permute-start | bytes 393224 | tf_op jit(solution)/shard_map/ppermute | solution.py:47
  29.2 6.5 %collective-permute-start.15 = (bf16[1,32,2048]{2,1,0:T(8,128)(2,1)S(1)}, bf16[1,32,2048]{2,1,0:T(8,128)(2,1)S(1)}, u32[]{:S(2)}, u32[]{:S(2)}) collective-permute-start(bf16[1,32,2048]{2,1,0:T(8,128)(2,1)S(1)} %shard_map.117), channel_id=1, source_target_pairs={{0,1},{1,0},{2,3},{3,2},{4,5},{5,4},{6,7},{7,6},{8,9},{9,8},{10,11... | collective-permute-start | bytes 393224 | tf_op jit(solution)/shard_map/ppermute | solution.py:47
  35.8 6.4 %collective-permute-start.17 = (bf16[1,8,2048]{2,1,0:T(8,128)(2,1)S(1)}, bf16[1,8,2048]{2,1,0:T(8,128)(2,1)S(1)}, u32[]{:S(2)}, u32[]{:S(2)}) collective-permute-start(bf16[1,8,2048]{2,1,0:T(8,128)(2,1)S(1)} %get-tuple-element.51), channel_id=1, source_target_pairs={{0,24},{1,25},{2,26},{3,27},{4,28},{5,29},{6,30},{7,31},{8,16},{9,... | collective-permute-start | bytes 98312 | tf_op jit(solution)/shard_map/ppermute | solution.py:47
  37.4 4.9 %collective-permute-start.18 = (bf16[1,8,2048]{2,1,0:T(8,128)(2,1)S(1)}, bf16[1,8,2048]{2,1,0:T(8,128)(2,1)S(1)}, u32[]{:S(2)}, u32[]{:S(2)}) collective-permute-start(bf16[1,8,2048]{2,1,0:T(8,128)(2,1)S(1)} %get-tuple-element.52), channel_id=1, source_target_pairs={{0,16},{1,17},{2,18},{3,19},{4,20},{5,21},{6,22},{7,23},{8,24},{9,... | collective-permute-start | bytes 98312 | tf_op jit(solution)/shard_map/ppermute | solution.py:47
  38.0 4.6 %collective-permute-start.19 = (bf16[1,8,2048]{2,1,0:T(8,128)(2,1)S(1)}, bf16[1,8,2048]{2,1,0:T(8,128)(2,1)S(1)}, u32[]{:S(2)}, u32[]{:S(2)}) collective-permute-start(bf16[1,8,2048]{2,1,0:T(8,128)(2,1)S(1)} %get-tuple-element.53), channel_id=1, source_target_pairs={{0,8},{1,9},{2,10},{3,11},{4,12},{5,13},{6,14},{7,15},{8,0},{9,1},... | collective-permute-start | bytes 98312 | tf_op jit(solution)/shard_map/ppermute | solution.py:47

commit v8 on v7

--- a/solution.py
+++ b/solution.py
@@ -110,15 +110,34 @@
     )(*outside((w,)), block)
 
 
-def fetch_behind(weights, inside, after):
+def rows_of(x, width, mine, experts):
+    blocks, rows, full = x.shape
+    half, lanes = rows // 2, full - width
+    m = blocks * half
+    token = x[:, :half, :width].reshape(m, width)
+    side = x[:, :half, width:].reshape(m, lanes).astype(F32)
+    lane = lax.broadcasted_iota(jnp.int32, (1, lanes), 1)
+    scale = jnp.where(lane == mine, 1.0 / 256.0, 0.0) + jnp.where(lane == mine + experts, 1.0 / 65536.0, 0.0)
+    coef = jnp.sum(side * scale, axis=1, keepdims=True)
+    return token, coef, (coef * x[:, half:, :width].reshape(m, width).astype(F32)).astype(BF16)
+
+
+def fetch_behind(weights, inside, held, me, experts):
     n = len(weights)
-
-    def body(*refs):
-        outs = refs[n + 2 : -1]
+    count = len(held)
+    width = inside.shape[0]
+    m = sum(h.shape[0] * h.shape[1] for h in held) // 2
+
+    def body(*refs):
+        outs = refs[n + 2 + count : -1]
         copies = [pltpu.make_async_copy(refs[k], outs[k], refs[-1].at[k]) for k in range(n)]
         for c in copies:
             c.start()
         outs[n][...] = refs[n][...].T
+        x = jnp.concatenate([r[...] for r in refs[n + 2 : n + 2 + count]], axis=0)
+        token, coef, dout = rows_of(x, width, refs[n + 1][0], experts)
+        outs[n + 2][...], outs[n + 4][...] = token, dout
+        outs[n + 3][...] = jnp.broadcast_to(coef, (m, 128))
         copies[0].wait()
         outs[n + 1][...] = outs[0][...].T
         for c in copies[1:]:
@@ -126,13 +145,14 @@
 
     return pl.pallas_call(
         body,
-        out_shape=[shape(*w.shape) for w in weights] + [shape(*inside.shape[::-1]), shape(*weights[0].shape[::-1])],
-        in_specs=[hbm() for _ in weights] + [vmem(), pl.BlockSpec(memory_space=pl.ANY)],
-        out_specs=[vmem() for _ in range(n + 2)],
+        out_shape=[shape(*w.shape) for w in weights] + [shape(*inside.shape[::-1]), shape(*weights[0].shape[::-1])]
+        + [shape(m, width), shape(m, 128, dtype=F32), shape(m, width)],
+        in_specs=[hbm() for _ in weights] + [vmem(), pl.BlockSpec(memory_space=pltpu.SMEM)] + [vmem()] * count,
+        out_specs=[vmem() for _ in range(n + 5)],
         scratch_shapes=[pltpu.SemaphoreType.DMA((n,))],
-        compiler_params=params(),
+        compiler_params=params(LARGE),
         cost_estimate=cost(0, 8 << 20),
-    )(*outside(weights), inside, after)
+    )(*outside(weights), inside, me, *held)
 
 
 def regroup(blocks):
@@ -156,29 +176,26 @@
     )(*blocks)
 
 
-def expert_math(pieces, me, w_gate, turned, w_up, w_down, experts, splits):
-    blocks = sum(p.shape[0] for p in pieces)
+def expert_math(pieces, ready, me, w_gate, turned, w_up, w_down, experts, splits):
+    blocks = sum(splits)
     width, hid = w_gate.shape
     _, rows, full = pieces[0].shape
-    lanes = full - width
     half = rows // 2
     m = blocks * half
-    count = len(pieces)
-
-    def body(*refs):
+    count, had = len(pieces), len(ready)
+
+    def body(*refs):
+        early, refs = refs[count : count + had], refs[:count] + refs[count + had :]
         me_ref, wg_ref, gw_ref, dw_ref, wu_ref, wd_ref = refs[count : count + 6]
         outs = refs[count + 6 :]
         parts, (t_ref, do_ref, h_ref, dg_ref, du_ref) = outs[: len(splits)], outs[len(splits) :]
         x = jnp.concatenate([r[...] for r in refs[:count]], axis=0)
-        token = x[:, :half, :width].reshape(m, width)
-        t_ref[...] = token
-        side = x[:, :half, width:].reshape(m, lanes).astype(F32)
-        lane = lax.broadcasted_iota(jnp.int32, (1, lanes), 1)
-        mine = me_ref[0]
-        scale = jnp.where(lane == mine, 1.0 / 256.0, 0.0) + jnp.where(lane == mine + experts, 1.0 / 65536.0, 0.0)
-        coef = jnp.sum(side * scale, axis=1, keepdims=True)
-        dout = (coef * x[:, half:, :width].reshape(m, width).astype(F32)).astype(BF16)
-        do_ref[...] = dout
+        token, coef, dout = rows_of(x, width, me_ref[0], experts)
+        if had:
+            token = jnp.concatenate([early[0][...], token], axis=0)
+            coef = jnp.concatenate([early[1][:, :1], coef], axis=0)
+            dout = jnp.concatenate([early[2][...], dout], axis=0)
+        t_ref[...], do_ref[...] = token, dout
         gate = dot(token, wg_ref[...])
         upper = dot(token, wu_ref[...])
         dact = dot(dout, dw_ref[...])
@@ -204,11 +221,11 @@
     got = pl.pallas_call(
         body,
         out_shape=outs,
-        in_specs=[vmem()] * count + [pl.BlockSpec(memory_space=pltpu.SMEM)] + [vmem()] * 5,
+        in_specs=[vmem()] * (count + had) + [pl.BlockSpec(memory_space=pltpu.SMEM)] + [vmem()] * 5,
         out_specs=[vmem() for _ in outs],
         compiler_params=params(LARGE),
         cost_estimate=cost(12 * m * width * hid, 10 << 20),
-    )(*pieces, me, w_gate, *turned, w_up, w_down)
+    )(*pieces, *ready, me, w_gate, *turned, w_up, w_down)
     return list(got[: len(splits)]), got[len(splits) :]
 
 
@@ -328,19 +345,20 @@
         held = [block] + exchange_all(block, masks, total)
         block = jnp.concatenate(held, axis=0)
     wg, own = fetch(wg, held[0])
-    wd, wu, *turned = fetch_behind((wd, wu), wg, held[1])
+    wd, wu, *turned = fetch_behind((wd, wu), wg, held, me, experts)
+    turned, ready = turned[:2], turned[2:]
     pieces = held + [exchange(h, core, total) for h in [own] + held[1:]]
 
     ways = len(held)
     groups = total // GROUP
     size = groups // 2 // ways
     if groups <= CHUNK:
-        parts, kept = expert_math(pieces, me, wg, turned, wu, wd, experts, [size] * (2 * ways))
+        parts, kept = expert_math(pieces[len(held) :], ready, me, wg, turned, wu, wd, experts, [size] * (2 * ways))
     else:
         whole = jnp.concatenate(pieces, axis=0)
         sums, saved = [], []
         for at in range(0, groups, CHUNK):
-            (got,), rest = expert_math([whole[at : at + CHUNK]], me, wg, turned, wu, wd, experts, [CHUNK])
+            (got,), rest = expert_math([whole[at : at + CHUNK]], [], me, wg, turned, wu, wd, experts, [CHUNK])
             sums.append(got)
             saved.append(rest)
         got = jnp.concatenate(sums, axis=0)

time: 43.5 us -> 43.6 us (level)
  no operation moved by 1% of the time
where the time goes in v8:
time: 43.6 us; the launch traced here: 43.2 us
  starting transfers between devices  19.1 us (44%)
  Pallas kernels  12.4 us (28%)
  waiting for transfers between devices  10.9 us (25%)
  between operations  0.75 us (2%)
    ppermute x20, starting transfers between devices, exchange(): return lax.ppermute(x, AXES, [(i, i ^ mask) for i in range(total)])  19.1 us
    ppermute x20, waiting for transfers between devices, exchange(): return lax.ppermute(x, AXES, [(i, i ^ mask) for i in range(total)])  10.9 us
    pallas_call x2, Pallas kernels, weight_grads(): pl.pallas_call(body, grid=(steps,), out_shape=[shape(rows, cols) for _ in...  4.48 us
    pallas_call x1, Pallas kernels, expert_math(): pl.pallas_call(body, out_shape=outs, in_specs=[vmem()] * (count + had) +...  2.3 us
    pallas_call x1, Pallas kernels, fetch_behind(): pl.pallas_call(body, out_shape=[shape(*w.shape) for w in weights] + [shap...  2.24 us
    pallas_call x1, Pallas kernels, fetch(): pl.pallas_call(body, out_shape=[shape(*w.shape), shape(*block.shape)], in...  1.6 us
    pallas_call x1, Pallas kernels, pack(): pl.pallas_call(body, out_shape=shape(1, 2 * rows, width + lanes), in_spec...  0.92 us
  transfers between devices with their start and end apart: 20, of which 9 were waited for; matrix products, arithmetic and copies ran while one was open for 0% of the time, Pallas kernels for 20%

profile of v8, /device:TPU:0, one launch (start us, length us, event | category | flops | bytes accessed | tf_op | source)
XLA Modules:
  0.0 43.2 jit_solution(6832930726630538654)
XLA Ops:
  0.6 0.9 %shard_map.110.refs_0_ = bf16[1,8,2176]{2,1,0:T(8,128)(2,1)S(1)} custom-call(bf16[4,2048]{1,0:T(4,128)(2,1)} %t_in.1, s32[4,8]{1,0:T(4,128)} %i_in.1, s32[4,8]{1,0:T(4,128)} %w_in.1, bf16[4,2048]{1,0:T(4,128)(2,1)} %g_in.1), custom_call_target="tpu_custom_call" | custom-call | bytes 81920 | tf_op jit(solution)/shard_map/pallas_call | solution.py:84
  1.6 5.1 %collective-permute-start.2 = (bf16[1,8,2176]{2,1,0:T(8,128)(2,1)S(1)}, bf16[1,8,2176]{2,1,0:T(8,128)(2,1)S(1)}, u32[]{:S(2)}, u32[]{:S(2)}) collective-permute-start(bf16[1,8,2176]{2,1,0:T(8,128)(2,1)S(1)} %shard_map.110.refs_0_), channel_id=1, source_target_pairs={{0,24},{1,25},{2,26},{3,27},{4,28},{5,29},{6,30},{7,31},{8,16},{9,... | collective-permute-start | bytes 104456 | tf_op jit(solution)/shard_map/ppermute | solution.py:47
  6.7 0.0 collective-permute-start.1
  6.7 0.6 %collective-permute-start = (bf16[1,8,2176]{2,1,0:T(8,128)(2,1)S(1)}, bf16[1,8,2176]{2,1,0:T(8,128)(2,1)S(1)}, u32[]{:S(2)}, u32[]{:S(2)}) collective-permute-start(bf16[1,8,2176]{2,1,0:T(8,128)(2,1)S(1)} %shard_map.110.refs_0_), channel_id=1, source_target_pairs={{0,8},{1,9},{2,10},{3,11},{4,12},{5,13},{6,14},{7,15},{8,0},{9,1},... | collective-permute-start | bytes 104456 | tf_op jit(solution)/shard_map/ppermute | solution.py:47
  7.3 1.3 %collective-permute-done.2.refs_3_ = bf16[1,8,2176]{2,1,0:T(8,128)(2,1)S(1)} collective-permute-done((bf16[1,8,2176]{2,1,0:T(8,128)(2,1)S(1)}, bf16[1,8,2176]{2,1,0:T(8,128)(2,1)S(1)}, u32[]{:S(2)}, u32[]{:S(2)}) %collective-permute-start.2) | collective-permute-done | bytes 34848 | tf_op jit(solution)/shard_map/ppermute | solution.py:47
  8.6 2.9 %collective-permute-done.1.refs_2_ = bf16[1,8,2176]{2,1,0:T(8,128)(2,1)S(1)} collective-permute-done((bf16[1,8,2176]{2,1,0:T(8,128)(2,1)S(1)}, bf16[1,8,2176]{2,1,0:T(8,128)(2,1)S(1)}, u32[]{:S(2)}, u32[]{:S(2)}) %collective-permute-start.1) | collective-permute-done | bytes 34848 | tf_op jit(solution)/shard_map/ppermute | solution.py:47
  11.5 0.0 collective-permute-done.refs_1_
  11.6 2.5 %collective-permute-start.8 = (bf16[1,32,2176]{2,1,0:T(8,128)(2,1)S(1)}, bf16[1,32,2176]{2,1,0:T(8,128)(2,1)S(1)}, u32[]{:S(2)}, u32[]{:S(2)}) collective-permute-start(bf16[1,32,2176]{2,1,0:T(8,128)(2,1)S(1)} %shard_map.111.b_ref.refs_4_), channel_id=1, source_target_pairs={{0,5},{1,4},{2,7},{3,6},{4,1},{5,0},{6,3},{7,2},{8,13},{9,12},{10,... | collective-permute-start | bytes 417800 | tf_op jit(solution)/shard_map/ppermute | solution.py:47
  14.1 0.5 %collective-permute-start.6 = (bf16[1,32,2176]{2,1,0:T(8,128)(2,1)S(1)}, bf16[1,32,2176]{2,1,0:T(8,128)(2,1)S(1)}, u32[]{:S(2)}, u32[]{:S(2)}) collective-permute-start(bf16[1,32,2176]{2,1,0:T(8,128)(2,1)S(1)} %shard_map.111.b_ref.refs_4_), channel_id=1, source_target_pairs={{0,4},{1,5},{2,6},{3,7},{4,0},{5,1},{6,2},{7,3},{8,12},{9,13},{10,... | collective-permute-start | bytes 417800 | tf_op jit(solution)/shard_map/ppermute | solution.py:47
  14.6 0.5 %collective-permute-start.4 = (bf16[1,32,2176]{2,1,0:T(8,128)(2,1)S(1)}, bf16[1,32,2176]{2,1,0:T(8,128)(2,1)S(1)}, u32[]{:S(2)}, u32[]{:S(2)}) collective-permute-start(bf16[1,32,2176]{2,1,0:T(8,128)(2,1)S(1)} %shard_map.111.b_ref.refs_4_), channel_id=1, source_target_pairs={{0,1},{1,0},{2,3},{3,2},{4,5},{5,4},{6,7},{7,6},{8,9},{9,8},{10,11... | collective-permute-start | bytes 417800 | tf_op jit(solution)/shard_map/ppermute | solution.py:47
  15.1 1.6 %shard_map.112 = (bf16[2048,512]{1,0:T(8,128)(2,1)S(1)}, bf16[1,32,2176]{2,1,0:T(8,128)(2,1)S(1)}) custom-call(bf16[2048,512]{1,0:T(8,128)(2,1)} %bitcast.8, bf16[1,32,2176]{2,1,0:T(8,128)(2,1)S(1)} %shard_map.111.b_ref.refs_4_), custom_call_target="tpu_custom_call" | custom-call | bytes 4194304 | tf_op jit(solution)/shard_map/pallas_call | solution.py:102
  16.7 0.1 collective-permute-start.3
  16.8 2.3 %collective-permute-done.8.refs_7_ = bf16[1,32,2176]{2,1,0:T(8,128)(2,1)S(1)} collective-permute-done((bf16[1,32,2176]{2,1,0:T(8,128)(2,1)S(1)}, bf16[1,32,2176]{2,1,0:T(8,128)(2,1)S(1)}, u32[]{:S(2)}, u32[]{:S(2)}) %collective-permute-start.8) | collective-permute-done | bytes 139296 | tf_op jit(solution)/shard_map/ppermute | solution.py:47
  19.1 0.0 collective-permute-start.9
  19.1 0.8 %collective-permute-done.6.refs_6_ = bf16[1,32,2176]{2,1,0:T(8,128)(2,1)S(1)} collective-permute-done((bf16[1,32,2176]{2,1,0:T(8,128)(2,1)S(1)}, bf16[1,32,2176]{2,1,0:T(8,128)(2,1)S(1)}, u32[]{:S(2)}, u32[]{:S(2)}) %collective-permute-start.6) | collective-permute-done | bytes 139296 | tf_op jit(solution)/shard_map/ppermute | solution.py:47
  19.8 0.0 collective-permute-start.7
  19.9 0.0 collective-permute-done.4.refs_5_
  19.9 0.5 %collective-permute-start.5 = (bf16[1,32,2176]{2,1,0:T(8,128)(2,1)S(1)}, bf16[1,32,2176]{2,1,0:T(8,128)(2,1)S(1)}, u32[]{:S(2)}, u32[]{:S(2)}) collective-permute-start(bf16[1,32,2176]{2,1,0:T(8,128)(2,1)S(1)} %collective-permute-done.4.refs_5_), channel_id=1, source_target_pairs={{0,2},{1,3},{2,0},{3,1},{4,6},{5,7},{6,4},{7,5},{8,10},{9,11},{10,... | collective-permute-start | bytes 417800 | tf_op jit(solution)/shard_map/ppermute | solution.py:47
  20.4 2.2 %shard_map.113 = (bf16[512,2048]{1,0:T(8,128)(2,1)S(1)}, bf16[2048,512]{1,0:T(8,128)(2,1)S(1)}, bf16[512,2048]{1,0:T(8,128)(2,1)S(1)}, bf16[2048,512]{1,0:T(8,12...) custom-call(bf16[512,2048]{1,0:T(8,128)(2,1)} %bitcast.9, ...), custom_call_target="tpu_custom_call" | custom-call | bytes 8388608 | tf_op jit(solution)/shard_map/pallas_call | solution.py:146
  22.6 0.0 collective-permute-done.3.refs_0_
  22.6 0.0 collective-permute-done.9.refs_3_
  22.6 0.0 collective-permute-done.7.refs_2_
  22.6 0.0 collective-permute-done.5.refs_1_
  22.7 2.3 %shard_map.114 = (bf16[1,32,2048]{2,1,0:T(8,128)(2,1)S(1)}, bf16[1,32,2048]{2,1,0:T(8,128)(2,1)S(1)}, bf16[1,32,2048]{2,1,0:T(8,128)(2,1)S(1)}, bf16[1,32,2048]{...) custom-call(bf16[1,32,2176]{2,1,0:T(8,128)(2,1)S(1)} %collective-per, ...), custom_call_target="tpu_custom_call" | custom-call | flops 1610612736 | bytes 10485760 | tf_op jit(solution)/shard_map/pallas_call | solution.py:221
  25.0 0.1 collective-permute-start.10
  25.0 0.5 %collective-permute-start.12 = (bf16[1,32,2048]{2,1,0:T(8,128)(2,1)S(1)}, bf16[1,32,2048]{2,1,0:T(8,128)(2,1)S(1)}, u32[]{:S(2)}, u32[]{:S(2)}) collective-permute-start(bf16[1,32,2048]{2,1,0:T(8,128)(2,1)S(1)} %get-tuple-element.47), channel_id=1, source_target_pairs={{0,2},{1,3},{2,0},{3,1},{4,6},{5,7},{6,4},{7,5},{8,10},{9,11},{10,... | collective-permute-start | bytes 393224 | tf_op jit(solution)/shard_map/ppermute | solution.py:47
  25.5 0.1 collective-permute-start.14
  25.6 0.4 collective-permute-start.16
  26.1 0.3 collective-permute-done.10.b_ref
  26.4 1.5 %collective-permute-start.11 = (bf16[1,32,2048]{2,1,0:T(8,128)(2,1)S(1)}, bf16[1,32,2048]{2,1,0:T(8,128)(2,1)S(1)}, u32[]{:S(2)}, u32[]{:S(2)}) collective-permute-start(bf16[1,32,2048]{2,1,0:T(8,128)(2,1)S(1)} %shard_map.115), channel_id=1, source_target_pairs={{0,5},{1,4},{2,7},{3,6},{4,1},{5,0},{6,3},{7,2},{8,13},{9,12},{10,... | collective-permute-start | bytes 393224 | tf_op jit(solution)/shard_map/ppermute | solution.py:47
  27.9 0.0 collective-permute-done.12.b_ref
  27.9 1.3 %collective-permute-start.13 = (bf16[1,32,2048]{2,1,0:T(8,128)(2,1)S(1)}, bf16[1,32,2048]{2,1,0:T(8,128)(2,1)S(1)}, u32[]{:S(2)}, u32[]{:S(2)}) collective-permute-start(bf16[1,32,2048]{2,1,0:T(8,128)(2,1)S(1)} %shard_map.116), channel_id=1, source_target_pairs={{0,4},{1,5},{2,6},{3,7},{4,0},{5,1},{6,2},{7,3},{8,12},{9,13},{10,... | collective-permute-start | bytes 393224 | tf_op jit(solution)/shard_map/ppermute | solution.py:47
  29.2 0.0 collective-permute-done.14.b_ref
  29.2 1.0 %collective-permute-start.15 = (bf16[1,32,2048]{2,1,0:T(8,128)(2,1)S(1)}, bf16[1,32,2048]{2,1,0:T(8,128)(2,1)S(1)}, u32[]{:S(2)}, u32[]{:S(2)}) collective-permute-start(bf16[1,32,2048]{2,1,0:T(8,128)(2,1)S(1)} %shard_map.117), channel_id=1, source_target_pairs={{0,1},{1,0},{2,3},{3,2},{4,5},{5,4},{6,7},{7,6},{8,9},{9,8},{10,11... | collective-permute-start | bytes 393224 | tf_op jit(solution)/shard_map/ppermute | solution.py:47
  30.2 2.6 %shard_map.118 = (bf16[2048,512]{1,0:T(8,128)(2,1)}, bf16[2048,512]{1,0:T(8,128)(2,1)}) custom-call(bf16[128,2048]{1,0:T(8,128)(2,1)S(1)} %get-tuple-element.52.l_ref, bf16[128,512]{1,0:T(8,128)(2,1)S(1)} %get-tuple-element.53.refs_0_, bf16[128,512]{1,0:T(8,128)(2,1)S(1)} %get-tuple-element.54.refs_1_), custom_call_target="tpu_custom_call" | custom-call | flops 536870912 | bytes 4194304 | tf_op jit(solution)/shard_map/pallas_call | solution.py:242
  32.8 0.0 collective-permute-done.16.refs_4_
  32.8 1.0 %collective-permute-done.11.refs_0_ = bf16[1,32,2048]{2,1,0:T(8,128)(2,1)S(1)} collective-permute-done((bf16[1,32,2048]{2,1,0:T(8,128)(2,1)S(1)}, bf16[1,32,2048]{2,1,0:T(8,128)(2,1)S(1)}, u32[]{:S(2)}, u32[]{:S(2)}) %collective-permute-start.11) | collective-permute-done | bytes 131104 | tf_op jit(solution)/shard_map/ppermute | solution.py:47
  33.7 2.0 %collective-permute-done.13.refs_1_ = bf16[1,32,2048]{2,1,0:T(8,128)(2,1)S(1)} collective-permute-done((bf16[1,32,2048]{2,1,0:T(8,128)(2,1)S(1)}, bf16[1,32,2048]{2,1,0:T(8,128)(2,1)S(1)}, u32[]{:S(2)}, u32[]{:S(2)}) %collective-permute-start.13) | collective-permute-done | bytes 131104 | tf_op jit(solution)/shard_map/ppermute | solution.py:47
  35.7 0.0 collective-permute-done.15.refs_2_
  35.7 0.1 shard_map.119
  35.9 1.7 %collective-permute-start.17 = (bf16[1,8,2048]{2,1,0:T(8,128)(2,1)S(1)}, bf16[1,8,2048]{2,1,0:T(8,128)(2,1)S(1)}, u32[]{:S(2)}, u32[]{:S(2)}) collective-permute-start(bf16[1,8,2048]{2,1,0:T(8,128)(2,1)S(1)} %get-tuple-element.57), channel_id=1, source_target_pairs={{0,24},{1,25},{2,26},{3,27},{4,28},{5,29},{6,30},{7,31},{8,16},{9,... | collective-permute-start | bytes 98312 | tf_op jit(solution)/shard_map/ppermute | solution.py:47
  37.5 0.5 %collective-permute-start.18 = (bf16[1,8,2048]{2,1,0:T(8,128)(2,1)S(1)}, bf16[1,8,2048]{2,1,0:T(8,128)(2,1)S(1)}, u32[]{:S(2)}, u32[]{:S(2)}) collective-permute-start(bf16[1,8,2048]{2,1,0:T(8,128)(2,1)S(1)} %get-tuple-element.58), channel_id=1, source_target_pairs={{0,16},{1,17},{2,18},{3,19},{4,20},{5,21},{6,22},{7,23},{8,24},{9,... | collective-permute-start | bytes 98312 | tf_op jit(solution)/shard_map/ppermute | solution.py:47
  38.0 2.3 %collective-permute-start.19 = (bf16[1,8,2048]{2,1,0:T(8,128)(2,1)S(1)}, bf16[1,8,2048]{2,1,0:T(8,128)(2,1)S(1)}, u32[]{:S(2)}, u32[]{:S(2)}) collective-permute-start(bf16[1,8,2048]{2,1,0:T(8,128)(2,1)S(1)} %get-tuple-element.59), channel_id=1, source_target_pairs={{0,8},{1,9},{2,10},{3,11},{4,12},{5,13},{6,14},{7,15},{8,0},{9,1},... | collective-permute-start | bytes 98312 | tf_op jit(solution)/shard_map/ppermute | solution.py:47
  40.3 1.9 %shard_map.120.refs_4_ = bf16[512,2048]{1,0:T(8,128)(2,1)} custom-call(bf16[128,512]{1,0:T(8,128)(2,1)S(1)} %get-tuple-element.60.l_ref, bf16[128,2048]{1,0:T(8,128)(2,1)S(1)} %get-tuple-element.61.refs_0_), custom_call_target="tpu_custom_call" | custom-call | flops 268435456 | bytes 2097152 | tf_op jit(solution)/shard_map/pallas_call | solution.py:242
  42.2 0.0 collective-permute-done.17.refs_1_
  42.2 0.1 collective-permute-done.18.refs_2_
  42.4 0.2 collective-permute-done.19.refs_3_
  42.6 0.6 %shard_map.121 = (bf16[4,2048]{1,0:T(4,128)(2,1)}, bf16[4,2048]{1,0:T(4,128)(2,1)}) custom-call(f32[1,8,2048]{2,1,0:T(8,128)S(1)} %get-tuple-element.56.refs_0_, bf16[1,8,2048]{2,1,0:T(8,128)(2,1)S(1)} %collective-permute-done.17.refs_1_, bf16[1,8,2048]{2,1,0:T(8,128)(2,1)S(1)} %collective-permute-done.18.refs_2_, ...), custom_call_target="tpu_custom_call" | custom-call | bytes 65536 | tf_op jit(solution)/shard_map/pallas_call | solution.py:324
  (4 shorter events, 0.1 us)
Async XLA Ops:
  1.6 7.0 %collective-permute-start.2 = (bf16[1,8,2176]{2,1,0:T(8,128)(2,1)S(1)}, bf16[1,8,2176]{2,1,0:T(8,128)(2,1)S(1)}, u32[]{:S(2)}, u32[]{:S(2)}) collective-permute-start(bf16[1,8,2176]{2,1,0:T(8,128)(2,1)S(1)} %shard_map.110.refs_0_), channel_id=1, source_target_pairs={{0,24},{1,25},{2,26},{3,27},{4,28},{5,29},{6,30},{7,31},{8,16},{9,... | collective-permute-start | bytes 104456 | tf_op jit(solution)/shard_map/ppermute | solution.py:47
  6.7 4.8 %collective-permute-start.1 = (bf16[1,8,2176]{2,1,0:T(8,128)(2,1)S(1)}, bf16[1,8,2176]{2,1,0:T(8,128)(2,1)S(1)}, u32[]{:S(2)}, u32[]{:S(2)}) collective-permute-start(bf16[1,8,2176]{2,1,0:T(8,128)(2,1)S(1)} %shard_map.110.refs_0_), channel_id=1, source_target_pairs={{0,16},{1,17},{2,18},{3,19},{4,20},{5,21},{6,22},{7,23},{8,24},{9,... | collective-permute-start | bytes 104456 | tf_op jit(solution)/shard_map/ppermute | solution.py:47
  6.7 4.8 %collective-permute-start = (bf16[1,8,2176]{2,1,0:T(8,128)(2,1)S(1)}, bf16[1,8,2176]{2,1,0:T(8,128)(2,1)S(1)}, u32[]{:S(2)}, u32[]{:S(2)}) collective-permute-start(bf16[1,8,2176]{2,1,0:T(8,128)(2,1)S(1)} %shard_map.110.refs_0_), channel_id=1, source_target_pairs={{0,8},{1,9},{2,10},{3,11},{4,12},{5,13},{6,14},{7,15},{8,0},{9,1},... | collective-permute-start | bytes 104456 | tf_op jit(solution)/shard_map/ppermute | solution.py:47
  11.6 7.5 %collective-permute-start.8 = (bf16[1,32,2176]{2,1,0:T(8,128)(2,1)S(1)}, bf16[1,32,2176]{2,1,0:T(8,128)(2,1)S(1)}, u32[]{:S(2)}, u32[]{:S(2)}) collective-permute-start(bf16[1,32,2176]{2,1,0:T(8,128)(2,1)S(1)} %shard_map.111.b_ref.refs_4_), channel_id=1, source_target_pairs={{0,5},{1,4},{2,7},{3,6},{4,1},{5,0},{6,3},{7,2},{8,13},{9,12},{10,... | collective-permute-start | bytes 417800 | tf_op jit(solution)/shard_map/ppermute | solution.py:47
  14.1 5.8 %collective-permute-start.6 = (bf16[1,32,2176]{2,1,0:T(8,128)(2,1)S(1)}, bf16[1,32,2176]{2,1,0:T(8,128)(2,1)S(1)}, u32[]{:S(2)}, u32[]{:S(2)}) collective-permute-start(bf16[1,32,2176]{2,1,0:T(8,128)(2,1)S(1)} %shard_map.111.b_ref.refs_4_), channel_id=1, source_target_pairs={{0,4},{1,5},{2,6},{3,7},{4,0},{5,1},{6,2},{7,3},{8,12},{9,13},{10,... | collective-permute-start | bytes 417800 | tf_op jit(solution)/shard_map/ppermute | solution.py:47
  14.6 5.3 %collective-permute-start.4 = (bf16[1,32,2176]{2,1,0:T(8,128)(2,1)S(1)}, bf16[1,32,2176]{2,1,0:T(8,128)(2,1)S(1)}, u32[]{:S(2)}, u32[]{:S(2)}) collective-permute-start(bf16[1,32,2176]{2,1,0:T(8,128)(2,1)S(1)} %shard_map.111.b_ref.refs_4_), channel_id=1, source_target_pairs={{0,1},{1,0},{2,3},{3,2},{4,5},{5,4},{6,7},{7,6},{8,9},{9,8},{10,11... | collective-permute-start | bytes 417800 | tf_op jit(solution)/shard_map/ppermute | solution.py:47
  16.7 5.9 %collective-permute-start.3 = (bf16[1,32,2176]{2,1,0:T(8,128)(2,1)S(1)}, bf16[1,32,2176]{2,1,0:T(8,128)(2,1)S(1)}, u32[]{:S(2)}, u32[]{:S(2)}) collective-permute-start(bf16[1,32,2176]{2,1,0:T(8,128)(2,1)S(1)} %get-tuple-element.35), channel_id=1, source_target_pairs={{0,2},{1,3},{2,0},{3,1},{4,6},{5,7},{6,4},{7,5},{8,10},{9,11},{10,... | collective-permute-start | bytes 417800 | tf_op jit(solution)/shard_map/ppermute | solution.py:47
  19.1 3.6 %collective-permute-start.9 = (bf16[1,32,2176]{2,1,0:T(8,128)(2,1)S(1)}, bf16[1,32,2176]{2,1,0:T(8,128)(2,1)S(1)}, u32[]{:S(2)}, u32[]{:S(2)}) collective-permute-start(bf16[1,32,2176]{2,1,0:T(8,128)(2,1)S(1)} %collective-permute-done.8.refs_7_), channel_id=1, source_target_pairs={{0,2},{1,3},{2,0},{3,1},{4,6},{5,7},{6,4},{7,5},{8,10},{9,11},{10,... | collective-permute-start | bytes 417800 | tf_op jit(solution)/shard_map/ppermute | solution.py:47
  19.8 2.8 %collective-permute-start.7 = (bf16[1,32,2176]{2,1,0:T(8,128)(2,1)S(1)}, bf16[1,32,2176]{2,1,0:T(8,128)(2,1)S(1)}, u32[]{:S(2)}, u32[]{:S(2)}) collective-permute-start(bf16[1,32,2176]{2,1,0:T(8,128)(2,1)S(1)} %collective-permute-done.6.refs_6_), channel_id=1, source_target_pairs={{0,2},{1,3},{2,0},{3,1},{4,6},{5,7},{6,4},{7,5},{8,10},{9,11},{10,... | collective-permute-start | bytes 417800 | tf_op jit(solution)/shard_map/ppermute | solution.py:47
  19.9 2.8 %collective-permute-start.5 = (bf16[1,32,2176]{2,1,0:T(8,128)(2,1)S(1)}, bf16[1,32,2176]{2,1,0:T(8,128)(2,1)S(1)}, u32[]{:S(2)}, u32[]{:S(2)}) collective-permute-start(bf16[1,32,2176]{2,1,0:T(8,128)(2,1)S(1)} %collective-permute-done.4.refs_5_), channel_id=1, source_target_pairs={{0,2},{1,3},{2,0},{3,1},{4,6},{5,7},{6,4},{7,5},{8,10},{9,11},{10,... | collective-permute-start | bytes 417800 | tf_op jit(solution)/shard_map/ppermute | solution.py:47
  25.0 1.4 %collective-permute-start.10 = (bf16[1,32,2048]{2,1,0:T(8,128)(2,1)S(1)}, bf16[1,32,2048]{2,1,0:T(8,128)(2,1)S(1)}, u32[]{:S(2)}, u32[]{:S(2)}) collective-permute-start(bf16[1,32,2048]{2,1,0:T(8,128)(2,1)S(1)} %get-tuple-element.45), channel_id=1, source_target_pairs={{0,2},{1,3},{2,0},{3,1},{4,6},{5,7},{6,4},{7,5},{8,10},{9,11},{10,... | collective-permute-start | bytes 393224 | tf_op jit(solution)/shard_map/ppermute | solution.py:47
  25.0 2.8 %collective-permute-start.12 = (bf16[1,32,2048]{2,1,0:T(8,128)(2,1)S(1)}, bf16[1,32,2048]{2,1,0:T(8,128)(2,1)S(1)}, u32[]{:S(2)}, u32[]{:S(2)}) collective-permute-start(bf16[1,32,2048]{2,1,0:T(8,128)(2,1)S(1)} %get-tuple-element.47), channel_id=1, source_target_pairs={{0,2},{1,3},{2,0},{3,1},{4,6},{5,7},{6,4},{7,5},{8,10},{9,11},{10,... | collective-permute-start | bytes 393224 | tf_op jit(solution)/shard_map/ppermute | solution.py:47
  25.5 3.6 %collective-permute-start.14 = (bf16[1,32,2048]{2,1,0:T(8,128)(2,1)S(1)}, bf16[1,32,2048]{2,1,0:T(8,128)(2,1)S(1)}, u32[]{:S(2)}, u32[]{:S(2)}) collective-permute-start(bf16[1,32,2048]{2,1,0:T(8,128)(2,1)S(1)} %get-tuple-element.49), channel_id=1, source_target_pairs={{0,2},{1,3},{2,0},{3,1},{4,6},{5,7},{6,4},{7,5},{8,10},{9,11},{10,... | collective-permute-start | bytes 393224 | tf_op jit(solution)/shard_map/ppermute | solution.py:47
  25.6 7.1 %collective-permute-start.16 = (bf16[1,32,2048]{2,1,0:T(8,128)(2,1)S(1)}, bf16[1,32,2048]{2,1,0:T(8,128)(2,1)S(1)}, u32[]{:S(2)}, u32[]{:S(2)}) collective-permute-start(bf16[1,32,2048]{2,1,0:T(8,128)(2,1)S(1)} %get-tuple-element.51), channel_id=1, source_target_pairs={{0,2},{1,3},{2,0},{3,1},{4,6},{5,7},{6,4},{7,5},{8,10},{9,11},{10,... | collective-permute-start | bytes 393224 | tf_op jit(solution)/shard_map/ppermute | solution.py:47
  26.4 7.3 %collective-permute-start.11 = (bf16[1,32,2048]{2,1,0:T(8,128)(2,1)S(1)}, bf16[1,32,2048]{2,1,0:T(8,128)(2,1)S(1)}, u32[]{:S(2)}, u32[]{:S(2)}) collective-permute-start(bf16[1,32,2048]{2,1,0:T(8,128)(2,1)S(1)} %shard_map.115), channel_id=1, source_target_pairs={{0,5},{1,4},{2,7},{3,6},{4,1},{5,0},{6,3},{7,2},{8,13},{9,12},{10,... | collective-permute-start | bytes 393224 | tf_op jit(solution)/shard_map/ppermute | solution.py:47
  27.9 7.8 %collective-permute-start.13 = (bf16[1,32,2048]{2,1,0:T(8,128)(2,1)S(1)}, bf16[1,32,2048]{2,1,0:T(8,128)(2,1)S(1)}, u32[]{:S(2)}, u32[]{:S(2)}) collective-permute-start(bf16[1,32,2048]{2,1,0:T(8,128)(2,1)S(1)} %shard_map.116), channel_id=1, source_target_pairs={{0,4},{1,5},{2,6},{3,7},{4,0},{5,1},{6,2},{7,3},{8,12},{9,13},{10,... | collective-permute-start | bytes 393224 | tf_op jit(solution)/shard_map/ppermute | solution.py:47
  29.2 6.5 %collective-permute-start.15 = (bf16[1,32,2048]{2,1,0:T(8,128)(2,1)S(1)}, bf16[1,32,2048]{2,1,0:T(8,128)(2,1)S(1)}, u32[]{:S(2)}, u32[]{:S(2)}) collective-permute-start(bf16[1,32,2048]{2,1,0:T(8,128)(2,1)S(1)} %shard_map.117), channel_id=1, source_target_pairs={{0,1},{1,0},{2,3},{3,2},{4,5},{5,4},{6,7},{7,6},{8,9},{9,8},{10,11... | collective-permute-start | bytes 393224 | tf_op jit(solution)/shard_map/ppermute | solution.py:47
  35.9 6.4 %collective-permute-start.17 = (bf16[1,8,2048]{2,1,0:T(8,128)(2,1)S(1)}, bf16[1,8,2048]{2,1,0:T(8,128)(2,1)S(1)}, u32[]{:S(2)}, u32[]{:S(2)}) collective-permute-start(bf16[1,8,2048]{2,1,0:T(8,128)(2,1)S(1)} %get-tuple-element.57), channel_id=1, source_target_pairs={{0,24},{1,25},{2,26},{3,27},{4,28},{5,29},{6,30},{7,31},{8,16},{9,... | collective-permute-start | bytes 98312 | tf_op jit(solution)/shard_map/ppermute | solution.py:47
  37.5 4.9 %collective-permute-start.18 = (bf16[1,8,2048]{2,1,0:T(8,128)(2,1)S(1)}, bf16[1,8,2048]{2,1,0:T(8,128)(2,1)S(1)}, u32[]{:S(2)}, u32[]{:S(2)}) collective-permute-start(bf16[1,8,2048]{2,1,0:T(8,128)(2,1)S(1)} %get-tuple-element.58), channel_id=1, source_target_pairs={{0,16},{1,17},{2,18},{3,19},{4,20},{5,21},{6,22},{7,23},{8,24},{9,... | collective-permute-start | bytes 98312 | tf_op jit(solution)/shard_map/ppermute | solution.py:47
  38.0 4.6 %collective-permute-start.19 = (bf16[1,8,2048]{2,1,0:T(8,128)(2,1)S(1)}, bf16[1,8,2048]{2,1,0:T(8,128)(2,1)S(1)}, u32[]{:S(2)}, u32[]{:S(2)}) collective-permute-start(bf16[1,8,2048]{2,1,0:T(8,128)(2,1)S(1)} %get-tuple-element.59), channel_id=1, source_target_pairs={{0,8},{1,9},{2,10},{3,11},{4,12},{5,13},{6,14},{7,15},{8,0},{9,1},... | collective-permute-start | bytes 98312 | tf_op jit(solution)/shard_map/ppermute | solution.py:47

commit v9 on v8

--- a/solution.py
+++ b/solution.py
@@ -197,10 +197,10 @@
             dout = jnp.concatenate([early[2][...], dout], axis=0)
         t_ref[...], do_ref[...] = token, dout
         gate = dot(token, wg_ref[...])
+        sig = jax.nn.sigmoid(gate)
+        swish = gate * sig
         upper = dot(token, wu_ref[...])
         dact = dot(dout, dw_ref[...])
-        sig = jax.nn.sigmoid(gate)
-        swish = gate * sig
         hidden = (swish * upper).astype(BF16)
         dgate = (dact * upper * sig * (1.0 + gate * (1.0 - sig))).astype(BF16)
         dupper = (dact * swish).astype(BF16)

time: 43.6 us -> 43.5 us (level)
  no operation moved by 1% of the time
where the time goes in v9:
time: 43.5 us; the launch traced here: 43.2 us
  starting transfers between devices  19.1 us (44%)
  Pallas kernels  12.4 us (29%)
  waiting for transfers between devices  10.9 us (25%)
  between operations  0.75 us (2%)
    ppermute x20, starting transfers between devices, exchange(): return lax.ppermute(x, AXES, [(i, i ^ mask) for i in range(total)])  19.1 us
    ppermute x20, waiting for transfers between devices, exchange(): return lax.ppermute(x, AXES, [(i, i ^ mask) for i in range(total)])  10.9 us
    pallas_call x2, Pallas kernels, weight_grads(): pl.pallas_call(body, grid=(steps,), out_shape=[shape(rows, cols) for _ in...  4.49 us
    pallas_call x1, Pallas kernels, expert_math(): pl.pallas_call(body, out_shape=outs, in_specs=[vmem()] * (count + had) +...  2.31 us
    pallas_call x1, Pallas kernels, fetch_behind(): pl.pallas_call(body, out_shape=[shape(*w.shape) for w in weights] + [shap...  2.24 us
    pallas_call x1, Pallas kernels, fetch(): pl.pallas_call(body, out_shape=[shape(*w.shape), shape(*block.shape)], in...  1.6 us
    pallas_call x1, Pallas kernels, pack(): pl.pallas_call(body, out_shape=shape(1, 2 * rows, width + lanes), in_spec...  0.92 us
  transfers between devices with their start and end apart: 20, of which 9 were waited for; matrix products, arithmetic and copies ran while one was open for 0% of the time, Pallas kernels for 20%

profile of v9, /device:TPU:0, one launch (start us, length us, event | category | flops | bytes accessed | tf_op | source)
XLA Modules:
  0.0 43.2 jit_solution(275089686043585201)
XLA Ops:
  0.6 0.9 %shard_map.110.refs_0_ = bf16[1,8,2176]{2,1,0:T(8,128)(2,1)S(1)} custom-call(bf16[4,2048]{1,0:T(4,128)(2,1)} %t_in.1, s32[4,8]{1,0:T(4,128)} %i_in.1, s32[4,8]{1,0:T(4,128)} %w_in.1, bf16[4,2048]{1,0:T(4,128)(2,1)} %g_in.1), custom_call_target="tpu_custom_call" | custom-call | bytes 81920 | tf_op jit(solution)/shard_map/pallas_call | solution.py:84
  1.6 5.1 %collective-permute-start.2 = (bf16[1,8,2176]{2,1,0:T(8,128)(2,1)S(1)}, bf16[1,8,2176]{2,1,0:T(8,128)(2,1)S(1)}, u32[]{:S(2)}, u32[]{:S(2)}) collective-permute-start(bf16[1,8,2176]{2,1,0:T(8,128)(2,1)S(1)} %shard_map.110.refs_0_), channel_id=1, source_target_pairs={{0,24},{1,25},{2,26},{3,27},{4,28},{5,29},{6,30},{7,31},{8,16},{9,... | collective-permute-start | bytes 104456 | tf_op jit(solution)/shard_map/ppermute | solution.py:47
  6.7 0.0 collective-permute-start.1
  6.7 0.6 %collective-permute-start = (bf16[1,8,2176]{2,1,0:T(8,128)(2,1)S(1)}, bf16[1,8,2176]{2,1,0:T(8,128)(2,1)S(1)}, u32[]{:S(2)}, u32[]{:S(2)}) collective-permute-start(bf16[1,8,2176]{2,1,0:T(8,128)(2,1)S(1)} %shard_map.110.refs_0_), channel_id=1, source_target_pairs={{0,8},{1,9},{2,10},{3,11},{4,12},{5,13},{6,14},{7,15},{8,0},{9,1},... | collective-permute-start | bytes 104456 | tf_op jit(solution)/shard_map/ppermute | solution.py:47
  7.3 1.3 %collective-permute-done.2.refs_3_ = bf16[1,8,2176]{2,1,0:T(8,128)(2,1)S(1)} collective-permute-done((bf16[1,8,2176]{2,1,0:T(8,128)(2,1)S(1)}, bf16[1,8,2176]{2,1,0:T(8,128)(2,1)S(1)}, u32[]{:S(2)}, u32[]{:S(2)}) %collective-permute-start.2) | collective-permute-done | bytes 34848 | tf_op jit(solution)/shard_map/ppermute | solution.py:47
  8.6 2.9 %collective-permute-done.1.refs_2_ = bf16[1,8,2176]{2,1,0:T(8,128)(2,1)S(1)} collective-permute-done((bf16[1,8,2176]{2,1,0:T(8,128)(2,1)S(1)}, bf16[1,8,2176]{2,1,0:T(8,128)(2,1)S(1)}, u32[]{:S(2)}, u32[]{:S(2)}) %collective-permute-start.1) | collective-permute-done | bytes 34848 | tf_op jit(solution)/shard_map/ppermute | solution.py:47
  11.5 0.0 collective-permute-done.refs_1_
  11.6 2.5 %collective-permute-start.8 = (bf16[1,32,2176]{2,1,0:T(8,128)(2,1)S(1)}, bf16[1,32,2176]{2,1,0:T(8,128)(2,1)S(1)}, u32[]{:S(2)}, u32[]{:S(2)}) collective-permute-start(bf16[1,32,2176]{2,1,0:T(8,128)(2,1)S(1)} %shard_map.111.b_ref.refs_4_), channel_id=1, source_target_pairs={{0,5},{1,4},{2,7},{3,6},{4,1},{5,0},{6,3},{7,2},{8,13},{9,12},{10,... | collective-permute-start | bytes 417800 | tf_op jit(solution)/shard_map/ppermute | solution.py:47
  14.1 0.5 %collective-permute-start.6 = (bf16[1,32,2176]{2,1,0:T(8,128)(2,1)S(1)}, bf16[1,32,2176]{2,1,0:T(8,128)(2,1)S(1)}, u32[]{:S(2)}, u32[]{:S(2)}) collective-permute-start(bf16[1,32,2176]{2,1,0:T(8,128)(2,1)S(1)} %shard_map.111.b_ref.refs_4_), channel_id=1, source_target_pairs={{0,4},{1,5},{2,6},{3,7},{4,0},{5,1},{6,2},{7,3},{8,12},{9,13},{10,... | collective-permute-start | bytes 417800 | tf_op jit(solution)/shard_map/ppermute | solution.py:47
  14.6 0.5 %collective-permute-start.4 = (bf16[1,32,2176]{2,1,0:T(8,128)(2,1)S(1)}, bf16[1,32,2176]{2,1,0:T(8,128)(2,1)S(1)}, u32[]{:S(2)}, u32[]{:S(2)}) collective-permute-start(bf16[1,32,2176]{2,1,0:T(8,128)(2,1)S(1)} %shard_map.111.b_ref.refs_4_), channel_id=1, source_target_pairs={{0,1},{1,0},{2,3},{3,2},{4,5},{5,4},{6,7},{7,6},{8,9},{9,8},{10,11... | collective-permute-start | bytes 417800 | tf_op jit(solution)/shard_map/ppermute | solution.py:47
  15.1 1.6 %shard_map.112 = (bf16[2048,512]{1,0:T(8,128)(2,1)S(1)}, bf16[1,32,2176]{2,1,0:T(8,128)(2,1)S(1)}) custom-call(bf16[2048,512]{1,0:T(8,128)(2,1)} %bitcast.8, bf16[1,32,2176]{2,1,0:T(8,128)(2,1)S(1)} %shard_map.111.b_ref.refs_4_), custom_call_target="tpu_custom_call" | custom-call | bytes 4194304 | tf_op jit(solution)/shard_map/pallas_call | solution.py:102
  16.7 0.1 collective-permute-start.3
  16.8 2.3 %collective-permute-done.8.refs_7_ = bf16[1,32,2176]{2,1,0:T(8,128)(2,1)S(1)} collective-permute-done((bf16[1,32,2176]{2,1,0:T(8,128)(2,1)S(1)}, bf16[1,32,2176]{2,1,0:T(8,128)(2,1)S(1)}, u32[]{:S(2)}, u32[]{:S(2)}) %collective-permute-start.8) | collective-permute-done | bytes 139296 | tf_op jit(solution)/shard_map/ppermute | solution.py:47
  19.1 0.0 collective-permute-start.9
  19.1 0.8 %collective-permute-done.6.refs_6_ = bf16[1,32,2176]{2,1,0:T(8,128)(2,1)S(1)} collective-permute-done((bf16[1,32,2176]{2,1,0:T(8,128)(2,1)S(1)}, bf16[1,32,2176]{2,1,0:T(8,128)(2,1)S(1)}, u32[]{:S(2)}, u32[]{:S(2)}) %collective-permute-start.6) | collective-permute-done | bytes 139296 | tf_op jit(solution)/shard_map/ppermute | solution.py:47
  19.8 0.0 collective-permute-start.7
  19.9 0.0 collective-permute-done.4.refs_5_
  19.9 0.5 %collective-permute-start.5 = (bf16[1,32,2176]{2,1,0:T(8,128)(2,1)S(1)}, bf16[1,32,2176]{2,1,0:T(8,128)(2,1)S(1)}, u32[]{:S(2)}, u32[]{:S(2)}) collective-permute-start(bf16[1,32,2176]{2,1,0:T(8,128)(2,1)S(1)} %collective-permute-done.4.refs_5_), channel_id=1, source_target_pairs={{0,2},{1,3},{2,0},{3,1},{4,6},{5,7},{6,4},{7,5},{8,10},{9,11},{10,... | collective-permute-start | bytes 417800 | tf_op jit(solution)/shard_map/ppermute | solution.py:47
  20.4 2.2 %shard_map.113 = (bf16[512,2048]{1,0:T(8,128)(2,1)S(1)}, bf16[2048,512]{1,0:T(8,128)(2,1)S(1)}, bf16[512,2048]{1,0:T(8,128)(2,1)S(1)}, bf16[2048,512]{1,0:T(8,12...) custom-call(bf16[512,2048]{1,0:T(8,128)(2,1)} %bitcast.9, ...), custom_call_target="tpu_custom_call" | custom-call | bytes 8388608 | tf_op jit(solution)/shard_map/pallas_call | solution.py:146
  22.6 0.0 collective-permute-done.3.refs_0_
  22.6 0.0 collective-permute-done.9.refs_3_
  22.6 0.0 collective-permute-done.7.refs_2_
  22.6 0.0 collective-permute-done.5.refs_1_
  22.7 2.3 %shard_map.114 = (bf16[1,32,2048]{2,1,0:T(8,128)(2,1)S(1)}, bf16[1,32,2048]{2,1,0:T(8,128)(2,1)S(1)}, bf16[1,32,2048]{2,1,0:T(8,128)(2,1)S(1)}, bf16[1,32,2048]{...) custom-call(bf16[1,32,2176]{2,1,0:T(8,128)(2,1)S(1)} %collective-per, ...), custom_call_target="tpu_custom_call" | custom-call | flops 1610612736 | bytes 10485760 | tf_op jit(solution)/shard_map/pallas_call | solution.py:221
  25.0 0.1 collective-permute-start.10
  25.0 0.5 %collective-permute-start.12 = (bf16[1,32,2048]{2,1,0:T(8,128)(2,1)S(1)}, bf16[1,32,2048]{2,1,0:T(8,128)(2,1)S(1)}, u32[]{:S(2)}, u32[]{:S(2)}) collective-permute-start(bf16[1,32,2048]{2,1,0:T(8,128)(2,1)S(1)} %get-tuple-element.47), channel_id=1, source_target_pairs={{0,2},{1,3},{2,0},{3,1},{4,6},{5,7},{6,4},{7,5},{8,10},{9,11},{10,... | collective-permute-start | bytes 393224 | tf_op jit(solution)/shard_map/ppermute | solution.py:47
  25.5 0.1 collective-permute-start.14
  25.6 0.4 collective-permute-start.16
  26.1 0.3 collective-permute-done.10.b_ref
  26.4 1.5 %collective-permute-start.11 = (bf16[1,32,2048]{2,1,0:T(8,128)(2,1)S(1)}, bf16[1,32,2048]{2,1,0:T(8,128)(2,1)S(1)}, u32[]{:S(2)}, u32[]{:S(2)}) collective-permute-start(bf16[1,32,2048]{2,1,0:T(8,128)(2,1)S(1)} %shard_map.115), channel_id=1, source_target_pairs={{0,5},{1,4},{2,7},{3,6},{4,1},{5,0},{6,3},{7,2},{8,13},{9,12},{10,... | collective-permute-start | bytes 393224 | tf_op jit(solution)/shard_map/ppermute | solution.py:47
  27.9 0.0 collective-permute-done.12.b_ref
  27.9 1.3 %collective-permute-start.13 = (bf16[1,32,2048]{2,1,0:T(8,128)(2,1)S(1)}, bf16[1,32,2048]{2,1,0:T(8,128)(2,1)S(1)}, u32[]{:S(2)}, u32[]{:S(2)}) collective-permute-start(bf16[1,32,2048]{2,1,0:T(8,128)(2,1)S(1)} %shard_map.116), channel_id=1, source_target_pairs={{0,4},{1,5},{2,6},{3,7},{4,0},{5,1},{6,2},{7,3},{8,12},{9,13},{10,... | collective-permute-start | bytes 393224 | tf_op jit(solution)/shard_map/ppermute | solution.py:47
  29.2 0.0 collective-permute-done.14.b_ref
  29.2 1.0 %collective-permute-start.15 = (bf16[1,32,2048]{2,1,0:T(8,128)(2,1)S(1)}, bf16[1,32,2048]{2,1,0:T(8,128)(2,1)S(1)}, u32[]{:S(2)}, u32[]{:S(2)}) collective-permute-start(bf16[1,32,2048]{2,1,0:T(8,128)(2,1)S(1)} %shard_map.117), channel_id=1, source_target_pairs={{0,1},{1,0},{2,3},{3,2},{4,5},{5,4},{6,7},{7,6},{8,9},{9,8},{10,11... | collective-permute-start | bytes 393224 | tf_op jit(solution)/shard_map/ppermute | solution.py:47
  30.2 2.6 %shard_map.118 = (bf16[2048,512]{1,0:T(8,128)(2,1)}, bf16[2048,512]{1,0:T(8,128)(2,1)}) custom-call(bf16[128,2048]{1,0:T(8,128)(2,1)S(1)} %get-tuple-element.52.l_ref, bf16[128,512]{1,0:T(8,128)(2,1)S(1)} %get-tuple-element.53.refs_0_, bf16[128,512]{1,0:T(8,128)(2,1)S(1)} %get-tuple-element.54.refs_1_), custom_call_target="tpu_custom_call" | custom-call | flops 536870912 | bytes 4194304 | tf_op jit(solution)/shard_map/pallas_call | solution.py:242
  32.8 0.0 collective-permute-done.16.refs_4_
  32.8 1.0 %collective-permute-done.11.refs_0_ = bf16[1,32,2048]{2,1,0:T(8,128)(2,1)S(1)} collective-permute-done((bf16[1,32,2048]{2,1,0:T(8,128)(2,1)S(1)}, bf16[1,32,2048]{2,1,0:T(8,128)(2,1)S(1)}, u32[]{:S(2)}, u32[]{:S(2)}) %collective-permute-start.11) | collective-permute-done | bytes 131104 | tf_op jit(solution)/shard_map/ppermute | solution.py:47
  33.7 2.0 %collective-permute-done.13.refs_1_ = bf16[1,32,2048]{2,1,0:T(8,128)(2,1)S(1)} collective-permute-done((bf16[1,32,2048]{2,1,0:T(8,128)(2,1)S(1)}, bf16[1,32,2048]{2,1,0:T(8,128)(2,1)S(1)}, u32[]{:S(2)}, u32[]{:S(2)}) %collective-permute-start.13) | collective-permute-done | bytes 131104 | tf_op jit(solution)/shard_map/ppermute | solution.py:47
  35.7 0.0 collective-permute-done.15.refs_2_
  35.7 0.1 shard_map.119
  35.9 1.6 %collective-permute-start.17 = (bf16[1,8,2048]{2,1,0:T(8,128)(2,1)S(1)}, bf16[1,8,2048]{2,1,0:T(8,128)(2,1)S(1)}, u32[]{:S(2)}, u32[]{:S(2)}) collective-permute-start(bf16[1,8,2048]{2,1,0:T(8,128)(2,1)S(1)} %get-tuple-element.57), channel_id=1, source_target_pairs={{0,24},{1,25},{2,26},{3,27},{4,28},{5,29},{6,30},{7,31},{8,16},{9,... | collective-permute-start | bytes 98312 | tf_op jit(solution)/shard_map/ppermute | solution.py:47
  37.5 0.5 %collective-permute-start.18 = (bf16[1,8,2048]{2,1,0:T(8,128)(2,1)S(1)}, bf16[1,8,2048]{2,1,0:T(8,128)(2,1)S(1)}, u32[]{:S(2)}, u32[]{:S(2)}) collective-permute-start(bf16[1,8,2048]{2,1,0:T(8,128)(2,1)S(1)} %get-tuple-element.58), channel_id=1, source_target_pairs={{0,16},{1,17},{2,18},{3,19},{4,20},{5,21},{6,22},{7,23},{8,24},{9,... | collective-permute-start | bytes 98312 | tf_op jit(solution)/shard_map/ppermute | solution.py:47
  38.0 2.3 %collective-permute-start.19 = (bf16[1,8,2048]{2,1,0:T(8,128)(2,1)S(1)}, bf16[1,8,2048]{2,1,0:T(8,128)(2,1)S(1)}, u32[]{:S(2)}, u32[]{:S(2)}) collective-permute-start(bf16[1,8,2048]{2,1,0:T(8,128)(2,1)S(1)} %get-tuple-element.59), channel_id=1, source_target_pairs={{0,8},{1,9},{2,10},{3,11},{4,12},{5,13},{6,14},{7,15},{8,0},{9,1},... | collective-permute-start | bytes 98312 | tf_op jit(solution)/shard_map/ppermute | solution.py:47
  40.3 1.9 %shard_map.120.refs_4_ = bf16[512,2048]{1,0:T(8,128)(2,1)} custom-call(bf16[128,512]{1,0:T(8,128)(2,1)S(1)} %get-tuple-element.60.l_ref, bf16[128,2048]{1,0:T(8,128)(2,1)S(1)} %get-tuple-element.61.refs_0_), custom_call_target="tpu_custom_call" | custom-call | flops 268435456 | bytes 2097152 | tf_op jit(solution)/shard_map/pallas_call | solution.py:242
  42.2 0.0 collective-permute-done.17.refs_1_
  42.2 0.1 collective-permute-done.18.refs_2_
  42.3 0.2 collective-permute-done.19.refs_3_
  42.6 0.6 %shard_map.121 = (bf16[4,2048]{1,0:T(4,128)(2,1)}, bf16[4,2048]{1,0:T(4,128)(2,1)}) custom-call(f32[1,8,2048]{2,1,0:T(8,128)S(1)} %get-tuple-element.56.refs_0_, bf16[1,8,2048]{2,1,0:T(8,128)(2,1)S(1)} %collective-permute-done.17.refs_1_, bf16[1,8,2048]{2,1,0:T(8,128)(2,1)S(1)} %collective-permute-done.18.refs_2_, ...), custom_call_target="tpu_custom_call" | custom-call | bytes 65536 | tf_op jit(solution)/shard_map/pallas_call | solution.py:324
  (4 shorter events, 0.1 us)
Async XLA Ops:
  1.6 7.0 %collective-permute-start.2 = (bf16[1,8,2176]{2,1,0:T(8,128)(2,1)S(1)}, bf16[1,8,2176]{2,1,0:T(8,128)(2,1)S(1)}, u32[]{:S(2)}, u32[]{:S(2)}) collective-permute-start(bf16[1,8,2176]{2,1,0:T(8,128)(2,1)S(1)} %shard_map.110.refs_0_), channel_id=1, source_target_pairs={{0,24},{1,25},{2,26},{3,27},{4,28},{5,29},{6,30},{7,31},{8,16},{9,... | collective-permute-start | bytes 104456 | tf_op jit(solution)/shard_map/ppermute | solution.py:47
  6.7 4.8 %collective-permute-start.1 = (bf16[1,8,2176]{2,1,0:T(8,128)(2,1)S(1)}, bf16[1,8,2176]{2,1,0:T(8,128)(2,1)S(1)}, u32[]{:S(2)}, u32[]{:S(2)}) collective-permute-start(bf16[1,8,2176]{2,1,0:T(8,128)(2,1)S(1)} %shard_map.110.refs_0_), channel_id=1, source_target_pairs={{0,16},{1,17},{2,18},{3,19},{4,20},{5,21},{6,22},{7,23},{8,24},{9,... | collective-permute-start | bytes 104456 | tf_op jit(solution)/shard_map/ppermute | solution.py:47
  6.7 4.8 %collective-permute-start = (bf16[1,8,2176]{2,1,0:T(8,128)(2,1)S(1)}, bf16[1,8,2176]{2,1,0:T(8,128)(2,1)S(1)}, u32[]{:S(2)}, u32[]{:S(2)}) collective-permute-start(bf16[1,8,2176]{2,1,0:T(8,128)(2,1)S(1)} %shard_map.110.refs_0_), channel_id=1, source_target_pairs={{0,8},{1,9},{2,10},{3,11},{4,12},{5,13},{6,14},{7,15},{8,0},{9,1},... | collective-permute-start | bytes 104456 | tf_op jit(solution)/shard_map/ppermute | solution.py:47
  11.6 7.5 %collective-permute-start.8 = (bf16[1,32,2176]{2,1,0:T(8,128)(2,1)S(1)}, bf16[1,32,2176]{2,1,0:T(8,128)(2,1)S(1)}, u32[]{:S(2)}, u32[]{:S(2)}) collective-permute-start(bf16[1,32,2176]{2,1,0:T(8,128)(2,1)S(1)} %shard_map.111.b_ref.refs_4_), channel_id=1, source_target_pairs={{0,5},{1,4},{2,7},{3,6},{4,1},{5,0},{6,3},{7,2},{8,13},{9,12},{10,... | collective-permute-start | bytes 417800 | tf_op jit(solution)/shard_map/ppermute | solution.py:47
  14.1 5.8 %collective-permute-start.6 = (bf16[1,32,2176]{2,1,0:T(8,128)(2,1)S(1)}, bf16[1,32,2176]{2,1,0:T(8,128)(2,1)S(1)}, u32[]{:S(2)}, u32[]{:S(2)}) collective-permute-start(bf16[1,32,2176]{2,1,0:T(8,128)(2,1)S(1)} %shard_map.111.b_ref.refs_4_), channel_id=1, source_target_pairs={{0,4},{1,5},{2,6},{3,7},{4,0},{5,1},{6,2},{7,3},{8,12},{9,13},{10,... | collective-permute-start | bytes 417800 | tf_op jit(solution)/shard_map/ppermute | solution.py:47
  14.6 5.3 %collective-permute-start.4 = (bf16[1,32,2176]{2,1,0:T(8,128)(2,1)S(1)}, bf16[1,32,2176]{2,1,0:T(8,128)(2,1)S(1)}, u32[]{:S(2)}, u32[]{:S(2)}) collective-permute-start(bf16[1,32,2176]{2,1,0:T(8,128)(2,1)S(1)} %shard_map.111.b_ref.refs_4_), channel_id=1, source_target_pairs={{0,1},{1,0},{2,3},{3,2},{4,5},{5,4},{6,7},{7,6},{8,9},{9,8},{10,11... | collective-permute-start | bytes 417800 | tf_op jit(solution)/shard_map/ppermute | solution.py:47
  16.7 5.9 %collective-permute-start.3 = (bf16[1,32,2176]{2,1,0:T(8,128)(2,1)S(1)}, bf16[1,32,2176]{2,1,0:T(8,128)(2,1)S(1)}, u32[]{:S(2)}, u32[]{:S(2)}) collective-permute-start(bf16[1,32,2176]{2,1,0:T(8,128)(2,1)S(1)} %get-tuple-element.35), channel_id=1, source_target_pairs={{0,2},{1,3},{2,0},{3,1},{4,6},{5,7},{6,4},{7,5},{8,10},{9,11},{10,... | collective-permute-start | bytes 417800 | tf_op jit(solution)/shard_map/ppermute | solution.py:47
  19.1 3.6 %collective-permute-start.9 = (bf16[1,32,2176]{2,1,0:T(8,128)(2,1)S(1)}, bf16[1,32,2176]{2,1,0:T(8,128)(2,1)S(1)}, u32[]{:S(2)}, u32[]{:S(2)}) collective-permute-start(bf16[1,32,2176]{2,1,0:T(8,128)(2,1)S(1)} %collective-permute-done.8.refs_7_), channel_id=1, source_target_pairs={{0,2},{1,3},{2,0},{3,1},{4,6},{5,7},{6,4},{7,5},{8,10},{9,11},{10,... | collective-permute-start | bytes 417800 | tf_op jit(solution)/shard_map/ppermute | solution.py:47
  19.8 2.8 %collective-permute-start.7 = (bf16[1,32,2176]{2,1,0:T(8,128)(2,1)S(1)}, bf16[1,32,2176]{2,1,0:T(8,128)(2,1)S(1)}, u32[]{:S(2)}, u32[]{:S(2)}) collective-permute-start(bf16[1,32,2176]{2,1,0:T(8,128)(2,1)S(1)} %collective-permute-done.6.refs_6_), channel_id=1, source_target_pairs={{0,2},{1,3},{2,0},{3,1},{4,6},{5,7},{6,4},{7,5},{8,10},{9,11},{10,... | collective-permute-start | bytes 417800 | tf_op jit(solution)/shard_map/ppermute | solution.py:47
  19.9 2.8 %collective-permute-start.5 = (bf16[1,32,2176]{2,1,0:T(8,128)(2,1)S(1)}, bf16[1,32,2176]{2,1,0:T(8,128)(2,1)S(1)}, u32[]{:S(2)}, u32[]{:S(2)}) collective-permute-start(bf16[1,32,2176]{2,1,0:T(8,128)(2,1)S(1)} %collective-permute-done.4.refs_5_), channel_id=1, source_target_pairs={{0,2},{1,3},{2,0},{3,1},{4,6},{5,7},{6,4},{7,5},{8,10},{9,11},{10,... | collective-permute-start | bytes 417800 | tf_op jit(solution)/shard_map/ppermute | solution.py:47
  25.0 1.4 %collective-permute-start.10 = (bf16[1,32,2048]{2,1,0:T(8,128)(2,1)S(1)}, bf16[1,32,2048]{2,1,0:T(8,128)(2,1)S(1)}, u32[]{:S(2)}, u32[]{:S(2)}) collective-permute-start(bf16[1,32,2048]{2,1,0:T(8,128)(2,1)S(1)} %get-tuple-element.45), channel_id=1, source_target_pairs={{0,2},{1,3},{2,0},{3,1},{4,6},{5,7},{6,4},{7,5},{8,10},{9,11},{10,... | collective-permute-start | bytes 393224 | tf_op jit(solution)/shard_map/ppermute | solution.py:47
  25.0 2.8 %collective-permute-start.12 = (bf16[1,32,2048]{2,1,0:T(8,128)(2,1)S(1)}, bf16[1,32,2048]{2,1,0:T(8,128)(2,1)S(1)}, u32[]{:S(2)}, u32[]{:S(2)}) collective-permute-start(bf16[1,32,2048]{2,1,0:T(8,128)(2,1)S(1)} %get-tuple-element.47), channel_id=1, source_target_pairs={{0,2},{1,3},{2,0},{3,1},{4,6},{5,7},{6,4},{7,5},{8,10},{9,11},{10,... | collective-permute-start | bytes 393224 | tf_op jit(solution)/shard_map/ppermute | solution.py:47
  25.5 3.6 %collective-permute-start.14 = (bf16[1,32,2048]{2,1,0:T(8,128)(2,1)S(1)}, bf16[1,32,2048]{2,1,0:T(8,128)(2,1)S(1)}, u32[]{:S(2)}, u32[]{:S(2)}) collective-permute-start(bf16[1,32,2048]{2,1,0:T(8,128)(2,1)S(1)} %get-tuple-element.49), channel_id=1, source_target_pairs={{0,2},{1,3},{2,0},{3,1},{4,6},{5,7},{6,4},{7,5},{8,10},{9,11},{10,... | collective-permute-start | bytes 393224 | tf_op jit(solution)/shard_map/ppermute | solution.py:47
  25.6 7.1 %collective-permute-start.16 = (bf16[1,32,2048]{2,1,0:T(8,128)(2,1)S(1)}, bf16[1,32,2048]{2,1,0:T(8,128)(2,1)S(1)}, u32[]{:S(2)}, u32[]{:S(2)}) collective-permute-start(bf16[1,32,2048]{2,1,0:T(8,128)(2,1)S(1)} %get-tuple-element.51), channel_id=1, source_target_pairs={{0,2},{1,3},{2,0},{3,1},{4,6},{5,7},{6,4},{7,5},{8,10},{9,11},{10,... | collective-permute-start | bytes 393224 | tf_op jit(solution)/shard_map/ppermute | solution.py:47
  26.4 7.3 %collective-permute-start.11 = (bf16[1,32,2048]{2,1,0:T(8,128)(2,1)S(1)}, bf16[1,32,2048]{2,1,0:T(8,128)(2,1)S(1)}, u32[]{:S(2)}, u32[]{:S(2)}) collective-permute-start(bf16[1,32,2048]{2,1,0:T(8,128)(2,1)S(1)} %shard_map.115), channel_id=1, source_target_pairs={{0,5},{1,4},{2,7},{3,6},{4,1},{5,0},{6,3},{7,2},{8,13},{9,12},{10,... | collective-permute-start | bytes 393224 | tf_op jit(solution)/shard_map/ppermute | solution.py:47
  27.9 7.8 %collective-permute-start.13 = (bf16[1,32,2048]{2,1,0:T(8,128)(2,1)S(1)}, bf16[1,32,2048]{2,1,0:T(8,128)(2,1)S(1)}, u32[]{:S(2)}, u32[]{:S(2)}) collective-permute-start(bf16[1,32,2048]{2,1,0:T(8,128)(2,1)S(1)} %shard_map.116), channel_id=1, source_target_pairs={{0,4},{1,5},{2,6},{3,7},{4,0},{5,1},{6,2},{7,3},{8,12},{9,13},{10,... | collective-permute-start | bytes 393224 | tf_op jit(solution)/shard_map/ppermute | solution.py:47
  29.2 6.5 %collective-permute-start.15 = (bf16[1,32,2048]{2,1,0:T(8,128)(2,1)S(1)}, bf16[1,32,2048]{2,1,0:T(8,128)(2,1)S(1)}, u32[]{:S(2)}, u32[]{:S(2)}) collective-permute-start(bf16[1,32,2048]{2,1,0:T(8,128)(2,1)S(1)} %shard_map.117), channel_id=1, source_target_pairs={{0,1},{1,0},{2,3},{3,2},{4,5},{5,4},{6,7},{7,6},{8,9},{9,8},{10,11... | collective-permute-start | bytes 393224 | tf_op jit(solution)/shard_map/ppermute | solution.py:47
  35.9 6.4 %collective-permute-start.17 = (bf16[1,8,2048]{2,1,0:T(8,128)(2,1)S(1)}, bf16[1,8,2048]{2,1,0:T(8,128)(2,1)S(1)}, u32[]{:S(2)}, u32[]{:S(2)}) collective-permute-start(bf16[1,8,2048]{2,1,0:T(8,128)(2,1)S(1)} %get-tuple-element.57), channel_id=1, source_target_pairs={{0,24},{1,25},{2,26},{3,27},{4,28},{5,29},{6,30},{7,31},{8,16},{9,... | collective-permute-start | bytes 98312 | tf_op jit(solution)/shard_map/ppermute | solution.py:47
  37.5 4.9 %collective-permute-start.18 = (bf16[1,8,2048]{2,1,0:T(8,128)(2,1)S(1)}, bf16[1,8,2048]{2,1,0:T(8,128)(2,1)S(1)}, u32[]{:S(2)}, u32[]{:S(2)}) collective-permute-start(bf16[1,8,2048]{2,1,0:T(8,128)(2,1)S(1)} %get-tuple-element.58), channel_id=1, source_target_pairs={{0,16},{1,17},{2,18},{3,19},{4,20},{5,21},{6,22},{7,23},{8,24},{9,... | collective-permute-start | bytes 98312 | tf_op jit(solution)/shard_map/ppermute | solution.py:47
  38.0 4.6 %collective-permute-start.19 = (bf16[1,8,2048]{2,1,0:T(8,128)(2,1)S(1)}, bf16[1,8,2048]{2,1,0:T(8,128)(2,1)S(1)}, u32[]{:S(2)}, u32[]{:S(2)}) collective-permute-start(bf16[1,8,2048]{2,1,0:T(8,128)(2,1)S(1)} %get-tuple-element.59), channel_id=1, source_target_pairs={{0,8},{1,9},{2,10},{3,11},{4,12},{5,13},{6,14},{7,15},{8,0},{9,1},... | collective-permute-start | bytes 98312 | tf_op jit(solution)/shard_map/ppermute | solution.py:47
